TPU v7x, 256 devices: a whole 4x4x8 slice. The times are simulated.
256 devices in a mesh: dp: 32 (over x, z_lo, core), inner: 2 (over z_hi), outer: 4 (over y).
Axes of the slice: x: 4, y: 4, z: 8 (z_hi: 2, z_lo: 4; z = z_hi * 4 + z_lo), core: 2. Of those that a mesh axis runs over, the one named last changes fastest.
Arguments:
- partials: bfloat16 [256, 120, 16384], P(('dp', 'inner', 'outer')), parts along dimension 0, may hold values from -5 to 5
- residual: bfloat16 [3840, 16384], P('dp', ('inner', 'outer')), parts along dimension 0, may hold values from -18 to 18
- norm_gain: float32 [16384], replicated, may hold values from 0.25 to 1.75
- kv_weight: bfloat16 [16384, 8, 256], P(None, ('inner', 'outer')), may hold values from -0.046875 to 0.046875
Outputs:
- stream: bfloat16 [3840, 16384], P('dp', ('inner', 'outer')), parts along dimension 0
- kv_pair: bfloat16 [3840, 8, 256], P('dp', ('inner', 'outer')), parts along dimension 0
There are 32 independent parts, one for each index of `dp`. A program takes and returns all parts, laid end to end along the dimension named above; an argument that names none is the same for every part. Nothing has to cross between parts.
All inputs are finite; a program needn't handle non-finite values.
Results may differ from a plain program's by a relative error of at most 0.015.
Values may be sent and summed in bfloat16 or wider, within the bound.
No kernel may reach another device: no remote copies, remote signals or barrier semaphores. Data moves between devices by JAX's collectives and lax.ppermute only.
A program may use at most 128 MiB of HBM per device.

v0:
```python
import jax
import jax.numpy as jnp
from jax import lax
from jax.sharding import PartitionSpec as P


def body(partials, residual, norm_gain, kv_weight):
    own_part = partials[0].astype(jnp.float32)
    half_sum = lax.psum_scatter(
        own_part.astype(jnp.bfloat16), "inner", scatter_dimension=1, tiled=True
    )
    level_one = lax.optimization_barrier(half_sum).astype(jnp.float32)
    level_two = lax.psum_scatter(
        level_one.astype(jnp.bfloat16), "outer", scatter_dimension=1, tiled=True
    ).astype(jnp.float32)
    stream = (residual.astype(jnp.float32) + level_two).astype(jnp.bfloat16)
    values = stream.astype(jnp.float32)
    rows = stream.shape[0]
    width = norm_gain.shape[0]
    local = stream.shape[1]
    heads_local = kv_weight.shape[1]
    pair = kv_weight.shape[2]
    gain_local = lax.dynamic_slice_in_dim(
        norm_gain, lax.axis_index(("inner", "outer")) * local, local
    )
    squares = lax.psum(jnp.sum(values * values, axis=1), ("inner", "outer"))
    factor = lax.rsqrt(squares / width + 1e-05)
    normed = (values * factor[:, None] * gain_local[None, :]).astype(jnp.bfloat16)
    flat_weight = kv_weight.reshape(width, heads_local * pair)
    total = jnp.dot(
        lax.all_gather(normed, ("inner", "outer"), axis=1, tiled=True),
        flat_weight,
        preferred_element_type=jnp.float32,
    )
    kv_pair = total.astype(jnp.bfloat16).reshape(rows, heads_local, pair)
    return (stream, kv_pair)


def solution(mesh):
    placed = (
        P(("dp", "inner", "outer"), None, None),
        P("dp", ("inner", "outer")),
        P(),
        P(None, ("inner", "outer"), None),
    )
    return jax.shard_map(
        body,
        mesh=mesh,
        in_specs=placed,
        out_specs=(P("dp", ("inner", "outer")), P("dp", ("inner", "outer"), None)),
        check_vma=False,
    )
```

profile of v0, /device:TPU:32, one launch (start us, length us, event | category | flops | bytes accessed | tf_op | source)
XLA Modules:
  0.0 289.2 jit_solution(1654955887740112704)
XLA Ops:
  7.2 0.0 copy-start.1
  7.2 0.0 reduce-scatter.3.cloned.1.call-start
  7.2 0.7 reduce-scatter.3.cloned.1.call-update
  7.9 0.0 reduce-scatter.5.cloned.1.call-start
  8.0 107.7 %reduce-scatter.3.cloned.1.call-done = bf16[120,8192]{1,0:T(8,128)(2,1)} async-done(((bf16[120,16384]{1,0:T(8,128)(2,1)}), bf16[120,8192]{1,0:T(8,128)(2,1)}) %reduce-scatter.3.cloned.1.call-update) | async-done | bytes 1966096 | tf_op jit(solution)/shard_map/reduce_scatter | solution.py:9
  115.7 0.0 reduce-scatter.5.cloned.1.call-update
  115.7 0.0 all-gather.2.cloned.1.call-start
  115.8 0.7 dynamic_slice.3
  116.5 31.1 %reduce-scatter.5.cloned.1.call-done = bf16[120,2048]{1,0:T(8,128)(2,1)} async-done(((bf16[120,8192]{1,0:T(8,128)(2,1)}), bf16[120,2048]{1,0:T(8,128)(2,1)}) %reduce-scatter.5.cloned.1.call-update) | async-done | bytes 491536 | tf_op jit(solution)/shard_map/reduce_scatter | solution.py:13
  147.6 0.0 copy-done.1
  147.6 1.3 fusion.8
  148.9 0.0 copy-start
  148.9 28.9 %psum.7 = f32[120]{0:T(128)S(1)} all-reduce(f32[120]{0:T(128)S(1)} %get-tuple-element.2), channel_id=1, replica_groups=mesh['dp'=32,'inner'=2,'outer'=4] {'inner','outer'}, use_global_device_ids=true, to_apply=%region_3.0 | all-reduce | flops 120 | bytes 960 | tf_op jit(solution)/shard_map/psum | solution.py:26
  177.8 1.0 fusion.10
  178.8 0.0 all-gather.2.cloned.1.call-update
  178.8 97.4 %all-gather.2.cloned.1.call-done = bf16[120,16384]{1,0:T(8,128)(2,1)} async-done(((bf16[120,2048]{1,0:T(8,128)(2,1)}), bf16[120,16384]{1,0:T(8,128)(2,1)}) %all-gather.2.cloned.1.call-update) | async-done | bytes 3932176 | tf_op jit(solution)/shard_map/all_gather | solution.py:31
  276.2 6.5 %fusion.5 = bf16[120,1,256]{2,0,1:T(8,128)(2,1)} fusion(bf16[120,16384]{1,0:T(8,128)(2,1)} %all-gather.2.cloned.1.call-done, bf16[16384,1,256]{2,0,1:T(8,128)(2,1)} %param.7), kind=kOutput, calls=%fused_computation.5 | convolution fusion | flops 1006663680 | bytes 12382208 | tf_op jit(solution)/shard_map/dot_general | solution.py:30
  282.7 0.0 copy-done
  (1 shorter events, 0.0 us)
Async XLA Ops:
  7.2 140.4 %copy-start.1 = (bf16[120,2048]{1,0:T(8,128)(2,1)S(1)}, bf16[120,2048]{1,0:T(8,128)(2,1)}, u32[]{:S(2)}) copy-start(bf16[120,2048]{1,0:T(8,128)(2,1)} %param.5) | copy-start | bytes 1474564
  7.2 108.5 %reduce-scatter.3.cloned.1.call-start = ((), (), s32[]{:S(2)}) async-start(), calls=%async_computation.2 | async-start | bytes 5898240 | tf_op jit(solution)/shard_map/reduce_scatter | solution.py:9
  7.9 139.7 %reduce-scatter.5.cloned.1.call-start = ((), (), s32[]{:S(2)}) async-start(), calls=%async_computation.3 | async-start | bytes 2457600 | tf_op jit(solution)/shard_map/reduce_scatter | solution.py:13
  115.7 160.5 %all-gather.2.cloned.1.call-start = ((), (), s32[]{:S(2)}) async-start(), calls=%async_computation.4 | async-start | bytes 4423680 | tf_op jit(solution)/shard_map/all_gather | solution.py:31
  148.9 133.8 %copy-start = (bf16[120,2048]{1,0:T(8,128)(2,1)}, bf16[120,2048]{1,0:T(8,128)(2,1)S(1)}, u32[]{:S(2)}) copy-start(bf16[120,2048]{1,0:T(8,128)(2,1)S(1)} %get-tuple-element.3) | copy-start | bytes 1474564
Sparse Core Ops, SparseCore 0:
  10.5 105.1 reduce-scatter.2
  118.4 29.0 reduce-scatter.4
  178.9 97.2 all-gather.1
where the time goes:
time: 289 us
  waiting for transfers between devices  237 us (82%)
  blocking collectives  28.9 us (10%)
  between operations  13.8 us (5%)
  matrix products  6.52 us (2%)
    reduce_scatter x1, waiting for transfers between devices, body(): lax.psum_scatter(own_part.astype(jnp.bfloat16), 'inner', scatter_dimensio...  108 us
    all_gather x1, waiting for transfers between devices, body(): lax.all_gather(normed, ('inner', 'outer'), axis=1, tiled=True)  97.4 us
    reduce_scatter x1, waiting for transfers between devices, body(): lax.psum_scatter(level_one.astype(jnp.bfloat16), 'outer', scatter_dimensi...  31.1 us
    psum x1, blocking collectives, body(): squares = lax.psum(jnp.sum(values * values, axis=1), ('inner', 'outer'))  28.9 us
    dot_general x1, matrix products, body(): jnp.dot(lax.all_gather(normed, ('inner', 'outer'), axis=1, tiled=True), f...  6.52 us
  transfers between devices with their start and end apart: 3, of which 3 were waited for; matrix products, arithmetic and copies ran while one was open for 0% of the time, Pallas kernels for 0%

commit v1 on v0

v1 whole, which is shorter than its diff:
```python
import functools

import jax
import jax.numpy as jnp
from jax import lax
from jax.experimental import pallas as pl
from jax.experimental.pallas import tpu as pltpu
from jax.sharding import Mesh
from jax.sharding import PartitionSpec as P

BF = jnp.bfloat16
F32 = jnp.float32
OUTER = 4
UNIT = 256
CHUNKS = (256, 512, 640, 640)
VMEM = pl.BlockSpec(memory_space=pltpu.VMEM)
ANY = pl.BlockSpec(memory_space=pl.ANY)
SMEM = pl.BlockSpec(memory_space=pltpu.SMEM)
PAIR_A = [(o, o ^ 1) for o in range(4)]
PAIR_B = [(o, o ^ 3) for o in range(4)]
SWAP = [(0, 1), (1, 0)]


def shift(k):
    return [(o, (o + k) % 4) for o in range(4)]


def params(**more):
    return pltpu.CompilerParams(vmem_limit_bytes=48 * 1024 * 1024, **more)


def cost(flops, nbytes):
    return pl.CostEstimate(flops=flops, bytes_accessed=nbytes, transcendentals=0)


def pick_columns(partial, block_ids, n, start, n_out):
    rows, width = partial.shape
    block = width // 8
    per, first = block // 128, start // 128
    unit = 128

    def spec(t):
        return pl.BlockSpec(
            (rows, unit), lambda g, ids: (0, ids[t] * per + first + g)
        )

    def kernel(ids, *refs):
        ins, outs = refs[: 2 * n_out], refs[2 * n_out :]
        for j in range(n_out):
            outs[j][0] = ins[2 * j][...]
            outs[j][1] = ins[2 * j + 1][...]

    return pl.pallas_call(
        kernel,
        grid_spec=pltpu.PrefetchScalarGridSpec(
            num_scalar_prefetch=1,
            grid=(n // unit,),
            in_specs=[spec(t) for t in range(2 * n_out)],
            out_specs=[
                pl.BlockSpec((2, rows, unit), lambda g, ids: (0, 0, g))
                for _ in range(n_out)
            ],
        ),
        out_shape=[jax.ShapeDtypeStruct((2, rows, n), BF)] * n_out,
        compiler_params=params(),
        cost_estimate=cost(0, 8 * n_out * rows * n),
    )(block_ids, *([partial] * (2 * n_out)))


def first_add(partial, block_ids, from_a, from_b, start):
    rows, width = partial.shape
    n = from_a.shape[2]
    per, first = width // 8 // 128, start // 128
    unit = 128

    def spec(t):
        return pl.BlockSpec(
            (rows, unit), lambda g, ids: (0, ids[t] * per + first + g)
        )

    def kernel(ids, a0, a1, b0, b1, ra, rb, to_a, to_b, keep):
        keep[0] = a0[...].astype(F32) + ra[0].astype(F32)
        to_b[...] = (a1[...].astype(F32) + ra[1].astype(F32)).astype(BF)
        keep[1] = b0[...].astype(F32) + rb[0].astype(F32)
        to_a[...] = (b1[...].astype(F32) + rb[1].astype(F32)).astype(BF)

    pair = pl.BlockSpec((2, rows, unit), lambda g, ids: (0, 0, g))
    flat = pl.BlockSpec((rows, unit), lambda g, ids: (0, g))
    return pl.pallas_call(
        kernel,
        grid_spec=pltpu.PrefetchScalarGridSpec(
            num_scalar_prefetch=1,
            grid=(n // unit,),
            in_specs=[spec(0), spec(1), spec(2), spec(3), pair, pair],
            out_specs=[flat, flat, pair],
        ),
        out_shape=[
            jax.ShapeDtypeStruct((rows, n), BF),
            jax.ShapeDtypeStruct((rows, n), BF),
            jax.ShapeDtypeStruct((2, rows, n), F32),
        ],
        compiler_params=params(),
        cost_estimate=cost(4 * rows * n, 28 * rows * n),
    )(block_ids, partial, partial, partial, partial, from_a, from_b)


def second_add(inner, keep, from_a, from_b, residual, start):
    _, rows, n = keep.shape
    unit = 128
    first = start // unit

    def kernel(ids, keep, ra, rb, res, out, send):
        extra = res[...].astype(F32)
        zero = jnp.zeros_like(extra)
        left = keep[0] + rb[...].astype(F32) + jnp.where(ids[0] == 0, extra, zero)
        right = keep[1] + ra[...].astype(F32) + jnp.where(ids[0] == 1, extra, zero)
        out[0] = left
        out[1] = right
        send[0] = left.astype(BF)
        send[1] = right.astype(BF)

    pair = pl.BlockSpec((2, rows, unit), lambda g, ids: (0, 0, g))
    flat = pl.BlockSpec((rows, unit), lambda g, ids: (0, g))
    return pl.pallas_call(
        kernel,
        grid_spec=pltpu.PrefetchScalarGridSpec(
            num_scalar_prefetch=1,
            grid=(n // unit,),
            in_specs=[
                pair,
                flat,
                flat,
                pl.BlockSpec((rows, unit), lambda g, ids: (0, first + g)),
            ],
            out_specs=[pair, pair],
        ),
        out_shape=[
            jax.ShapeDtypeStruct((2, rows, n), F32),
            jax.ShapeDtypeStruct((2, rows, n), BF),
        ],
        compiler_params=params(),
        cost_estimate=cost(4 * rows * n, 26 * rows * n),
    )(inner, keep, from_a, from_b, residual)


def update(inner, local, arrived, gain, start):
    _, rows, n = local.shape
    unit = 128
    first = start // unit

    def kernel(ids, local, arrived, gain, stream, scaled, squares):
        both = (local[...] + arrived[...].astype(F32)).astype(BF)
        values = both.astype(F32)
        stream[...] = jnp.where(ids[0] == 0, values[0], values[1]).astype(BF)
        scaled[...] = (values * gain[...]).astype(BF)
        part = values[0] * values[0] + values[1] * values[1]

        @pl.when(pl.program_id(0) == 0)
        def _():
            squares[...] = part

        @pl.when(pl.program_id(0) > 0)
        def _():
            squares[...] += part

    pair = pl.BlockSpec((2, rows, unit), lambda g, ids: (0, 0, g))
    flat = pl.BlockSpec((rows, unit), lambda g, ids: (0, g))
    return pl.pallas_call(
        kernel,
        grid_spec=pltpu.PrefetchScalarGridSpec(
            num_scalar_prefetch=1,
            grid=(n // unit,),
            in_specs=[
                pair,
                pair,
                pl.BlockSpec((2, 1, unit), lambda g, ids: (0, 0, first + g)),
            ],
            out_specs=[
                flat,
                pair,
                pl.BlockSpec((rows, unit), lambda g, ids: (0, 0)),
            ],
        ),
        out_shape=[
            jax.ShapeDtypeStruct((rows, n), BF),
            jax.ShapeDtypeStruct((2, rows, n), BF),
            jax.ShapeDtypeStruct((rows, unit), F32),
        ],
        compiler_params=params(),
        cost_estimate=cost(8 * rows * n, 20 * rows * n),
    )(inner, local, arrived, gain)


def pick_weights(weight, row_ids):
    pair = weight.shape[1]

    def spec(t):
        return pl.BlockSpec((UNIT, pair), lambda g, ids: (ids[t], 0))

    def kernel(ids, *refs):
        for j in range(3):
            refs[6 + j][0] = refs[2 * j][...]
            refs[6 + j][1] = refs[2 * j + 1][...]

    return pl.pallas_call(
        kernel,
        grid_spec=pltpu.PrefetchScalarGridSpec(
            num_scalar_prefetch=1,
            grid=(1,),
            in_specs=[spec(t) for t in range(6)],
            out_specs=[
                pl.BlockSpec((2, UNIT, pair), lambda g, ids: (0, 0, 0))
                for _ in range(3)
            ],
        ),
        out_shape=[jax.ShapeDtypeStruct((2, UNIT, pair), BF)] * 3,
        compiler_params=params(),
        cost_estimate=cost(0, 24 * UNIT * pair),
    )(row_ids, *([weight] * 6))


def project(own_rows, scaled, squares, gathered, weight):
    rows = scaled[0].shape[1]
    pair = weight.shape[1]
    units = gathered.shape[0]
    n_chunk = len(scaled)

    def kernel(ids, *refs):
        xs = refs[:n_chunk]
        sq = refs[n_chunk : 2 * n_chunk]
        far, near = refs[2 * n_chunk : 2 * n_chunk + 2]
        m1, m2, m3, own, total, far_buf, near_buf, far_sem, near_sem = refs[
            2 * n_chunk + 2 :
        ]
        copies = []
        for q in range(units):
            one = pltpu.make_async_copy(far.at[q], far_buf.at[q], far_sem.at[q])
            one.start()
            two = []
            for i in range(2):
                at = pl.multiple_of(ids[i] + q * UNIT, UNIT)
                c = pltpu.make_async_copy(
                    near.at[pl.ds(at, UNIT), :], near_buf.at[q, i], near_sem.at[q, i]
                )
                c.start()
                two.append(c)
            copies.append([one] + two)
        acc = [jnp.zeros((rows, pair), F32) for _ in range(4)]
        q = 0
        for x in xs:
            for u in range(x.shape[2] // 128):
                pass
        spans = []
        for x_id, x in enumerate(xs):
            at = 0
            while at < x.shape[2]:
                here = sum(xs[t].shape[2] for t in range(x_id)) + at
                room = UNIT - here % UNIT
                size = min(room, x.shape[2] - at)
                spans.append((x_id, at, here // UNIT, here % UNIT, size))
                at += size
        waited = set()
        for x_id, at, q, inside, size in spans:
            if q not in waited:
                for c in copies[q]:
                    c.wait()
                waited.add(q)
            for i in range(2):
                value = xs[x_id][i, :, at : at + size]
                acc[0] += jnp.dot(
                    value,
                    near_buf[q, i, inside : inside + size, :],
                    preferred_element_type=F32,
                )
                for k in range(3):
                    acc[k + 1] += jnp.dot(
                        value,
                        far_buf[q, k, i, inside : inside + size, :],
                        preferred_element_type=F32,
                    )
        lanes = sq[0][...]
        for other in sq[1:]:
            lanes = lanes + other[...]
        whole = jnp.sum(lanes, axis=1, keepdims=True)
        own[...] = acc[0]
        total[...] = jnp.broadcast_to(whole, total.shape)
        high = whole.astype(BF)
        low = (whole - high.astype(F32)).astype(BF)
        lane = lax.broadcasted_iota(jnp.int32, (rows, 128), 1)
        tail = jnp.where(lane < 64, high.astype(F32), low.astype(F32)).astype(BF)
        for k, m in enumerate((m1, m2, m3)):
            m[:, :pair] = acc[k + 1].astype(BF)
            m[:, pair:] = tail

    return pl.pallas_call(
        kernel,
        in_specs=[SMEM] + [VMEM] * (2 * n_chunk) + [ANY, ANY],
        out_specs=[VMEM] * 5,
        out_shape=[jax.ShapeDtypeStruct((rows, pair + 128), BF)] * 3
        + [
            jax.ShapeDtypeStruct((rows, pair), F32),
            jax.ShapeDtypeStruct((rows, 128), F32),
        ],
        scratch_shapes=[
            pltpu.VMEM((units, 3, 2, UNIT, pair), BF),
            pltpu.VMEM((units, 2, UNIT, pair), BF),
            pltpu.SemaphoreType.DMA((units,)),
            pltpu.SemaphoreType.DMA((units, 2)),
        ],
        compiler_params=params(),
        cost_estimate=cost(2 * rows * 4096 * 1024, 10 * 1024 * 1024),
    )(own_rows, *scaled, *squares, gathered, weight)


def finish(own, total, arrived, width):
    rows, pair = own.shape

    def kernel(own, total, a, b, c, out):
        value = own[...]
        squares = total[:, :1]
        for m in (a, b, c):
            value = value + m[:, :pair].astype(F32)
            tail = m[:, pair:].astype(F32)
            squares = squares + tail[:, :1] + tail[:, 64:65]
        factor = lax.rsqrt(squares * (1.0 / width) + 1e-05)
        out[...] = (value * factor).astype(BF)

    return pl.pallas_call(
        kernel,
        in_specs=[VMEM] * 5,
        out_specs=VMEM,
        out_shape=jax.ShapeDtypeStruct((rows, pair), BF),
        compiler_params=params(),
        cost_estimate=cost(8 * rows * pair, 12 * rows * pair),
    )(own, total, *arrived)


def body(partials, residual, norm_gain, kv_weight):
    partial = partials[0]
    rows, width = partial.shape
    pair = kv_weight.shape[2]
    weight = kv_weight.reshape(width, pair)
    o = lax.axis_index("outer").astype(jnp.int32)
    i = lax.axis_index("inner").astype(jnp.int32)
    q = (lax.axis_index("x") * 2 + lax.axis_index("core")).astype(jnp.int32)
    inner = i.reshape(1)
    block = width // 8
    per_block = block // UNIT

    ids = []
    for k in (1, 2, 3):
        there = (o + k) % OUTER
        ids += [there * per_block + q, (OUTER + there) * per_block + q]
    sent = pick_weights(weight, jnp.stack(ids))
    got = [lax.ppermute(s, "outer", shift(k)) for k, s in zip((1, 2, 3), sent)]
    gathered = lax.all_gather(jnp.stack(got), ("x", "core"), axis=0)

    send_ids = jnp.stack([o ^ 1, o ^ 2, OUTER + (o ^ 3), OUTER + (o ^ 2)])
    keep_ids = jnp.stack([o, o ^ 3, OUTER + o, OUTER + (o ^ 1)])
    gain = lax.dynamic_index_in_dim(
        norm_gain.reshape(2, OUTER, block), o, 1, keepdims=True
    )
    streams, scaled, squares = [], [], []
    start = 0
    for n in CHUNKS:
        to_a, to_b = pick_columns(partial, send_ids, n, start, 2)
        from_a = lax.ppermute(to_a, "outer", PAIR_A)
        from_b = lax.ppermute(to_b, "outer", PAIR_B)
        to_a, to_b, keep = first_add(partial, keep_ids, from_a, from_b, start)
        from_a = lax.ppermute(to_a, "outer", PAIR_A)
        from_b = lax.ppermute(to_b, "outer", PAIR_B)
        local, to_z = second_add(inner, keep, from_a, from_b, residual, start)
        from_z = lax.ppermute(to_z, "inner", SWAP)
        s, x, sq = update(inner, local, from_z, gain, start)
        streams.append(s)
        scaled.append(x)
        squares.append(sq)
        start += n

    own_rows = jnp.stack([o * block, (OUTER + o) * block])
    *messages, own, total = project(own_rows, scaled, squares, gathered, weight)
    arrived = [
        lax.ppermute(m, "outer", shift(-k)) for k, m in zip((1, 2, 3), messages)
    ]
    kv = finish(own, total, arrived, width)
    stream = jnp.concatenate(streams, axis=1)
    return stream, kv.reshape(rows, 1, pair)


def solution(mesh):
    fine = Mesh(
        mesh.devices.reshape(4, 4, 2, 2, 4), ("x", "z_lo", "core", "inner", "outer")
    )
    dp = ("x", "z_lo", "core")
    placed = (
        P((*dp, "inner", "outer"), None, None),
        P(dp, ("inner", "outer")),
        P(),
        P(None, ("inner", "outer"), None),
    )
    return jax.shard_map(
        body,
        mesh=fine,
        in_specs=placed,
        out_specs=(P(dp, ("inner", "outer")), P(dp, ("inner", "outer"), None)),
        check_vma=False,
    )
```

time: 289 us -> 153 us (0.53)
  waiting for transfers between devices: 237 us -> 40.4 us
  starting transfers between devices: 0.11 us -> 44.7 us
  Pallas kernels: 0 us -> 36.5 us
  blocking collectives: 28.9 us -> 0 us
  local copies, waits for them, and re-layouts: 0.71 us -> 13.7 us
  matrix products: 6.52 us -> 0 us
    reduce_scatter x2 -> x0, waiting for transfers between devices: 139 us -> none  [the longest x1 108 us: body(): lax.psum_scatter(own_part.astype(jnp.bfloat16), 'inner', scatter_dimensio...]
    all_gather x1, waiting for transfers between devices: 97.4 us -> 0.02 us  [body(): gathered = lax.all_gather(jnp.stack(got), ('x', 'core'), axis=0)]
    ppermute x0 -> x26, starting transfers between devices: none -> 44.7 us  [the longest x8 13.1 us: body(): from_b = lax.ppermute(to_b, 'outer', PAIR_B)]
    ppermute x0 -> x26, waiting for transfers between devices: none -> 40.4 us  [the longest x4 18.1 us: body(): from_z = lax.ppermute(to_z, 'inner', SWAP)]
    pallas_call x0 -> x19, Pallas kernels: none -> 36.5 us  [the longest x4 8.72 us: first_add(): pl.pallas_call(kernel, grid_spec=pltpu.PrefetchScalarGridSpec(num_scalar_...]
    psum x1 -> x0, blocking collectives: 28.9 us -> none  [body(): squares = lax.psum(jnp.sum(values * values, axis=1), ('inner', 'outer'))]
    unnamed x4 -> x36, local copies, waits for them, and re-layouts: 0.01 us -> 12.1 us
    dot_general x1 -> x0, matrix products: 6.52 us -> none  [body(): jnp.dot(lax.all_gather(normed, ('inner', 'outer'), axis=1, tiled=True), f...]
  transfers between devices with their start and end apart: 3 -> 27, of which waited for: 3 -> 9; matrix products, arithmetic and copies ran while one was open for 0% -> 2% of each run, Pallas kernels for 0% -> 19%
where the time goes in v1:
time: 153 us; the launch traced here: 152 us
  starting transfers between devices  44.7 us (29%)
  waiting for transfers between devices  40.4 us (26%)
  Pallas kernels  36.5 us (24%)
  between operations  14.3 us (9%)
  local copies, waits for them, and re-layouts  13.7 us (9%)
  other arithmetic  2.03 us (1%)
    ppermute x4, waiting for transfers between devices, body(): from_z = lax.ppermute(to_z, 'inner', SWAP)  18.1 us
    ppermute x8, starting transfers between devices, body(): from_b = lax.ppermute(to_b, 'outer', PAIR_B)  13.1 us
    ppermute x4, starting transfers between devices, body(): from_z = lax.ppermute(to_z, 'inner', SWAP)  12.2 us
    unnamed x36, local copies, waits for them, and re-layouts  12.1 us
    ppermute x3, waiting for transfers between devices, body(): got = [lax.ppermute(s, 'outer', shift(k)) for k, s in zip((1, 2, 3), sent)]  10.3 us
    pallas_call x4, Pallas kernels, first_add(): pl.pallas_call(kernel, grid_spec=pltpu.PrefetchScalarGridSpec(num_scalar_...  8.72 us
    pallas_call x4, Pallas kernels, second_add(): pl.pallas_call(kernel, grid_spec=pltpu.PrefetchScalarGridSpec(num_scalar_...  8.72 us
    pallas_call x4, Pallas kernels, pick_columns(): pl.pallas_call(kernel, grid_spec=pltpu.PrefetchScalarGridSpec(num_scalar_...  7.96 us
  transfers between devices with their start and end apart: 27, of which 9 were waited for; matrix products, arithmetic and copies ran while one was open for 2% of the time, Pallas kernels for 19%

profile of v1, /device:TPU:32, one launch (start us, length us, event | category | flops | bytes accessed | tf_op | source)
XLA Modules:
  0.0 151.6 jit_solution(12868390655567307903)
XLA Ops:
  10.8 2.9 %collective-permute-start.21 = (bf16[2,256,256]{2,1,0:T(8,128)(2,1)S(1)}, bf16[2,256,256]{2,1,0:T(8,128)(2,1)S(1)}, u32[]{:S(2)}, u32[]{:S(2)}) collective-permute-start(bf16[2,256,256]{2,1,0:T(8,128)(2,1)S(1)} %get-tuple-element.91), channel_id=1, source_target_pairs={{0,2},{1,3},{2,0},{3,1},{4,6},{5,7},{6,4},{7,5},{8,10},{9,11},{10,... | collective-permute-start | bytes 786440 | tf_op jit(solution)/shard_map/ppermute | solution.py:355
  15.0 3.5 %collective-permute-done.20 = bf16[2,256,256]{2,1,0:T(8,128)(2,1)S(1)} collective-permute-done((bf16[2,256,256]{2,1,0:T(8,128)(2,1)S(1)}, bf16[2,256,256]{2,1,0:T(8,128)(2,1)S(1)}, u32[]{:S(2)}, u32[]{:S(2)}) %collective-permute-start.20) | collective-permute-done | bytes 262176 | tf_op jit(solution)/shard_map/ppermute | solution.py:355
  18.5 6.8 %collective-permute-done.21 = bf16[2,256,256]{2,1,0:T(8,128)(2,1)S(1)} collective-permute-done((bf16[2,256,256]{2,1,0:T(8,128)(2,1)S(1)}, bf16[2,256,256]{2,1,0:T(8,128)(2,1)S(1)}, u32[]{:S(2)}, u32[]{:S(2)}) %collective-permute-start.21) | collective-permute-done | bytes 262176 | tf_op jit(solution)/shard_map/ppermute | solution.py:355
  26.4 2.1 %copy-done = bf16[1,120,16384]{2,1,0:T(8,128)(2,1)S(1)} copy-done((bf16[1,120,16384]{2,1,0:T(8,128)(2,1)S(1)}, bf16[1,120,16384]{2,1,0:T(8,128)(2,1)}, u32[]{:S(2)}) %copy-start) | copy-done | bytes 3932184
  34.7 2.7 %shard_map.71 = (bf16[2,120,640]{2,1,0:T(8,128)(2,1)}, bf16[2,120,640]{2,1,0:T(8,128)(2,1)S(1)}) custom-call(s32[4]{0:T(128)S(1)} %pad_add_fusion.1.ids, bf16[120,16384]{1,0:T(8,128)(2,1)S(1)} %bitcast.32, bf16[120,16384]{1,0:T(8,128)(2,1)S(1)} %bitcast.33, bf16[120,16384]{1,0:T(8,128)(2,1)S(1)} %bitcast.34, bf16[120,16384]{1,0:T(8,128)(2,1)S(1)} %bitcast.35), custom_call_target="tpu_custom_call" | custom-call | bytes 1228800 | tf_op jit(solution)/shard_map/pallas_call | solution.py:53
  40.3 2.8 %shard_map.67 = (bf16[2,120,640]{2,1,0:T(8,128)(2,1)S(1)}, bf16[2,120,640]{2,1,0:T(8,128)(2,1)}) custom-call(s32[4]{0:T(128)S(1)} %pad_add_fusion.1.ids, bf16[120,16384]{1,0:T(8,128)(2,1)S(1)} %bitcast.39, bf16[120,16384]{1,0:T(8,128)(2,1)S(1)} %bitcast.37, bf16[120,16384]{1,0:T(8,128)(2,1)S(1)} %bitcast.38, bf16[120,16384]{1,0:T(8,128)(2,1)S(1)} %bitcast.36), custom_call_target="tpu_custom_call" | custom-call | bytes 1228800 | tf_op jit(solution)/shard_map/pallas_call | solution.py:53
  46.5 2.2 %copy-done.1 = bf16[1,120,16384]{2,1,0:T(8,128)(2,1)S(1)} copy-done((bf16[1,120,16384]{2,1,0:T(8,128)(2,1)S(1)}, bf16[1,120,16384]{2,1,0:T(8,128)(2,1)}, u32[]{:S(2)}) %copy-start.1) | copy-done | bytes 3932184
  48.7 2.2 %shard_map.64 = (bf16[120,512]{1,0:T(8,128)(2,1)S(1)}, bf16[120,512]{1,0:T(8,128)(2,1)}, f32[2,120,512]{2,1,0:T(8,128)S(1)}) custom-call(s32[4]{0:T(128)S(1)} %pad_add_fusion.ids, bf16[120,16384]{1,0:T(8,128)(2,1)S(1)} %bitcast.40, bf16[120,16384]{1,0:T(8,128)(2,1)S(1)} %bitcast.41, bf16[120,16384]{1,0:T(8,128)(2,1)S(1)} %bitcast.42, ...), custom_call_target="tpu_custom_call" | custom-call | flops 245760 | bytes 1720320 | tf_op jit(solution)/shard_map/pallas_call | solution.py:89
  50.9 5.9 %collective-permute-done.1.rb = bf16[2,120,256]{2,1,0:T(8,128)(2,1)S(1)} collective-permute-done((bf16[2,120,256]{2,1,0:T(8,128)(2,1)}, bf16[2,120,256]{2,1,0:T(8,128)(2,1)S(1)}, u32[]{:S(2)}, u32[]{:S(2)}) %collective-permute-start.1) | collective-permute-done | bytes 122912 | tf_op jit(solution)/shard_map/ppermute | solution.py:368
  57.8 2.1 %collective-permute-start.2 = (bf16[120,256]{1,0:T(8,128)(2,1)S(1)}, bf16[120,256]{1,0:T(8,128)(2,1)S(1)}, u32[]{:S(2)}, u32[]{:S(2)}) collective-permute-start(bf16[120,256]{1,0:T(8,128)(2,1)S(1)} %get-tuple-element.53), channel_id=1, source_target_pairs={{0,1},{1,0},{2,3},{3,2},{4,5},{5,4},{6,7},{7,6},{8,9},{9,8},{10,11... | collective-permute-start | bytes 184328 | tf_op jit(solution)/shard_map/ppermute | solution.py:370
  61.1 2.8 %shard_map.72 = (bf16[120,640]{1,0:T(8,128)(2,1)}, bf16[120,640]{1,0:T(8,128)(2,1)}, f32[2,120,640]{2,1,0:T(8,128)S(1)}) custom-call(s32[4]{0:T(128)S(1)} %pad_add_fusion.ids, bf16[120,16384]{1,0:T(8,128)(2,1)S(1)} %bitcast.48, bf16[120,16384]{1,0:T(8,128)(2,1)S(1)} %bitcast.49, bf16[120,16384]{1,0:T(8,128)(2,1)S(1)} %bitcast.50, ...), custom_call_target="tpu_custom_call" | custom-call | flops 307200 | bytes 2150400 | tf_op jit(solution)/shard_map/pallas_call | solution.py:89
  63.9 2.1 %collective-permute-start.18 = (bf16[120,640]{1,0:T(8,128)(2,1)}, bf16[120,640]{1,0:T(8,128)(2,1)}, u32[]{:S(2)}, u32[]{:S(2)}) collective-permute-start(bf16[120,640]{1,0:T(8,128)(2,1)} %get-tuple-element.78), channel_id=1, source_target_pairs={{0,3},{1,2},{2,1},{3,0},{4,7},{5,6},{6,5},{7,4},{8,11},{9,10},{10,... | collective-permute-start | bytes 460808 | tf_op jit(solution)/shard_map/ppermute | solution.py:371
  66.1 2.8 %shard_map.68 = (bf16[120,640]{1,0:T(8,128)(2,1)}, bf16[120,640]{1,0:T(8,128)(2,1)}, f32[2,120,640]{2,1,0:T(8,128)S(1)}) custom-call(s32[4]{0:T(128)S(1)} %pad_add_fusion.ids, bf16[120,16384]{1,0:T(8,128)(2,1)S(1)} %bitcast.52, bf16[120,16384]{1,0:T(8,128)(2,1)S(1)} %bitcast.53, bf16[120,16384]{1,0:T(8,128)(2,1)S(1)} %bitcast.54, ...), custom_call_target="tpu_custom_call" | custom-call | flops 307200 | bytes 2150400 | tf_op jit(solution)/shard_map/pallas_call | solution.py:89
  79.6 6.3 %collective-permute-start.4 = (bf16[2,120,256]{2,1,0:T(8,128)(2,1)}, bf16[2,120,256]{2,1,0:T(8,128)(2,1)}, u32[]{:S(2)}, u32[]{:S(2)}) collective-permute-start(bf16[2,120,256]{2,1,0:T(8,128)(2,1)} %get-tuple-element.56), channel_id=1, source_target_pairs={{0,4},{4,0},{1,5},{5,1},{2,6},{6,2},{3,7},{7,3},{8,12},{12,8},{9,1... | collective-permute-start | bytes 368648 | tf_op jit(solution)/shard_map/ppermute | solution.py:373
  89.3 3.1 %shard_map.73 = (f32[2,120,640]{2,1,0:T(8,128)S(1)}, bf16[2,120,640]{2,1,0:T(8,128)(2,1)}) custom-call(s32[1]{0:T(128)} %bitcast.ids, f32[2,120,640]{2,1,0:T(8,128)S(1)} %get-tuple-element.76.keep, bf16[120,640]{1,0:T(8,128)(2,1)S(1)} %collective-permute-done.17.ra, bf16[120,640]{1,0:T(8,128)(2,1)} %collective-permute-done.18.rb, bf16[120,2048]{1,0:T(8,128)(2,1)S(1)} %copy-done.2), custom_call_target="tpu_custom_call" | custom-call | flops 307200 | bytes 1996800 | tf_op jit(solution)/shard_map/pallas_call | solution.py:124
  92.4 5.9 %collective-permute-start.19 = (bf16[2,120,640]{2,1,0:T(8,128)(2,1)}, bf16[2,120,640]{2,1,0:T(8,128)(2,1)S(1)}, u32[]{:S(2)}, u32[]{:S(2)}) collective-permute-start(bf16[2,120,640]{2,1,0:T(8,128)(2,1)} %get-tuple-element.80), channel_id=1, source_target_pairs={{0,4},{4,0},{1,5},{5,1},{2,6},{6,2},{3,7},{7,3},{8,12},{12,8},{9,1... | collective-permute-start | bytes 921608 | tf_op jit(solution)/shard_map/ppermute | solution.py:373
  98.3 3.2 %shard_map.69 = (f32[2,120,640]{2,1,0:T(8,128)S(1)}, bf16[2,120,640]{2,1,0:T(8,128)(2,1)}) custom-call(s32[1]{0:T(128)} %bitcast.ids, f32[2,120,640]{2,1,0:T(8,128)S(1)} %get-tuple-element.68.keep, bf16[120,640]{1,0:T(8,128)(2,1)} %collective-permute-done.12.ra, bf16[120,640]{1,0:T(8,128)(2,1)} %collective-permute-done.13.rb, bf16[120,2048]{1,0:T(8,128)(2,1)S(1)} %copy-done.2), custom_call_target="tpu_custom_call" | custom-call | flops 307200 | bytes 1996800 | tf_op jit(solution)/shard_map/pallas_call | solution.py:124
  104.1 3.6 %collective-permute-done.9.arrived = bf16[2,120,512]{2,1,0:T(8,128)(2,1)} collective-permute-done((bf16[2,120,512]{2,1,0:T(8,128)(2,1)}, bf16[2,120,512]{2,1,0:T(8,128)(2,1)}, u32[]{:S(2)}, u32[]{:S(2)}) %collective-permute-start.9) | collective-permute-done | bytes 245792 | tf_op jit(solution)/shard_map/ppermute | solution.py:373
  109.7 9.4 %collective-permute-done.19.arrived = bf16[2,120,640]{2,1,0:T(8,128)(2,1)S(1)} collective-permute-done((bf16[2,120,640]{2,1,0:T(8,128)(2,1)}, bf16[2,120,640]{2,1,0:T(8,128)(2,1)S(1)}, u32[]{:S(2)}, u32[]{:S(2)}) %collective-permute-start.19) | collective-permute-done | bytes 307232 | tf_op jit(solution)/shard_map/ppermute | solution.py:373
  119.6 5.1 %collective-permute-done.14.arrived = bf16[2,120,640]{2,1,0:T(8,128)(2,1)S(1)} collective-permute-done((bf16[2,120,640]{2,1,0:T(8,128)(2,1)}, bf16[2,120,640]{2,1,0:T(8,128)(2,1)S(1)}, u32[]{:S(2)}, u32[]{:S(2)}) %collective-permute-start.14) | collective-permute-done | bytes 307232 | tf_op jit(solution)/shard_map/ppermute | solution.py:373
  127.9 4.5 %shard_map.76 = (bf16[120,384]{1,0:T(8,128)(2,1)S(1)}, bf16[120,384]{1,0:T(8,128)(2,1)S(1)}, bf16[120,384]{1,0:T(8,128)(2,1)S(1)}, f32[120,256]{1,0:T(8,128)S(1)}, f32[120,128]{1,0:T(8,128)S(1)}) custom-call(s32[2]{0:T(128)S(1)} %pad_add_fusion.2.ids, bf16[2,120,256]{2,1,0:T(8,128)(2,1)S(1)} %copy-done.8, ...), custom_call_target="tpu_custom_call" | custom-call | flops 1006632960 | bytes 10485760 | tf_op jit(solution)/shard_map/pallas_call | solution.py:295
  132.4 2.5 %collective-permute-start.23 = (bf16[120,384]{1,0:T(8,128)(2,1)S(1)}, bf16[120,384]{1,0:T(8,128)(2,1)S(1)}, u32[]{:S(2)}, u32[]{:S(2)}) collective-permute-start(bf16[120,384]{1,0:T(8,128)(2,1)S(1)} %get-tuple-element.95), channel_id=1, source_target_pairs={{0,3},{1,0},{2,1},{3,2},{4,7},{5,4},{6,5},{7,6},{8,11},{9,8},{10,9... | collective-permute-start | bytes 276488 | tf_op jit(solution)/shard_map/ppermute | solution.py:383
  135.0 3.3 %collective-permute-start.24 = (bf16[120,384]{1,0:T(8,128)(2,1)S(1)}, bf16[120,384]{1,0:T(8,128)(2,1)S(1)}, u32[]{:S(2)}, u32[]{:S(2)}) collective-permute-start(bf16[120,384]{1,0:T(8,128)(2,1)S(1)} %get-tuple-element.96), channel_id=1, source_target_pairs={{0,2},{1,3},{2,0},{3,1},{4,6},{5,7},{6,4},{7,5},{8,10},{9,11},{10,... | collective-permute-start | bytes 276488 | tf_op jit(solution)/shard_map/ppermute | solution.py:383
  141.0 3.0 %collective-permute-done.25.c = bf16[120,384]{1,0:T(8,128)(2,1)S(1)} collective-permute-done((bf16[120,384]{1,0:T(8,128)(2,1)S(1)}, bf16[120,384]{1,0:T(8,128)(2,1)S(1)}, u32[]{:S(2)}, u32[]{:S(2)}) %collective-permute-start.25) | collective-permute-done | bytes 92192 | tf_op jit(solution)/shard_map/ppermute | solution.py:383
  (94 shorter events, 46.6 us)
Async XLA Ops:
  7.2 118.1 %all-gather.3.cloned.1.call-start = ((), (), s32[]{:S(2)}) async-start(), calls=%async_computation | async-start | bytes 7077888 | tf_op jit(solution)/shard_map/all_gather | solution.py:356
  9.1 9.4 %collective-permute-start.20 = (bf16[2,256,256]{2,1,0:T(8,128)(2,1)S(1)}, bf16[2,256,256]{2,1,0:T(8,128)(2,1)S(1)}, u32[]{:S(2)}, u32[]{:S(2)}) collective-permute-start(bf16[2,256,256]{2,1,0:T(8,128)(2,1)S(1)} %get-tuple-element.90), channel_id=1, source_target_pairs={{0,1},{1,2},{2,3},{3,0},{4,5},{5,6},{6,7},{7,4},{8,9},{9,10},{10,1... | collective-permute-start | bytes 786440 | tf_op jit(solution)/shard_map/ppermute | solution.py:355
  10.8 14.5 %collective-permute-start.21 = (bf16[2,256,256]{2,1,0:T(8,128)(2,1)S(1)}, bf16[2,256,256]{2,1,0:T(8,128)(2,1)S(1)}, u32[]{:S(2)}, u32[]{:S(2)}) collective-permute-start(bf16[2,256,256]{2,1,0:T(8,128)(2,1)S(1)} %get-tuple-element.91), channel_id=1, source_target_pairs={{0,2},{1,3},{2,0},{3,1},{4,6},{5,7},{6,4},{7,5},{8,10},{9,11},{10,... | collective-permute-start | bytes 786440 | tf_op jit(solution)/shard_map/ppermute | solution.py:355
  13.7 11.6 %collective-permute-start.22 = (bf16[2,256,256]{2,1,0:T(8,128)(2,1)S(1)}, bf16[2,256,256]{2,1,0:T(8,128)(2,1)S(1)}, u32[]{:S(2)}, u32[]{:S(2)}) collective-permute-start(bf16[2,256,256]{2,1,0:T(8,128)(2,1)S(1)} %get-tuple-element.92), channel_id=1, source_target_pairs={{0,3},{1,0},{2,1},{3,2},{4,7},{5,4},{6,5},{7,6},{8,11},{9,8},{10,9... | collective-permute-start | bytes 786440 | tf_op jit(solution)/shard_map/ppermute | solution.py:355
  29.6 13.5 %collective-permute-start.5 = (bf16[2,120,512]{2,1,0:T(8,128)(2,1)S(1)}, bf16[2,120,512]{2,1,0:T(8,128)(2,1)S(1)}, u32[]{:S(2)}, u32[]{:S(2)}) collective-permute-start(bf16[2,120,512]{2,1,0:T(8,128)(2,1)S(1)} %get-tuple-element.58), channel_id=1, source_target_pairs={{0,1},{1,0},{2,3},{3,2},{4,5},{5,4},{6,7},{7,6},{8,9},{9,8},{10,11... | collective-permute-start | bytes 737288 | tf_op jit(solution)/shard_map/ppermute | solution.py:367
  30.9 14.1 %collective-permute-start.6 = (bf16[2,120,512]{2,1,0:T(8,128)(2,1)S(1)}, bf16[2,120,512]{2,1,0:T(8,128)(2,1)S(1)}, u32[]{:S(2)}, u32[]{:S(2)}) collective-permute-start(bf16[2,120,512]{2,1,0:T(8,128)(2,1)S(1)} %get-tuple-element.59), channel_id=1, source_target_pairs={{0,3},{1,2},{2,1},{3,0},{4,7},{5,6},{6,5},{7,4},{8,11},{9,10},{10,... | collective-permute-start | bytes 737288 | tf_op jit(solution)/shard_map/ppermute | solution.py:368
  34.3 8.8 %collective-permute-start = (bf16[2,120,256]{2,1,0:T(8,128)(2,1)S(1)}, bf16[2,120,256]{2,1,0:T(8,128)(2,1)S(1)}, u32[]{:S(2)}, u32[]{:S(2)}) collective-permute-start(bf16[2,120,256]{2,1,0:T(8,128)(2,1)S(1)} %get-tuple-element.50), channel_id=1, source_target_pairs={{0,1},{1,0},{2,3},{3,2},{4,5},{5,4},{6,7},{7,6},{8,9},{9,8},{10,11... | collective-permute-start | bytes 368648 | tf_op jit(solution)/shard_map/ppermute | solution.py:367
  37.4 20.4 %collective-permute-start.15 = (bf16[2,120,640]{2,1,0:T(8,128)(2,1)}, bf16[2,120,640]{2,1,0:T(8,128)(2,1)S(1)}, u32[]{:S(2)}, u32[]{:S(2)}) collective-permute-start(bf16[2,120,640]{2,1,0:T(8,128)(2,1)} %get-tuple-element.74), channel_id=1, source_target_pairs={{0,1},{1,0},{2,3},{3,2},{4,5},{5,4},{6,7},{7,6},{8,9},{9,8},{10,11... | collective-permute-start | bytes 921608 | tf_op jit(solution)/shard_map/ppermute | solution.py:367
  39.0 21.0 %collective-permute-start.16 = (bf16[2,120,640]{2,1,0:T(8,128)(2,1)S(1)}, bf16[2,120,640]{2,1,0:T(8,128)(2,1)S(1)}, u32[]{:S(2)}, u32[]{:S(2)}) collective-permute-start(bf16[2,120,640]{2,1,0:T(8,128)(2,1)S(1)} %get-tuple-element.75), channel_id=1, source_target_pairs={{0,3},{1,2},{2,1},{3,0},{4,7},{5,6},{6,5},{7,4},{8,11},{9,10},{10,... | collective-permute-start | bytes 921608 | tf_op jit(solution)/shard_map/ppermute | solution.py:368
  43.1 20.8 %collective-permute-start.10 = (bf16[2,120,640]{2,1,0:T(8,128)(2,1)S(1)}, bf16[2,120,640]{2,1,0:T(8,128)(2,1)S(1)}, u32[]{:S(2)}, u32[]{:S(2)}) collective-permute-start(bf16[2,120,640]{2,1,0:T(8,128)(2,1)S(1)} %get-tuple-element.66), channel_id=1, source_target_pairs={{0,1},{1,0},{2,3},{3,2},{4,5},{5,4},{6,7},{7,6},{8,9},{9,8},{10,11... | collective-permute-start | bytes 921608 | tf_op jit(solution)/shard_map/ppermute | solution.py:367
  43.1 20.8 %collective-permute-start.11 = (bf16[2,120,640]{2,1,0:T(8,128)(2,1)}, bf16[2,120,640]{2,1,0:T(8,128)(2,1)S(1)}, u32[]{:S(2)}, u32[]{:S(2)}) collective-permute-start(bf16[2,120,640]{2,1,0:T(8,128)(2,1)} %get-tuple-element.67), channel_id=1, source_target_pairs={{0,3},{1,2},{2,1},{3,0},{4,7},{5,6},{6,5},{7,4},{8,11},{9,10},{10,... | collective-permute-start | bytes 921608 | tf_op jit(solution)/shard_map/ppermute | solution.py:368
  45.1 11.8 %collective-permute-start.1 = (bf16[2,120,256]{2,1,0:T(8,128)(2,1)}, bf16[2,120,256]{2,1,0:T(8,128)(2,1)S(1)}, u32[]{:S(2)}, u32[]{:S(2)}) collective-permute-start(bf16[2,120,256]{2,1,0:T(8,128)(2,1)} %get-tuple-element.51), channel_id=1, source_target_pairs={{0,3},{1,2},{2,1},{3,0},{4,7},{5,6},{6,5},{7,4},{8,11},{9,10},{10,... | collective-permute-start | bytes 368648 | tf_op jit(solution)/shard_map/ppermute | solution.py:368
  56.9 15.1 %collective-permute-start.7 = (bf16[120,512]{1,0:T(8,128)(2,1)S(1)}, bf16[120,512]{1,0:T(8,128)(2,1)S(1)}, u32[]{:S(2)}, u32[]{:S(2)}) collective-permute-start(bf16[120,512]{1,0:T(8,128)(2,1)S(1)} %get-tuple-element.61), channel_id=1, source_target_pairs={{0,1},{1,0},{2,3},{3,2},{4,5},{5,4},{6,7},{7,6},{8,9},{9,8},{10,11... | collective-permute-start | bytes 368648 | tf_op jit(solution)/shard_map/ppermute | solution.py:370
  57.8 11.0 %collective-permute-start.2 = (bf16[120,256]{1,0:T(8,128)(2,1)S(1)}, bf16[120,256]{1,0:T(8,128)(2,1)S(1)}, u32[]{:S(2)}, u32[]{:S(2)}) collective-permute-start(bf16[120,256]{1,0:T(8,128)(2,1)S(1)} %get-tuple-element.53), channel_id=1, source_target_pairs={{0,1},{1,0},{2,3},{3,2},{4,5},{5,4},{6,7},{7,6},{8,9},{9,8},{10,11... | collective-permute-start | bytes 184328 | tf_op jit(solution)/shard_map/ppermute | solution.py:370
  60.0 10.2 %collective-permute-start.3 = (bf16[120,256]{1,0:T(8,128)(2,1)S(1)}, bf16[120,256]{1,0:T(8,128)(2,1)S(1)}, u32[]{:S(2)}, u32[]{:S(2)}) collective-permute-start(bf16[120,256]{1,0:T(8,128)(2,1)S(1)} %get-tuple-element.54), channel_id=1, source_target_pairs={{0,3},{1,2},{2,1},{3,0},{4,7},{5,6},{6,5},{7,4},{8,11},{9,10},{10,... | collective-permute-start | bytes 184328 | tf_op jit(solution)/shard_map/ppermute | solution.py:371
  63.9 25.4 %collective-permute-start.17 = (bf16[120,640]{1,0:T(8,128)(2,1)}, bf16[120,640]{1,0:T(8,128)(2,1)S(1)}, u32[]{:S(2)}, u32[]{:S(2)}) collective-permute-start(bf16[120,640]{1,0:T(8,128)(2,1)} %get-tuple-element.77), channel_id=1, source_target_pairs={{0,1},{1,0},{2,3},{3,2},{4,5},{5,4},{6,7},{7,6},{8,9},{9,8},{10,11... | collective-permute-start | bytes 460808 | tf_op jit(solution)/shard_map/ppermute | solution.py:370
  63.9 25.3 %collective-permute-start.18 = (bf16[120,640]{1,0:T(8,128)(2,1)}, bf16[120,640]{1,0:T(8,128)(2,1)}, u32[]{:S(2)}, u32[]{:S(2)}) collective-permute-start(bf16[120,640]{1,0:T(8,128)(2,1)} %get-tuple-element.78), channel_id=1, source_target_pairs={{0,3},{1,2},{2,1},{3,0},{4,7},{5,6},{6,5},{7,4},{8,11},{9,10},{10,... | collective-permute-start | bytes 460808 | tf_op jit(solution)/shard_map/ppermute | solution.py:371
  68.9 29.4 %collective-permute-start.12 = (bf16[120,640]{1,0:T(8,128)(2,1)}, bf16[120,640]{1,0:T(8,128)(2,1)}, u32[]{:S(2)}, u32[]{:S(2)}) collective-permute-start(bf16[120,640]{1,0:T(8,128)(2,1)} %get-tuple-element.69), channel_id=1, source_target_pairs={{0,1},{1,0},{2,3},{3,2},{4,5},{5,4},{6,7},{7,6},{8,9},{9,8},{10,11... | collective-permute-start | bytes 460808 | tf_op jit(solution)/shard_map/ppermute | solution.py:370
  70.8 27.5 %collective-permute-start.13 = (bf16[120,640]{1,0:T(8,128)(2,1)}, bf16[120,640]{1,0:T(8,128)(2,1)}, u32[]{:S(2)}, u32[]{:S(2)}) collective-permute-start(bf16[120,640]{1,0:T(8,128)(2,1)} %get-tuple-element.70), channel_id=1, source_target_pairs={{0,3},{1,2},{2,1},{3,0},{4,7},{5,6},{6,5},{7,4},{8,11},{9,10},{10,... | collective-permute-start | bytes 460808 | tf_op jit(solution)/shard_map/ppermute | solution.py:371
  79.6 22.9 %collective-permute-start.4 = (bf16[2,120,256]{2,1,0:T(8,128)(2,1)}, bf16[2,120,256]{2,1,0:T(8,128)(2,1)}, u32[]{:S(2)}, u32[]{:S(2)}) collective-permute-start(bf16[2,120,256]{2,1,0:T(8,128)(2,1)} %get-tuple-element.56), channel_id=1, source_target_pairs={{0,4},{4,0},{1,5},{5,1},{2,6},{6,2},{3,7},{7,3},{8,12},{12,8},{9,1... | collective-permute-start | bytes 368648 | tf_op jit(solution)/shard_map/ppermute | solution.py:373
  89.3 18.4 %collective-permute-start.9 = (bf16[2,120,512]{2,1,0:T(8,128)(2,1)}, bf16[2,120,512]{2,1,0:T(8,128)(2,1)}, u32[]{:S(2)}, u32[]{:S(2)}) collective-permute-start(bf16[2,120,512]{2,1,0:T(8,128)(2,1)} %get-tuple-element.64), channel_id=1, source_target_pairs={{0,4},{4,0},{1,5},{5,1},{2,6},{6,2},{3,7},{7,3},{8,12},{12,8},{9,1... | collective-permute-start | bytes 737288 | tf_op jit(solution)/shard_map/ppermute | solution.py:373
  92.4 26.7 %collective-permute-start.19 = (bf16[2,120,640]{2,1,0:T(8,128)(2,1)}, bf16[2,120,640]{2,1,0:T(8,128)(2,1)S(1)}, u32[]{:S(2)}, u32[]{:S(2)}) collective-permute-start(bf16[2,120,640]{2,1,0:T(8,128)(2,1)} %get-tuple-element.80), channel_id=1, source_target_pairs={{0,4},{4,0},{1,5},{5,1},{2,6},{6,2},{3,7},{7,3},{8,12},{12,8},{9,1... | collective-permute-start | bytes 921608 | tf_op jit(solution)/shard_map/ppermute | solution.py:373
  101.5 23.2 %collective-permute-start.14 = (bf16[2,120,640]{2,1,0:T(8,128)(2,1)}, bf16[2,120,640]{2,1,0:T(8,128)(2,1)S(1)}, u32[]{:S(2)}, u32[]{:S(2)}) collective-permute-start(bf16[2,120,640]{2,1,0:T(8,128)(2,1)} %get-tuple-element.72), channel_id=1, source_target_pairs={{0,4},{4,0},{1,5},{5,1},{2,6},{6,2},{3,7},{7,3},{8,12},{12,8},{9,1... | collective-permute-start | bytes 921608 | tf_op jit(solution)/shard_map/ppermute | solution.py:373
  132.4 7.5 %collective-permute-start.23 = (bf16[120,384]{1,0:T(8,128)(2,1)S(1)}, bf16[120,384]{1,0:T(8,128)(2,1)S(1)}, u32[]{:S(2)}, u32[]{:S(2)}) collective-permute-start(bf16[120,384]{1,0:T(8,128)(2,1)S(1)} %get-tuple-element.95), channel_id=1, source_target_pairs={{0,3},{1,0},{2,1},{3,2},{4,7},{5,4},{6,5},{7,6},{8,11},{9,8},{10,9... | collective-permute-start | bytes 276488 | tf_op jit(solution)/shard_map/ppermute | solution.py:383
  (21 other events, 119.9 us)
Sparse Core Ops, SparseCore 0:
  26.4 45.4 all-gather.2

commit v2 on v0

v2 whole, which is shorter than its diff:
```python
import jax
import jax.numpy as jnp
from jax import lax
from jax.experimental import pallas as pl
from jax.experimental.pallas import tpu as pltpu
from jax.sharding import Mesh
from jax.sharding import PartitionSpec as P

BF = jnp.bfloat16
F32 = jnp.float32
OUTER = 4
UNIT = 256
CHUNKS = ((0, 512), (512, 896), (1408, 640))
ANY = pl.BlockSpec(memory_space=pl.ANY)
HBM = pl.BlockSpec(memory_space=pltpu.HBM)
VMEM = pl.BlockSpec(memory_space=pltpu.VMEM)
SMEM = pl.BlockSpec(memory_space=pltpu.SMEM)
PAIR_A = [(o, o ^ 1) for o in range(4)]
PAIR_B = [(o, o ^ 3) for o in range(4)]
SWAP = [(0, 1), (1, 0)]
MB = 1024 * 1024
COSTS = (12.0, 10.0, 10.0, 12.0)
COPY = pltpu.SemaphoreType.DMA


def shift(k):
    return [(o, (o + k) % 4) for o in range(4)]


def sds(*shape, dtype=BF):
    return pltpu.VMEM(shape, dtype)


def pin(*arrays):
    return [pltpu.with_memory_space_constraint(a, pltpu.HBM) for a in arrays]


def call(
    name, kernel, ids, args, in_specs, out_shape, scratch=(), after=(), mb=4, out_specs=None
):
    share = 0.0
    if after and isinstance(after[-1], float):
        *after, share = after
    in_specs = [SMEM, *in_specs] + [ANY] * len(after)
    args = [ids, *args, *after]
    inner = kernel
    spot = len(args) - len(after)

    def kernel(*refs):
        inner(*refs[:spot], *refs[len(args) :])

    return pl.pallas_call(
        kernel,
        in_specs=in_specs,
        out_specs=out_specs or [VMEM] * len(out_shape),
        out_shape=out_shape,
        scratch_shapes=list(scratch),
        compiler_params=pltpu.CompilerParams(vmem_limit_bytes=mb * MB),
        cost_estimate=pl.CostEstimate(
            flops=int(share * 1e9), bytes_accessed=int(share * MB), transcendentals=0
        ),
        name=name,
    )(*args)


def run(copies):
    for c in copies:
        c.start()
    for c in copies:
        c.wait()


def pick_columns(ids, partial, chunk, after=()):
    rows, width = partial.shape
    start, n = chunk
    block = width // 8

    def kernel(ids, src, to_a, to_b, own, sem):
        o = ids[1]
        run(
            [
                pltpu.make_async_copy(
                    src.at[
                        :, pl.ds(pl.multiple_of((half + there) * block + start, 128), n)
                    ],
                    out.at[slot],
                    sem.at[t],
                )
                for t, (out, slot, half, there) in enumerate(
                    (
                        (to_a, 0, 0, o ^ 1),
                        (to_a, 1, 0, o ^ 2),
                        (to_b, 0, OUTER, o ^ 3),
                        (to_b, 1, OUTER, o ^ 2),
                        (own, 0, 0, o),
                        (own, 1, 0, o ^ 3),
                        (own, 2, OUTER, o),
                        (own, 3, OUTER, o ^ 1),
                    )
                )
            ]
        )

    return call(
        "pick_columns",
        kernel,
        ids,
        (partial,),
        [HBM],
        [sds(2, rows, n), sds(2, rows, n), sds(4, rows, n)],
        [COPY((8,))],
        after,
    )


def first_add(ids, own, from_a, from_b, after=()):
    _, rows, n = own.shape

    def kernel(ids, own, ra, rb, to_a, to_b, keep):
        to_b[...] = (own[1].astype(F32) + ra[1].astype(F32)).astype(BF)
        to_a[...] = (own[3].astype(F32) + rb[1].astype(F32)).astype(BF)
        keep[0] = own[0].astype(F32) + ra[0].astype(F32)
        keep[1] = own[2].astype(F32) + rb[0].astype(F32)

    return call(
        "first_add",
        kernel,
        ids,
        (own, from_a, from_b),
        [VMEM] * 3,
        [sds(rows, n), sds(rows, n), sds(2, rows, n, dtype=F32)],
        after=after,
    )


def second_add(ids, keep, from_a, from_b, residual, chunk, after=()):
    _, rows, n = keep.shape
    start = chunk[0]

    def kernel(ids, keep, ra, rb, res, out, send):
        extra = res[:, start : start + n].astype(F32)
        zero = jnp.zeros_like(extra)
        left = keep[0] + rb[...].astype(F32) + jnp.where(ids[0] == 0, extra, zero)
        right = keep[1] + ra[...].astype(F32) + jnp.where(ids[0] == 1, extra, zero)
        out[0] = left
        out[1] = right
        send[0] = left.astype(BF)
        send[1] = right.astype(BF)

    return call(
        "second_add",
        kernel,
        ids,
        (keep, from_a, from_b, residual),
        [VMEM] * 4,
        [sds(2, rows, n, dtype=F32), sds(2, rows, n)],
        after=after,
    )


def update(ids, local, arrived, gain, chunk, after=()):
    _, rows, n = local.shape
    start = chunk[0]
    block = gain.shape[0] // 8

    def kernel(ids, local, arrived, gain, stream, scaled, squares):
        mine = ids[0] == 0
        part = jnp.zeros((rows, 128), F32)
        for u in range(n // 128):
            at = slice(u * 128, (u + 1) * 128)
            values = []
            for i in range(2):
                row = (i * OUTER + ids[1]) * block + start // 128 + u
                value = (local[i, :, at] + arrived[i, :, at].astype(F32)).astype(BF)
                wide = value.astype(F32)
                scaled[i, :, at] = (wide * gain[pl.ds(row, 1), :]).astype(BF)
                part = part + wide * wide
                values.append(wide)
            stream[:, at] = jnp.where(mine, values[0], values[1]).astype(BF)
        squares[...] = part

    return call(
        "update",
        kernel,
        ids,
        (local, arrived, gain),
        [VMEM] * 3,
        [sds(rows, n), sds(2, rows, n), sds(rows, 128, dtype=F32)],
        after=after,
    )


def pick_weights(ids, weight, after=()):
    width, pair = weight.shape
    block = width // 8

    def kernel(ids, src, *refs):
        outs, sem = refs[:3], refs[3]
        q = ids[2] * 2 + ids[3]
        copies = []
        for k in range(3):
            there = lax.rem(ids[1] + k + 1, OUTER)
            for i in range(2):
                at = pl.multiple_of((i * OUTER + there) * block + q * UNIT, UNIT)
                copies.append(
                    pltpu.make_async_copy(
                        src.at[pl.ds(at, UNIT), :], outs[k].at[i], sem.at[2 * k + i]
                    )
                )
        run(copies)

    return call(
        "pick_weights",
        kernel,
        ids,
        (weight,),
        [HBM],
        [sds(2, UNIT, pair)] * 3,
        [COPY((6,))],
        after,
    )


def stack(ids, pieces, after=()):
    shape = pieces[0].shape

    def kernel(ids, a, b, c, out, sem):
        run(
            [
                pltpu.make_async_copy(src, out.at[k], sem.at[k])
                for k, src in enumerate((a, b, c))
            ]
        )

    return call(
        "stack",
        kernel,
        ids,
        pieces,
        [VMEM] * 3,
        [sds(3, *shape)],
        [COPY((3,))],
        after,
    )[0]


def project(ids, streams, scaled, squares, pieces, weight):
    rows = scaled[0].shape[1]
    width, pair = weight.shape
    block = width // 8
    n_chunk = len(scaled)
    shifts = (0, 1, 2, 3, 0, 1, 3)

    def kernel(ids, *refs):
        refs = list(refs)

        def take(count):
            taken = refs[:count]
            del refs[:count]
            return taken

        ys, xs, sq = take(n_chunk), take(n_chunk), take(n_chunk)
        pieces = take(7)
        (mine,) = take(1)
        some, own, total, stream = take(4)
        x_buf, mine_buf, y_sem, x_sem, mine_sem = refs
        copies = [
            pltpu.make_async_copy(
                mine.at[
                    pl.ds(pl.multiple_of((i * OUTER + ids[1]) * block, block), block), :
                ],
                mine_buf.at[i],
                mine_sem.at[i],
            )
            for i in range(2)
        ]
        moves = [
            pltpu.make_async_copy(x, x_buf.at[:, :, pl.ds(start, n)], x_sem.at[t])
            for t, (x, (start, n)) in enumerate(zip(xs, CHUNKS))
        ]
        leave = [
            pltpu.make_async_copy(y, stream.at[:, pl.ds(start, n)], y_sem.at[t])
            for t, (y, (start, n)) in enumerate(zip(ys, CHUNKS))
        ]
        for c in moves + copies + leave:
            c.start()
        lanes = sq[0][...]
        for more in sq[1:]:
            lanes = lanes + more[...]
        whole_sum = jnp.sum(lanes, axis=1, keepdims=True)
        total[...] = jnp.broadcast_to(whole_sum, total.shape)
        for c in moves:
            c.wait()
        acc = [jnp.zeros((rows, pair), F32) for _ in range(3)]
        for t, piece in enumerate(pieces):
            core = ids[3] if t < 4 else 1 - ids[3]
            source = lax.rem(ids[2] + 4 - shifts[t], 4)
            at = pl.multiple_of((2 * source + core) * UNIT, UNIT)
            for i in range(2):
                value = x_buf[i, :, pl.ds(at, UNIT)]
                for k in range(3):
                    acc[k] += jnp.dot(value, piece[k, i], preferred_element_type=F32)
        for k in range(3):
            some[k] = acc[k]
        for c in copies:
            c.wait()
        own[...] = jnp.dot(
            x_buf[0], mine_buf[0], preferred_element_type=F32
        ) + jnp.dot(x_buf[1], mine_buf[1], preferred_element_type=F32)
        for c in leave:
            c.wait()

    return call(
        "project",
        kernel,
        ids,
        (*streams, *scaled, *squares, *pieces, weight),
        [VMEM] * (3 * n_chunk + 7) + [HBM],
        [
            sds(3, rows, pair, dtype=F32),
            sds(rows, pair, dtype=F32),
            sds(rows, 128, dtype=F32),
            jax.ShapeDtypeStruct((rows, block), BF),
        ],
        [
            pltpu.VMEM((2, rows, block), BF),
            pltpu.VMEM((2, block, pair), BF),
            COPY((n_chunk,)),
            COPY((n_chunk,)),
            COPY((2,)),
        ],
        mb=8,
        out_specs=[VMEM] * 3 + [ANY],
    )


def complete(ids, some, total, scaled, piece):
    _, rows, pair = some.shape
    n_chunk = len(scaled)
    block = sum(n for _, n in CHUNKS)

    def kernel(ids, some, total, *refs):
        xs = refs[:n_chunk]
        piece, *messages, x_buf, x_sem = refs[n_chunk:]
        moves = [
            pltpu.make_async_copy(x, x_buf.at[:, :, pl.ds(start, n)], x_sem.at[t])
            for t, (x, (start, n)) in enumerate(zip(xs, CHUNKS))
        ]
        for c in moves:
            c.start()
        whole_sum = total[:, :1]
        high = whole_sum.astype(BF)
        low = (whole_sum - high.astype(F32)).astype(BF)
        lane = lax.broadcasted_iota(jnp.int32, (rows, 128), 1)
        tail = jnp.where(lane < 64, high.astype(F32), low.astype(F32)).astype(BF)
        for m in messages:
            m[:, pair:] = tail
        for c in moves:
            c.wait()
        source = lax.rem(ids[2] + 2, 4)
        at = pl.multiple_of((2 * source + 1 - ids[3]) * UNIT, UNIT)
        left, right = x_buf[0, :, pl.ds(at, UNIT)], x_buf[1, :, pl.ds(at, UNIT)]
        for k, m in enumerate(messages):
            value = (
                some[k]
                + jnp.dot(left, piece[k, 0], preferred_element_type=F32)
                + jnp.dot(right, piece[k, 1], preferred_element_type=F32)
            )
            m[:, :pair] = value.astype(BF)

    return call(
        "complete",
        kernel,
        ids,
        (some, total, *scaled, piece),
        [VMEM] * (3 + n_chunk),
        [sds(rows, pair + 128)] * 3,
        [pltpu.VMEM((2, rows, block), BF), COPY((n_chunk,))],
    )


def finish(ids, own, total, arrived, width):
    rows, pair = own.shape

    def kernel(ids, own, total, a, b, c, out):
        value = own[...]
        squares = total[:, :1]
        for m in (a, b, c):
            value = value + m[:, :pair].astype(F32)
            tail = m[:, pair:].astype(F32)
            squares = squares + tail[:, :1] + tail[:, 64:65]
        factor = lax.rsqrt(squares * (1.0 / width) + 1e-05)
        out[...] = (value * factor).astype(BF)

    return call(
        "finish",
        kernel,
        ids,
        (own, total, *arrived),
        [VMEM] * 5,
        [jax.ShapeDtypeStruct((rows, pair), BF)],
    )[0]


def gate(ids, value, *after):
    def kernel(*refs):
        pass

    return pl.pallas_call(
        kernel,
        in_specs=[SMEM, ANY] + [ANY] * len(after),
        out_specs=ANY,
        out_shape=jax.ShapeDtypeStruct(value.shape, value.dtype),
        input_output_aliases={1: 0},
        compiler_params=pltpu.CompilerParams(vmem_limit_bytes=4 * MB),
        cost_estimate=pl.CostEstimate(flops=0, bytes_accessed=0, transcendentals=0),
    )(ids, value, *after)


def body(partials, residual, norm_gain, kv_weight):
    partial = partials[0]
    rows, width = partial.shape
    pair = kv_weight.shape[2]
    weight = kv_weight.reshape(width, pair)
    partial, weight = pin(partial, weight)
    ids = jnp.stack(
        [lax.axis_index(a).astype(jnp.int32) for a in ("inner", "outer", "x", "core")]
    )
    gain = norm_gain.reshape(width // 128, 128)

    def send(label, value, axis, pairs):
        with jax.named_scope(label):
            return lax.ppermute(value, axis, pairs)

    def cross(label, pair):
        return (
            send(label + "_a", pair[0], "outer", PAIR_A),
            send(label + "_b", pair[1], "outer", PAIR_B),
        )

    c0, c1, c2 = CHUNKS
    *p0, own0 = pick_columns(ids, partial, c0)
    r0 = cross("first0", p0)
    sent = pick_weights(ids, weight, [own0])
    got = [send(f"weights{k}", s, "outer", shift(k)) for k, s in zip((1, 2, 3), sent)]
    *f0, keep0 = first_add(ids, own0, *r0, [sent[0]])
    r0 = cross("second0", f0)
    local0, z0 = second_add(ids, keep0, *r0, residual, c0)
    z0 = send("inner0", z0, "inner", SWAP)
    *p1, own1 = pick_columns(ids, partial, c1, [local0])
    r1 = cross("first1", p1)
    near0 = stack(ids, got, [own1, COSTS[3]])
    near1 = send("along_x1", near0, "x", shift(1))
    near3 = send("along_x3", near0, "x", shift(3))
    *f1, keep1 = first_add(ids, own1, *r1, [near0])
    r1 = cross("second1", f1)
    stream0, scaled0, squares0 = update(ids, local0, z0, gain, c0, [keep1, COSTS[0]])
    local1, z1 = second_add(ids, keep1, *r1, residual, c1, [stream0])
    z1 = send("inner1", z1, "inner", SWAP)
    *p2, own2 = pick_columns(ids, partial, c2, [local1])
    r2 = cross("first2", p2)
    near0 = gate(ids, near0, near1, near3)
    near2 = send("along_x2", near0, "x", shift(2))
    *f2, keep2 = first_add(ids, own2, *r2, [own2])
    r2 = cross("second2", f2)
    local2, z2 = second_add(ids, keep2, *r2, residual, c2)
    z2 = send("inner2", z2, "inner", SWAP)
    far0 = send("core0", near0, "core", SWAP)
    far1 = send("core1", near1, "core", SWAP)
    far3 = send("core3", near3, "core", SWAP)
    stream1, scaled1, squares1 = update(ids, local1, z1, gain, c1, [local2, COSTS[1]])
    stream2, scaled2, squares2 = update(ids, local2, z2, gain, c2, [stream1, COSTS[2]])
    far2 = send("core2", near2, "core", SWAP)
    some, own, total, stream = project(
        ids,
        [stream0, stream1, stream2],
        [scaled0, scaled1, scaled2],
        [squares0, squares1, squares2],
        [near0, near1, near2, near3, far0, far1, far3],
        weight,
    )
    messages = complete(ids, some, total, [scaled0, scaled1, scaled2], far2)
    arrived = [
        send(f"products{k}", m, "outer", shift(-k)) for k, m in zip((1, 2, 3), messages)
    ]
    kv = finish(ids, own, total, arrived, width)
    return stream, kv.reshape(rows, 1, pair)


def solution(mesh):
    fine = Mesh(
        mesh.devices.reshape(4, 4, 2, 2, 4), ("x", "z_lo", "core", "inner", "outer")
    )
    dp = ("x", "z_lo", "core")
    placed = (
        P((*dp, "inner", "outer"), None, None),
        P(dp, ("inner", "outer")),
        P(),
        P(None, ("inner", "outer"), None),
    )
    return jax.shard_map(
        body,
        mesh=fine,
        in_specs=placed,
        out_specs=(P(dp, ("inner", "outer")), P(dp, ("inner", "outer"), None)),
        check_vma=False,
    )
```

time: 289 us -> 112 us (0.39)
  waiting for transfers between devices: 237 us -> 39.5 us
  starting transfers between devices: 0.11 us -> 49.9 us
  blocking collectives: 28.9 us -> 0 us
  Pallas kernels: 0 us -> 20.9 us
  between operations: 13.8 us -> 0.85 us
  matrix products: 6.52 us -> 0 us
    reduce_scatter x2 -> x0, waiting for transfers between devices: 139 us -> none  [the longest x1 108 us: body(): lax.psum_scatter(own_part.astype(jnp.bfloat16), 'inner', scatter_dimensio...]
    all_gather x1 -> x0, waiting for transfers between devices: 97.4 us -> none  [body(): lax.all_gather(normed, ('inner', 'outer'), axis=1, tiled=True)]
    ppermute x0 -> x28, starting transfers between devices: none -> 49.9 us  [send(): return lax.ppermute(value, axis, pairs)]
    ppermute x0 -> x28, waiting for transfers between devices: none -> 39.5 us  [send(): return lax.ppermute(value, axis, pairs)]
    psum x1 -> x0, blocking collectives: 28.9 us -> none  [body(): squares = lax.psum(jnp.sum(values * values, axis=1), ('inner', 'outer'))]
    pallas_call x0 -> x18, Pallas kernels: none -> 20.9 us  [the longest x17 20.3 us: call(): pl.pallas_call(kernel, in_specs=in_specs, out_specs=out_specs or [VMEM] *...]
    dot_general x1 -> x0, matrix products: 6.52 us -> none  [body(): jnp.dot(lax.all_gather(normed, ('inner', 'outer'), axis=1, tiled=True), f...]
  transfers between devices with their start and end apart: 3 -> 28, of which waited for: 3 -> 12; matrix products, arithmetic and copies ran while one was open for 0% -> 0% of each run, Pallas kernels for 0% -> 15%
where the time goes in v2:
time: 112 us; the launch traced here: 111 us
  starting transfers between devices  49.9 us (45%)
  waiting for transfers between devices  39.5 us (35%)
  Pallas kernels  20.9 us (19%)
    ppermute x28, starting transfers between devices, send(): return lax.ppermute(value, axis, pairs)  49.9 us
    ppermute x28, waiting for transfers between devices, send(): return lax.ppermute(value, axis, pairs)  39.5 us
    pallas_call x17, Pallas kernels, call(): pl.pallas_call(kernel, in_specs=in_specs, out_specs=out_specs or [VMEM] *...  20.3 us
  transfers between devices with their start and end apart: 28, of which 12 were waited for; matrix products, arithmetic and copies ran while one was open for 0% of the time, Pallas kernels for 15%

profile of v2, /device:TPU:32, one launch (start us, length us, event | category | flops | bytes accessed | tf_op | source)
XLA Modules:
  0.0 111.2 jit_solution(7774634513054981653)
XLA Ops:
  0.7 1.9 %pick_columns.3 = (bf16[2,120,512]{2,1,0:T(8,128)(2,1)S(1)}, bf16[2,120,512]{2,1,0:T(8,128)(2,1)S(1)}, bf16[4,120,512]{2,1,0:T(8,128)(2,1)S(1)}) custom-call(s32[4]{0:T(128)S(1)} %pad_add_fusion.refs_0_, bf16[120,16384]{1,0:T(8,128)(2,1)} %bitcast.11), custom_call_target="tpu_custom_call" | custom-call | tf_op jit(solution)/shard_map/pick_columns/pallas_call | solution.py:52
  2.6 1.7 %collective-permute-start = (bf16[2,120,512]{2,1,0:T(8,128)(2,1)S(1)}, bf16[2,120,512]{2,1,0:T(8,128)(2,1)S(1)}, u32[]{:S(2)}, u32[]{:S(2)}) collective-permute-start(bf16[2,120,512]{2,1,0:T(8,128)(2,1)S(1)} %get-tuple-element.46), channel_id=1, source_target_pairs={{0,1},{1,0},{2,3},{3,2},{4,5},{5,4},{6,7},{7,6},{8,9},{9,8},{10,11... | collective-permute-start | bytes 737288 | tf_op jit(solution)/shard_map/first0_a/ppermute | solution.py:433
  4.3 2.2 %collective-permute-start.1 = (bf16[2,120,512]{2,1,0:T(8,128)(2,1)S(1)}, bf16[2,120,512]{2,1,0:T(8,128)(2,1)S(1)}, u32[]{:S(2)}, u32[]{:S(2)}) collective-permute-start(bf16[2,120,512]{2,1,0:T(8,128)(2,1)S(1)} %get-tuple-element.47), channel_id=1, source_target_pairs={{0,3},{1,2},{2,1},{3,0},{4,7},{5,6},{6,5},{7,4},{8,11},{9,10},{10,... | collective-permute-start | bytes 737288 | tf_op jit(solution)/shard_map/first0_b/ppermute | solution.py:433
  6.5 1.8 %pick_weights.1 = (bf16[2,256,256]{2,1,0:T(8,128)(2,1)S(1)}, bf16[2,256,256]{2,1,0:T(8,128)(2,1)S(1)}, bf16[2,256,256]{2,1,0:T(8,128)(2,1)S(1)}) custom-call(s32[4]{0:T(128)S(1)} %pad_add_fusion.refs_0_, bf16[16384,256]{1,0:T(8,128)(2,1)} %bitcast.14, bf16[4,120,512]{2,1,0:T(8,128)(2,1)S(1)} %get-tuple-element.45.refs_2_.refs_1_), custom_call_target="tpu_custom_call" | custom-call | tf_op jit(solution)/shard_map/pick_weights/pallas_call | solution.py:52
  9.0 1.8 %collective-permute-start.8 = (bf16[2,256,256]{2,1,0:T(8,128)(2,1)S(1)}, bf16[2,256,256]{2,1,0:T(8,128)(2,1)S(1)}, u32[]{:S(2)}, u32[]{:S(2)}) collective-permute-start(bf16[2,256,256]{2,1,0:T(8,128)(2,1)S(1)} %get-tuple-element.57), channel_id=1, source_target_pairs={{0,2},{1,3},{2,0},{3,1},{4,6},{5,7},{6,4},{7,5},{8,10},{9,11},{10,... | collective-permute-start | bytes 786440 | tf_op jit(solution)/shard_map/weights2/ppermute | solution.py:433
  11.8 3.9 %collective-permute-done.1.refs_3_ = bf16[2,120,512]{2,1,0:T(8,128)(2,1)S(1)} collective-permute-done((bf16[2,120,512]{2,1,0:T(8,128)(2,1)S(1)}, bf16[2,120,512]{2,1,0:T(8,128)(2,1)S(1)}, u32[]{:S(2)}, u32[]{:S(2)}) %collective-permute-start.1) | collective-permute-done | bytes 245792 | tf_op jit(solution)/shard_map/first0_b/ppermute | solution.py:433
  16.5 4.3 %collective-permute-start.3 = (bf16[120,512]{1,0:T(8,128)(2,1)S(1)}, bf16[120,512]{1,0:T(8,128)(2,1)S(1)}, u32[]{:S(2)}, u32[]{:S(2)}) collective-permute-start(bf16[120,512]{1,0:T(8,128)(2,1)S(1)} %get-tuple-element.51), channel_id=1, source_target_pairs={{0,3},{1,2},{2,1},{3,0},{4,7},{5,6},{6,5},{7,4},{8,11},{9,10},{10,... | collective-permute-start | bytes 368648 | tf_op jit(solution)/shard_map/second0_b/ppermute | solution.py:433
  20.8 5.2 %collective-permute-done.2.refs_2_ = bf16[120,512]{1,0:T(8,128)(2,1)S(1)} collective-permute-done((bf16[120,512]{1,0:T(8,128)(2,1)S(1)}, bf16[120,512]{1,0:T(8,128)(2,1)S(1)}, u32[]{:S(2)}, u32[]{:S(2)}) %collective-permute-start.2) | collective-permute-done | bytes 122912 | tf_op jit(solution)/shard_map/second0_a/ppermute | solution.py:433
  27.4 2.1 %pick_columns.4 = (bf16[2,120,896]{2,1,0:T(8,128)(2,1)S(1)}, bf16[2,120,896]{2,1,0:T(8,128)(2,1)S(1)}, bf16[4,120,896]{2,1,0:T(8,128)(2,1)S(1)}) custom-call(s32[4]{0:T(128)S(1)} %pad_add_fusion.refs_0_, bf16[120,16384]{1,0:T(8,128)(2,1)} %bitcast.12, f32[2,120,512]{2,1,0:T(8,128)S(1)} %get-tuple-element.52.refs_2_.refs_1_), custom_call_target="tpu_custom_call" | custom-call | tf_op jit(solution)/shard_map/pick_columns/pallas_call | solution.py:52
  29.8 2.2 %collective-permute-start.6 = (bf16[2,120,896]{2,1,0:T(8,128)(2,1)S(1)}, bf16[2,120,896]{2,1,0:T(8,128)(2,1)S(1)}, u32[]{:S(2)}, u32[]{:S(2)}) collective-permute-start(bf16[2,120,896]{2,1,0:T(8,128)(2,1)S(1)} %get-tuple-element.56), channel_id=1, source_target_pairs={{0,3},{1,2},{2,1},{3,0},{4,7},{5,6},{6,5},{7,4},{8,11},{9,10},{10,... | collective-permute-start | bytes 1290248 | tf_op jit(solution)/shard_map/first1_b/ppermute | solution.py:433
  32.0 6.3 %collective-permute-start.4 = (bf16[2,120,512]{2,1,0:T(8,128)(2,1)S(1)}, bf16[2,120,512]{2,1,0:T(8,128)(2,1)S(1)}, u32[]{:S(2)}, u32[]{:S(2)}) collective-permute-start(bf16[2,120,512]{2,1,0:T(8,128)(2,1)S(1)} %get-tuple-element.53), channel_id=1, source_target_pairs={{0,4},{4,0},{1,5},{5,1},{2,6},{6,2},{3,7},{7,3},{8,12},{12,8},{9,1... | collective-permute-start | bytes 737288 | tf_op jit(solution)/shard_map/inner0/ppermute | solution.py:433
  40.5 1.7 %collective-permute-start.19 = (bf16[3,2,256,256]{3,2,1,0:T(8,128)(2,1)S(1)}, bf16[3,2,256,256]{3,2,1,0:T(8,128)(2,1)S(1)}, u32[]{:S(2)}, u32[]{:S(2)}) collective-permute-start(bf16[3,2,256,256]{3,2,1,0:T(8,128)(2,1)S(1)} %stack.21.refs_4_.refs_1_), channel_id=1, source_target_pairs={{0,192},{64,0},{128,64},{192,128},{1,193},{65,1},{129,65},{193,129... | collective-permute-start | bytes 2359304 | tf_op jit(solution)/shard_map/along_x3/ppermute | solution.py:433
  45.9 3.2 %collective-permute-done.4.refs_2_ = bf16[2,120,512]{2,1,0:T(8,128)(2,1)S(1)} collective-permute-done((bf16[2,120,512]{2,1,0:T(8,128)(2,1)S(1)}, bf16[2,120,512]{2,1,0:T(8,128)(2,1)S(1)}, u32[]{:S(2)}, u32[]{:S(2)}) %collective-permute-start.4) | collective-permute-done | bytes 245792 | tf_op jit(solution)/shard_map/inner0/ppermute | solution.py:433
  49.8 1.6 %collective-permute-done.11.refs_3_ = bf16[120,896]{1,0:T(8,128)(2,1)S(1)} collective-permute-done((bf16[120,896]{1,0:T(8,128)(2,1)S(1)}, bf16[120,896]{1,0:T(8,128)(2,1)S(1)}, u32[]{:S(2)}, u32[]{:S(2)}) %collective-permute-start.11) | collective-permute-done | bytes 215072 | tf_op jit(solution)/shard_map/second1_b/ppermute | solution.py:433
  52.2 2.0 %pick_columns.5 = (bf16[2,120,640]{2,1,0:T(8,128)(2,1)S(1)}, bf16[2,120,640]{2,1,0:T(8,128)(2,1)S(1)}, bf16[4,120,640]{2,1,0:T(8,128)(2,1)S(1)}) custom-call(s32[4]{0:T(128)S(1)} %pad_add_fusion.refs_0_, bf16[120,16384]{1,0:T(8,128)(2,1)} %bitcast.13, f32[2,120,896]{2,1,0:T(8,128)S(1)} %get-tuple-element.63.refs_2_.refs_1_), custom_call_target="tpu_custom_call" | custom-call | tf_op jit(solution)/shard_map/pick_columns/pallas_call | solution.py:52
  54.3 1.9 %collective-permute-start.14 = (bf16[2,120,640]{2,1,0:T(8,128)(2,1)S(1)}, bf16[2,120,640]{2,1,0:T(8,128)(2,1)S(1)}, u32[]{:S(2)}, u32[]{:S(2)}) collective-permute-start(bf16[2,120,640]{2,1,0:T(8,128)(2,1)S(1)} %get-tuple-element.67), channel_id=1, source_target_pairs={{0,3},{1,2},{2,1},{3,0},{4,7},{5,6},{6,5},{7,4},{8,11},{9,10},{10,... | collective-permute-start | bytes 921608 | tf_op jit(solution)/shard_map/first2_b/ppermute | solution.py:433
  56.2 6.3 %collective-permute-start.12 = (bf16[2,120,896]{2,1,0:T(8,128)(2,1)S(1)}, bf16[2,120,896]{2,1,0:T(8,128)(2,1)S(1)}, u32[]{:S(2)}, u32[]{:S(2)}) collective-permute-start(bf16[2,120,896]{2,1,0:T(8,128)(2,1)S(1)} %get-tuple-element.64), channel_id=1, source_target_pairs={{0,4},{4,0},{1,5},{5,1},{2,6},{6,2},{3,7},{7,3},{8,12},{12,8},{9,1... | collective-permute-start | bytes 1290248 | tf_op jit(solution)/shard_map/inner1/ppermute | solution.py:433
  66.0 3.1 %collective-permute-start.20 = (bf16[3,2,256,256]{3,2,1,0:T(8,128)(2,1)S(1)}, bf16[3,2,256,256]{3,2,1,0:T(8,128)(2,1)S(1)}, u32[]{:S(2)}, u32[]{:S(2)}) collective-permute-start(bf16[3,2,256,256]{3,2,1,0:T(8,128)(2,1)S(1)} %shard_map.59.refs_10_), channel_id=1, source_target_pairs={{0,128},{64,192},{128,0},{192,64},{1,129},{65,193},{129,1},{193,65... | collective-permute-start | bytes 2359304 | tf_op jit(solution)/shard_map/along_x2/ppermute | solution.py:433
  71.4 7.5 %collective-permute-done.12.refs_2_ = bf16[2,120,896]{2,1,0:T(8,128)(2,1)S(1)} collective-permute-done((bf16[2,120,896]{2,1,0:T(8,128)(2,1)S(1)}, bf16[2,120,896]{2,1,0:T(8,128)(2,1)S(1)}, u32[]{:S(2)}, u32[]{:S(2)}) %collective-permute-start.12) | collective-permute-done | bytes 430112 | tf_op jit(solution)/shard_map/inner1/ppermute | solution.py:433
  79.0 5.6 %collective-permute-start.17 = (bf16[2,120,640]{2,1,0:T(8,128)(2,1)S(1)}, bf16[2,120,640]{2,1,0:T(8,128)(2,1)S(1)}, u32[]{:S(2)}, u32[]{:S(2)}) collective-permute-start(bf16[2,120,640]{2,1,0:T(8,128)(2,1)S(1)} %get-tuple-element.73), channel_id=1, source_target_pairs={{0,4},{4,0},{1,5},{5,1},{2,6},{6,2},{3,7},{7,3},{8,12},{12,8},{9,1... | collective-permute-start | bytes 921608 | tf_op jit(solution)/shard_map/inner2/ppermute | solution.py:433
  85.5 10.5 %collective-permute-done.17.refs_2_ = bf16[2,120,640]{2,1,0:T(8,128)(2,1)S(1)} collective-permute-done((bf16[2,120,640]{2,1,0:T(8,128)(2,1)S(1)}, bf16[2,120,640]{2,1,0:T(8,128)(2,1)S(1)}, u32[]{:S(2)}, u32[]{:S(2)}) %collective-permute-start.17) | collective-permute-done | bytes 307232 | tf_op jit(solution)/shard_map/inner2/ppermute | solution.py:433
  96.7 3.2 %project.1 = (f32[3,120,256]{2,1,0:T(8,128)S(1)}, f32[120,256]{1,0:T(8,128)S(1)}, f32[120,128]{1,0:T(8,128)S(1)}, bf16[120,2048]{1,0:T(8,128)(2,1)}) custom-call(s32[4]{0:T(128)S(1)} %pad_add_fusion.refs_0_, bf16[120,512]{1,0:T(8,128)(2,1)S(1)} %get-tuple-element.60.refs_5_.refs_1_, bf16[120,896]{1,0:T(8,128)(2,1)S(1)} %get-tuple-element.72.refs_4_.refs_2_, ...), custom_call_target="tpu_custom_call" | custom-call | tf_op jit(solution)/shard_map/project/pallas_call | solution.py:52
  101.0 1.7 %collective-permute-start.25 = (bf16[120,384]{1,0:T(8,128)(2,1)S(1)}, bf16[120,384]{1,0:T(8,128)(2,1)S(1)}, u32[]{:S(2)}, u32[]{:S(2)}) collective-permute-start(bf16[120,384]{1,0:T(8,128)(2,1)S(1)} %get-tuple-element.85), channel_id=1, source_target_pairs={{0,3},{1,0},{2,1},{3,2},{4,7},{5,4},{6,5},{7,6},{8,11},{9,8},{10,9... | collective-permute-start | bytes 276488 | tf_op jit(solution)/shard_map/products1/ppermute | solution.py:433
  106.1 2.7 %collective-permute-done.26.refs_4_ = bf16[120,384]{1,0:T(8,128)(2,1)S(1)} collective-permute-done((bf16[120,384]{1,0:T(8,128)(2,1)S(1)}, bf16[120,384]{1,0:T(8,128)(2,1)S(1)}, u32[]{:S(2)}, u32[]{:S(2)}) %collective-permute-start.26) | collective-permute-done | bytes 92192 | tf_op jit(solution)/shard_map/products2/ppermute | solution.py:433
  (55 shorter events, 25.9 us)
Async XLA Ops:
  2.6 9.2 %collective-permute-start = (bf16[2,120,512]{2,1,0:T(8,128)(2,1)S(1)}, bf16[2,120,512]{2,1,0:T(8,128)(2,1)S(1)}, u32[]{:S(2)}, u32[]{:S(2)}) collective-permute-start(bf16[2,120,512]{2,1,0:T(8,128)(2,1)S(1)} %get-tuple-element.46), channel_id=1, source_target_pairs={{0,1},{1,0},{2,3},{3,2},{4,5},{5,4},{6,7},{7,6},{8,9},{9,8},{10,11... | collective-permute-start | bytes 737288 | tf_op jit(solution)/shard_map/first0_a/ppermute | solution.py:433
  4.3 11.4 %collective-permute-start.1 = (bf16[2,120,512]{2,1,0:T(8,128)(2,1)S(1)}, bf16[2,120,512]{2,1,0:T(8,128)(2,1)S(1)}, u32[]{:S(2)}, u32[]{:S(2)}) collective-permute-start(bf16[2,120,512]{2,1,0:T(8,128)(2,1)S(1)} %get-tuple-element.47), channel_id=1, source_target_pairs={{0,3},{1,2},{2,1},{3,0},{4,7},{5,6},{6,5},{7,4},{8,11},{9,10},{10,... | collective-permute-start | bytes 737288 | tf_op jit(solution)/shard_map/first0_b/ppermute | solution.py:433
  8.3 23.7 %collective-permute-start.7 = (bf16[2,256,256]{2,1,0:T(8,128)(2,1)S(1)}, bf16[2,256,256]{2,1,0:T(8,128)(2,1)S(1)}, u32[]{:S(2)}, u32[]{:S(2)}) collective-permute-start(bf16[2,256,256]{2,1,0:T(8,128)(2,1)S(1)} %get-tuple-element.48.refs_4_), channel_id=1, source_target_pairs={{0,1},{1,2},{2,3},{3,0},{4,5},{5,6},{6,7},{7,4},{8,9},{9,10},{10,1... | collective-permute-start | bytes 786440 | tf_op jit(solution)/shard_map/weights1/ppermute | solution.py:433
  9.0 29.2 %collective-permute-start.8 = (bf16[2,256,256]{2,1,0:T(8,128)(2,1)S(1)}, bf16[2,256,256]{2,1,0:T(8,128)(2,1)S(1)}, u32[]{:S(2)}, u32[]{:S(2)}) collective-permute-start(bf16[2,256,256]{2,1,0:T(8,128)(2,1)S(1)} %get-tuple-element.57), channel_id=1, source_target_pairs={{0,2},{1,3},{2,0},{3,1},{4,6},{5,7},{6,4},{7,5},{8,10},{9,11},{10,... | collective-permute-start | bytes 786440 | tf_op jit(solution)/shard_map/weights2/ppermute | solution.py:433
  10.9 27.4 %collective-permute-start.9 = (bf16[2,256,256]{2,1,0:T(8,128)(2,1)S(1)}, bf16[2,256,256]{2,1,0:T(8,128)(2,1)S(1)}, u32[]{:S(2)}, u32[]{:S(2)}) collective-permute-start(bf16[2,256,256]{2,1,0:T(8,128)(2,1)S(1)} %get-tuple-element.58), channel_id=1, source_target_pairs={{0,3},{1,0},{2,1},{3,2},{4,7},{5,4},{6,5},{7,6},{8,11},{9,8},{10,9... | collective-permute-start | bytes 786440 | tf_op jit(solution)/shard_map/weights3/ppermute | solution.py:433
  16.4 9.5 %collective-permute-start.2 = (bf16[120,512]{1,0:T(8,128)(2,1)S(1)}, bf16[120,512]{1,0:T(8,128)(2,1)S(1)}, u32[]{:S(2)}, u32[]{:S(2)}) collective-permute-start(bf16[120,512]{1,0:T(8,128)(2,1)S(1)} %get-tuple-element.50), channel_id=1, source_target_pairs={{0,1},{1,0},{2,3},{3,2},{4,5},{5,4},{6,7},{7,6},{8,9},{9,8},{10,11... | collective-permute-start | bytes 368648 | tf_op jit(solution)/shard_map/second0_a/ppermute | solution.py:433
  16.5 10.3 %collective-permute-start.3 = (bf16[120,512]{1,0:T(8,128)(2,1)S(1)}, bf16[120,512]{1,0:T(8,128)(2,1)S(1)}, u32[]{:S(2)}, u32[]{:S(2)}) collective-permute-start(bf16[120,512]{1,0:T(8,128)(2,1)S(1)} %get-tuple-element.51), channel_id=1, source_target_pairs={{0,3},{1,2},{2,1},{3,0},{4,7},{5,6},{6,5},{7,4},{8,11},{9,10},{10,... | collective-permute-start | bytes 368648 | tf_op jit(solution)/shard_map/second0_b/ppermute | solution.py:433
  29.6 12.6 %collective-permute-start.5 = (bf16[2,120,896]{2,1,0:T(8,128)(2,1)S(1)}, bf16[2,120,896]{2,1,0:T(8,128)(2,1)S(1)}, u32[]{:S(2)}, u32[]{:S(2)}) collective-permute-start(bf16[2,120,896]{2,1,0:T(8,128)(2,1)S(1)} %get-tuple-element.55), channel_id=1, source_target_pairs={{0,1},{1,0},{2,3},{3,2},{4,5},{5,4},{6,7},{7,6},{8,9},{9,8},{10,11... | collective-permute-start | bytes 1290248 | tf_op jit(solution)/shard_map/first1_a/ppermute | solution.py:433
  29.8 12.8 %collective-permute-start.6 = (bf16[2,120,896]{2,1,0:T(8,128)(2,1)S(1)}, bf16[2,120,896]{2,1,0:T(8,128)(2,1)S(1)}, u32[]{:S(2)}, u32[]{:S(2)}) collective-permute-start(bf16[2,120,896]{2,1,0:T(8,128)(2,1)S(1)} %get-tuple-element.56), channel_id=1, source_target_pairs={{0,3},{1,2},{2,1},{3,0},{4,7},{5,6},{6,5},{7,4},{8,11},{9,10},{10,... | collective-permute-start | bytes 1290248 | tf_op jit(solution)/shard_map/first1_b/ppermute | solution.py:433
  32.0 17.2 %collective-permute-start.4 = (bf16[2,120,512]{2,1,0:T(8,128)(2,1)S(1)}, bf16[2,120,512]{2,1,0:T(8,128)(2,1)S(1)}, u32[]{:S(2)}, u32[]{:S(2)}) collective-permute-start(bf16[2,120,512]{2,1,0:T(8,128)(2,1)S(1)} %get-tuple-element.53), channel_id=1, source_target_pairs={{0,4},{4,0},{1,5},{5,1},{2,6},{6,2},{3,7},{7,3},{8,12},{12,8},{9,1... | collective-permute-start | bytes 737288 | tf_op jit(solution)/shard_map/inner0/ppermute | solution.py:433
  38.9 26.6 %collective-permute-start.18 = (bf16[3,2,256,256]{3,2,1,0:T(8,128)(2,1)S(1)}, bf16[3,2,256,256]{3,2,1,0:T(8,128)(2,1)S(1)}, u32[]{:S(2)}, u32[]{:S(2)}) collective-permute-start(bf16[3,2,256,256]{3,2,1,0:T(8,128)(2,1)S(1)} %stack.21.refs_4_.refs_1_), channel_id=1, source_target_pairs={{0,64},{64,128},{128,192},{192,0},{1,65},{65,129},{129,193},{193,1... | collective-permute-start | bytes 2359304 | tf_op jit(solution)/shard_map/along_x1/ppermute | solution.py:433
  40.5 25.0 %collective-permute-start.19 = (bf16[3,2,256,256]{3,2,1,0:T(8,128)(2,1)S(1)}, bf16[3,2,256,256]{3,2,1,0:T(8,128)(2,1)S(1)}, u32[]{:S(2)}, u32[]{:S(2)}) collective-permute-start(bf16[3,2,256,256]{3,2,1,0:T(8,128)(2,1)S(1)} %stack.21.refs_4_.refs_1_), channel_id=1, source_target_pairs={{0,192},{64,0},{128,64},{192,128},{1,193},{65,1},{129,65},{193,129... | collective-permute-start | bytes 2359304 | tf_op jit(solution)/shard_map/along_x3/ppermute | solution.py:433
  43.3 6.6 %collective-permute-start.10 = (bf16[120,896]{1,0:T(8,128)(2,1)S(1)}, bf16[120,896]{1,0:T(8,128)(2,1)S(1)}, u32[]{:S(2)}, u32[]{:S(2)}) collective-permute-start(bf16[120,896]{1,0:T(8,128)(2,1)S(1)} %get-tuple-element.61), channel_id=1, source_target_pairs={{0,1},{1,0},{2,3},{3,2},{4,5},{5,4},{6,7},{7,6},{8,9},{9,8},{10,11... | collective-permute-start | bytes 645128 | tf_op jit(solution)/shard_map/second1_a/ppermute | solution.py:433
  44.4 7.1 %collective-permute-start.11 = (bf16[120,896]{1,0:T(8,128)(2,1)S(1)}, bf16[120,896]{1,0:T(8,128)(2,1)S(1)}, u32[]{:S(2)}, u32[]{:S(2)}) collective-permute-start(bf16[120,896]{1,0:T(8,128)(2,1)S(1)} %get-tuple-element.62), channel_id=1, source_target_pairs={{0,3},{1,2},{2,1},{3,0},{4,7},{5,6},{6,5},{7,4},{8,11},{9,10},{10,... | collective-permute-start | bytes 645128 | tf_op jit(solution)/shard_map/second1_b/ppermute | solution.py:433
  54.2 8.3 %collective-permute-start.13 = (bf16[2,120,640]{2,1,0:T(8,128)(2,1)S(1)}, bf16[2,120,640]{2,1,0:T(8,128)(2,1)S(1)}, u32[]{:S(2)}, u32[]{:S(2)}) collective-permute-start(bf16[2,120,640]{2,1,0:T(8,128)(2,1)S(1)} %get-tuple-element.66), channel_id=1, source_target_pairs={{0,1},{1,0},{2,3},{3,2},{4,5},{5,4},{6,7},{7,6},{8,9},{9,8},{10,11... | collective-permute-start | bytes 921608 | tf_op jit(solution)/shard_map/first2_a/ppermute | solution.py:433
  54.3 8.2 %collective-permute-start.14 = (bf16[2,120,640]{2,1,0:T(8,128)(2,1)S(1)}, bf16[2,120,640]{2,1,0:T(8,128)(2,1)S(1)}, u32[]{:S(2)}, u32[]{:S(2)}) collective-permute-start(bf16[2,120,640]{2,1,0:T(8,128)(2,1)S(1)} %get-tuple-element.67), channel_id=1, source_target_pairs={{0,3},{1,2},{2,1},{3,0},{4,7},{5,6},{6,5},{7,4},{8,11},{9,10},{10,... | collective-permute-start | bytes 921608 | tf_op jit(solution)/shard_map/first2_b/ppermute | solution.py:433
  56.2 22.8 %collective-permute-start.12 = (bf16[2,120,896]{2,1,0:T(8,128)(2,1)S(1)}, bf16[2,120,896]{2,1,0:T(8,128)(2,1)S(1)}, u32[]{:S(2)}, u32[]{:S(2)}) collective-permute-start(bf16[2,120,896]{2,1,0:T(8,128)(2,1)S(1)} %get-tuple-element.64), channel_id=1, source_target_pairs={{0,4},{4,0},{1,5},{5,1},{2,6},{6,2},{3,7},{7,3},{8,12},{12,8},{9,1... | collective-permute-start | bytes 1290248 | tf_op jit(solution)/shard_map/inner1/ppermute | solution.py:433
  64.3 6.4 %collective-permute-start.16 = (bf16[120,640]{1,0:T(8,128)(2,1)S(1)}, bf16[120,640]{1,0:T(8,128)(2,1)S(1)}, u32[]{:S(2)}, u32[]{:S(2)}) collective-permute-start(bf16[120,640]{1,0:T(8,128)(2,1)S(1)} %get-tuple-element.70), channel_id=1, source_target_pairs={{0,3},{1,2},{2,1},{3,0},{4,7},{5,6},{6,5},{7,4},{8,11},{9,10},{10,... | collective-permute-start | bytes 460808 | tf_op jit(solution)/shard_map/second2_b/ppermute | solution.py:433
  66.0 19.4 %collective-permute-start.20 = (bf16[3,2,256,256]{3,2,1,0:T(8,128)(2,1)S(1)}, bf16[3,2,256,256]{3,2,1,0:T(8,128)(2,1)S(1)}, u32[]{:S(2)}, u32[]{:S(2)}) collective-permute-start(bf16[3,2,256,256]{3,2,1,0:T(8,128)(2,1)S(1)} %shard_map.59.refs_10_), channel_id=1, source_target_pairs={{0,128},{64,192},{128,0},{192,64},{1,129},{65,193},{129,1},{193,65... | collective-permute-start | bytes 2359304 | tf_op jit(solution)/shard_map/along_x2/ppermute | solution.py:433
  69.1 27.5 %collective-permute-start.21 = (bf16[3,2,256,256]{3,2,1,0:T(8,128)(2,1)S(1)}, bf16[3,2,256,256]{3,2,1,0:T(8,128)(2,1)S(1)}, u32[]{:S(2)}, u32[]{:S(2)}) collective-permute-start(bf16[3,2,256,256]{3,2,1,0:T(8,128)(2,1)S(1)} %shard_map.59.refs_10_), channel_id=1, source_target_pairs={{0,8},{8,0},{1,9},{9,1},{2,10},{10,2},{3,11},{11,3},{4,12},{12,4},... | collective-permute-start | bytes 2359304 | tf_op jit(solution)/shard_map/core0/ppermute | solution.py:433
  69.1 27.5 %collective-permute-start.22 = (bf16[3,2,256,256]{3,2,1,0:T(8,128)(2,1)S(1)}, bf16[3,2,256,256]{3,2,1,0:T(8,128)(2,1)S(1)}, u32[]{:S(2)}, u32[]{:S(2)}) collective-permute-start(bf16[3,2,256,256]{3,2,1,0:T(8,128)(2,1)S(1)} %collective-permute-done.18.refs_2_.refs_11_), channel_id=1, source_target_pairs={{0,8},{8,0},{1,9},{9,1},{2,10},{10,2},{3,11},{11,3},{4,12},{12,4},... | collective-permute-start | bytes 2359304 | tf_op jit(solution)/shard_map/core1/ppermute | solution.py:433
  70.7 26.0 %collective-permute-start.23 = (bf16[3,2,256,256]{3,2,1,0:T(8,128)(2,1)S(1)}, bf16[3,2,256,256]{3,2,1,0:T(8,128)(2,1)S(1)}, u32[]{:S(2)}, u32[]{:S(2)}) collective-permute-start(bf16[3,2,256,256]{3,2,1,0:T(8,128)(2,1)S(1)} %collective-permute-done.19.refs_3_.refs_13_), channel_id=1, source_target_pairs={{0,8},{8,0},{1,9},{9,1},{2,10},{10,2},{3,11},{11,3},{4,12},{12,4},... | collective-permute-start | bytes 2359304 | tf_op jit(solution)/shard_map/core3/ppermute | solution.py:433
  79.0 17.0 %collective-permute-start.17 = (bf16[2,120,640]{2,1,0:T(8,128)(2,1)S(1)}, bf16[2,120,640]{2,1,0:T(8,128)(2,1)S(1)}, u32[]{:S(2)}, u32[]{:S(2)}) collective-permute-start(bf16[2,120,640]{2,1,0:T(8,128)(2,1)S(1)} %get-tuple-element.73), channel_id=1, source_target_pairs={{0,4},{4,0},{1,5},{5,1},{2,6},{6,2},{3,7},{7,3},{8,12},{12,8},{9,1... | collective-permute-start | bytes 921608 | tf_op jit(solution)/shard_map/inner2/ppermute | solution.py:433
  85.4 14.5 %collective-permute-start.24 = (bf16[3,2,256,256]{3,2,1,0:T(8,128)(2,1)S(1)}, bf16[3,2,256,256]{3,2,1,0:T(8,128)(2,1)S(1)}, u32[]{:S(2)}, u32[]{:S(2)}) collective-permute-start(bf16[3,2,256,256]{3,2,1,0:T(8,128)(2,1)S(1)} %collective-permute-done.20.refs_12_), channel_id=1, source_target_pairs={{0,8},{8,0},{1,9},{9,1},{2,10},{10,2},{3,11},{11,3},{4,12},{12,4},... | collective-permute-start | bytes 2359304 | tf_op jit(solution)/shard_map/core2/ppermute | solution.py:433
  (6 other events, 60.0 us)

commit v3 on v2

--- a/solution.py
+++ b/solution.py
@@ -10,7 +10,7 @@
 F32 = jnp.float32
 OUTER = 4
 UNIT = 256
-CHUNKS = ((0, 512), (512, 896), (1408, 640))
+CHUNKS = ((0, 640), (640, 896), (1536, 512))
 ANY = pl.BlockSpec(memory_space=pl.ANY)
 HBM = pl.BlockSpec(memory_space=pltpu.HBM)
 VMEM = pl.BlockSpec(memory_space=pltpu.VMEM)
@@ -19,7 +19,7 @@
 PAIR_B = [(o, o ^ 3) for o in range(4)]
 SWAP = [(0, 1), (1, 0)]
 MB = 1024 * 1024
-COSTS = (12.0, 10.0, 10.0, 12.0)
+COSTS = (0.0, 8.0, 0.0, 0.0, 0.0, 0.0, 0.0, 10.0, 0.0, 5.0, 5.0)
 COPY = pltpu.SemaphoreType.DMA
 
 
@@ -224,13 +224,10 @@
 def stack(ids, pieces, after=()):
     shape = pieces[0].shape
 
-    def kernel(ids, a, b, c, out, sem):
-        run(
-            [
-                pltpu.make_async_copy(src, out.at[k], sem.at[k])
-                for k, src in enumerate((a, b, c))
-            ]
-        )
+    def kernel(ids, a, b, c, out):
+        for k, src in enumerate((a, b, c)):
+            for i in range(2):
+                out[i, k] = src[i]
 
     return call(
         "stack",
@@ -238,10 +235,27 @@
         ids,
         pieces,
         [VMEM] * 3,
-        [sds(3, *shape)],
-        [COPY((3,))],
-        after,
+        [sds(2, 3, *shape[1:])],
+        after=after,
     )[0]
+
+
+def halves(ids, from_left, from_right, after=()):
+    shape = from_left.shape[1:]
+
+    def kernel(ids, a, b, left, right):
+        left[...] = a[0]
+        right[...] = b[1]
+
+    return call(
+        "halves",
+        kernel,
+        ids,
+        (from_left, from_right),
+        [VMEM] * 2,
+        [sds(*shape), sds(*shape)],
+        after=after,
+    )
 
 
 def project(ids, streams, scaled, squares, pieces, weight):
@@ -249,7 +263,8 @@
     width, pair = weight.shape
     block = width // 8
     n_chunk = len(scaled)
-    shifts = (0, 1, 2, 3, 0, 1, 3)
+    plan = [p[1:] for p in pieces]
+    pieces = [p[0] for p in pieces]
 
     def kernel(ids, *refs):
         refs = list(refs)
@@ -260,7 +275,7 @@
             return taken
 
         ys, xs, sq = take(n_chunk), take(n_chunk), take(n_chunk)
-        pieces = take(7)
+        pieces = take(len(plan))
         (mine,) = take(1)
         some, own, total, stream = take(4)
         x_buf, mine_buf, y_sem, x_sem, mine_sem = refs
@@ -292,14 +307,12 @@
         for c in moves:
             c.wait()
         acc = [jnp.zeros((rows, pair), F32) for _ in range(3)]
-        for t, piece in enumerate(pieces):
-            core = ids[3] if t < 4 else 1 - ids[3]
-            source = lax.rem(ids[2] + 4 - shifts[t], 4)
-            at = pl.multiple_of((2 * source + core) * UNIT, UNIT)
-            for i in range(2):
-                value = x_buf[i, :, pl.ds(at, UNIT)]
+        for piece, (first, count, step, crossed) in zip(pieces, plan):
+            for i in range(first, first + count):
+                value = x_buf[i, :, columns_of(ids, step, crossed)]
                 for k in range(3):
-                    acc[k] += jnp.dot(value, piece[k, i], preferred_element_type=F32)
+                    there = piece[k] if count == 1 else piece[i, k]
+                    acc[k] += jnp.dot(value, there, preferred_element_type=F32)
         for k in range(3):
             some[k] = acc[k]
         for c in copies:
@@ -315,7 +328,7 @@
         kernel,
         ids,
         (*streams, *scaled, *squares, *pieces, weight),
-        [VMEM] * (3 * n_chunk + 7) + [HBM],
+        [VMEM] * (3 * n_chunk + len(plan)) + [HBM],
         [
             sds(3, rows, pair, dtype=F32),
             sds(rows, pair, dtype=F32),
@@ -334,20 +347,22 @@
     )
 
 
-def complete(ids, some, total, scaled, piece):
+def columns_of(ids, step, crossed):
+    source = lax.rem(ids[2] + 4 - step, 4)
+    core = 1 - ids[3] if crossed else ids[3]
+    return pl.ds(pl.multiple_of((2 * source + core) * UNIT, UNIT), UNIT)
+
+
+def complete(ids, some, total, scaled, pieces):
     _, rows, pair = some.shape
     n_chunk = len(scaled)
     block = sum(n for _, n in CHUNKS)
 
     def kernel(ids, some, total, *refs):
         xs = refs[:n_chunk]
-        piece, *messages, x_buf, x_sem = refs[n_chunk:]
-        moves = [
-            pltpu.make_async_copy(x, x_buf.at[:, :, pl.ds(start, n)], x_sem.at[t])
-            for t, (x, (start, n)) in enumerate(zip(xs, CHUNKS))
-        ]
-        for c in moves:
-            c.start()
+        a, b, *messages, x_buf = refs[n_chunk:]
+        for x, (start, n) in zip(xs, CHUNKS):
+            x_buf[:, :, start : start + n] = x[...]
         whole_sum = total[:, :1]
         high = whole_sum.astype(BF)
         low = (whole_sum - high.astype(F32)).astype(BF)
@@ -355,16 +370,13 @@
         tail = jnp.where(lane < 64, high.astype(F32), low.astype(F32)).astype(BF)
         for m in messages:
             m[:, pair:] = tail
-        for c in moves:
-            c.wait()
-        source = lax.rem(ids[2] + 2, 4)
-        at = pl.multiple_of((2 * source + 1 - ids[3]) * UNIT, UNIT)
-        left, right = x_buf[0, :, pl.ds(at, UNIT)], x_buf[1, :, pl.ds(at, UNIT)]
+        left = x_buf[0, :, columns_of(ids, 2, True)]
+        right = x_buf[1, :, columns_of(ids, 2, True)]
         for k, m in enumerate(messages):
             value = (
                 some[k]
-                + jnp.dot(left, piece[k, 0], preferred_element_type=F32)
-                + jnp.dot(right, piece[k, 1], preferred_element_type=F32)
+                + jnp.dot(left, a[k], preferred_element_type=F32)
+                + jnp.dot(right, b[k], preferred_element_type=F32)
             )
             m[:, :pair] = value.astype(BF)
 
@@ -372,10 +384,10 @@
         "complete",
         kernel,
         ids,
-        (some, total, *scaled, piece),
-        [VMEM] * (3 + n_chunk),
+        (some, total, *scaled, *pieces),
+        [VMEM] * (4 + n_chunk),
         [sds(rows, pair + 128)] * 3,
-        [pltpu.VMEM((2, rows, block), BF), COPY((n_chunk,))],
+        [pltpu.VMEM((2, rows, block), BF)],
     )
 
 
@@ -402,21 +414,6 @@
     )[0]
 
 
-def gate(ids, value, *after):
-    def kernel(*refs):
-        pass
-
-    return pl.pallas_call(
-        kernel,
-        in_specs=[SMEM, ANY] + [ANY] * len(after),
-        out_specs=ANY,
-        out_shape=jax.ShapeDtypeStruct(value.shape, value.dtype),
-        input_output_aliases={1: 0},
-        compiler_params=pltpu.CompilerParams(vmem_limit_bytes=4 * MB),
-        cost_estimate=pl.CostEstimate(flops=0, bytes_accessed=0, transcendentals=0),
-    )(ids, value, *after)
-
-
 def body(partials, residual, norm_gain, kv_weight):
     partial = partials[0]
     rows, width = partial.shape
@@ -441,45 +438,55 @@
     c0, c1, c2 = CHUNKS
     *p0, own0 = pick_columns(ids, partial, c0)
     r0 = cross("first0", p0)
-    sent = pick_weights(ids, weight, [own0])
+    *p1, own1 = pick_columns(ids, partial, c1, [own0, COSTS[0]])
+    r1 = cross("first1", p1)
+    *f0, keep0 = first_add(ids, own0, *r0, [own1, COSTS[1]])
+    r0 = cross("second0", f0)
+    local0, z0 = second_add(ids, keep0, *r0, residual, c0, [keep0, COSTS[2]])
+    z0 = send("inner0", z0, "inner", SWAP)
+    *f1, keep1 = first_add(ids, own1, *r1, [local0, COSTS[3]])
+    r1 = cross("second1", f1)
+    sent = pick_weights(ids, weight, [keep1])
     got = [send(f"weights{k}", s, "outer", shift(k)) for k, s in zip((1, 2, 3), sent)]
-    *f0, keep0 = first_add(ids, own0, *r0, [sent[0]])
-    r0 = cross("second0", f0)
-    local0, z0 = second_add(ids, keep0, *r0, residual, c0)
-    z0 = send("inner0", z0, "inner", SWAP)
-    *p1, own1 = pick_columns(ids, partial, c1, [local0])
-    r1 = cross("first1", p1)
-    near0 = stack(ids, got, [own1, COSTS[3]])
-    near1 = send("along_x1", near0, "x", shift(1))
-    near3 = send("along_x3", near0, "x", shift(3))
-    *f1, keep1 = first_add(ids, own1, *r1, [near0])
-    r1 = cross("second1", f1)
-    stream0, scaled0, squares0 = update(ids, local0, z0, gain, c0, [keep1, COSTS[0]])
-    local1, z1 = second_add(ids, keep1, *r1, residual, c1, [stream0])
+    local1, z1 = second_add(ids, keep1, *r1, residual, c1, [sent[0], COSTS[4]])
     z1 = send("inner1", z1, "inner", SWAP)
     *p2, own2 = pick_columns(ids, partial, c2, [local1])
     r2 = cross("first2", p2)
-    near0 = gate(ids, near0, near1, near3)
-    near2 = send("along_x2", near0, "x", shift(2))
-    *f2, keep2 = first_add(ids, own2, *r2, [own2])
+    stream0, scaled0, squares0 = update(ids, local0, z0, gain, c0, [own2, COSTS[5]])
+    near0 = stack(ids, got, [stream0, COSTS[6]])
+    near1 = send("along_x1", near0, "x", shift(1))
+    near3 = send("along_x3", near0, "x", shift(3))
+    *f2, keep2 = first_add(ids, own2, *r2, [near0, COSTS[7]])
     r2 = cross("second2", f2)
-    local2, z2 = second_add(ids, keep2, *r2, residual, c2)
+    local2, z2 = second_add(ids, keep2, *r2, residual, c2, [keep2, COSTS[8]])
     z2 = send("inner2", z2, "inner", SWAP)
-    far0 = send("core0", near0, "core", SWAP)
-    far1 = send("core1", near1, "core", SWAP)
-    far3 = send("core3", near3, "core", SWAP)
-    stream1, scaled1, squares1 = update(ids, local1, z1, gain, c1, [local2, COSTS[1]])
-    stream2, scaled2, squares2 = update(ids, local2, z2, gain, c2, [stream1, COSTS[2]])
-    far2 = send("core2", near2, "core", SWAP)
+    left, right = halves(ids, near1, near3)
+    near2a = send("along_x2a", left, "x", shift(1))
+    near2b = send("along_x2b", right, "x", shift(3))
+    stream1, scaled1, squares1 = update(ids, local1, z1, gain, c1, [local2, COSTS[9]])
+    stream2, scaled2, squares2 = update(ids, local2, z2, gain, c2, [stream1, COSTS[10]])
+    far0, far1, far2a, far2b, far3 = [
+        send(f"core{k}", w, "core", SWAP)
+        for k, w in (("0", near0), ("1", near1), ("2a", near2a), ("2b", near2b), ("3", near3))
+    ]
     some, own, total, stream = project(
         ids,
         [stream0, stream1, stream2],
         [scaled0, scaled1, scaled2],
         [squares0, squares1, squares2],
-        [near0, near1, near2, near3, far0, far1, far3],
+        [
+            (near0, 0, 2, 0, False),
+            (near1, 0, 2, 1, False),
+            (near3, 0, 2, 3, False),
+            (near2a, 0, 1, 2, False),
+            (near2b, 1, 1, 2, False),
+            (far0, 0, 2, 0, True),
+            (far1, 0, 2, 1, True),
+            (far3, 0, 2, 3, True),
+        ],
         weight,
     )
-    messages = complete(ids, some, total, [scaled0, scaled1, scaled2], far2)
+    messages = complete(ids, some, total, [scaled0, scaled1, scaled2], [far2a, far2b])
     arrived = [
         send(f"products{k}", m, "outer", shift(-k)) for k, m in zip((1, 2, 3), messages)
     ]

time: 112 us -> 105 us (0.938)
  waiting for transfers between devices: 39.5 us -> 33.3 us
  starting transfers between devices: 49.9 us -> 48.2 us
    ppermute x28 -> x30, waiting for transfers between devices: 39.5 us -> 33.3 us  [send(): return lax.ppermute(value, axis, pairs)]
    ppermute x28 -> x30, starting transfers between devices: 49.9 us -> 48.2 us  [send(): return lax.ppermute(value, axis, pairs)]
    pallas_call x17 -> x18, Pallas kernels: 20.3 us -> 20.7 us  [call(): pl.pallas_call(kernel, in_specs=in_specs, out_specs=out_specs or [VMEM] *...]
  transfers between devices with their start and end apart: 28 -> 30, of which waited for: 12 -> 13; matrix products, arithmetic and copies ran while one was open for 0% -> 0% of each run, Pallas kernels for 15% -> 16%
where the time goes in v3:
time: 105 us; the launch traced here: 103 us
  starting transfers between devices  48.2 us (46%)
  waiting for transfers between devices  33.3 us (32%)
  Pallas kernels  20.7 us (20%)
    ppermute x30, starting transfers between devices, send(): return lax.ppermute(value, axis, pairs)  48.2 us
    ppermute x30, waiting for transfers between devices, send(): return lax.ppermute(value, axis, pairs)  33.3 us
    pallas_call x18, Pallas kernels, call(): pl.pallas_call(kernel, in_specs=in_specs, out_specs=out_specs or [VMEM] *...  20.7 us
  transfers between devices with their start and end apart: 30, of which 13 were waited for; matrix products, arithmetic and copies ran while one was open for 0% of the time, Pallas kernels for 16%

profile of v3, /device:TPU:32, one launch (start us, length us, event | category | flops | bytes accessed | tf_op | source)
XLA Modules:
  0.0 103.2 jit_solution(15236986842734407143)
XLA Ops:
  0.7 2.0 %pick_columns.3 = (bf16[2,120,640]{2,1,0:T(8,128)(2,1)S(1)}, bf16[2,120,640]{2,1,0:T(8,128)(2,1)S(1)}, bf16[4,120,640]{2,1,0:T(8,128)(2,1)S(1)}) custom-call(s32[4]{0:T(128)S(1)} %pad_add_fusion.refs_0_, bf16[120,16384]{1,0:T(8,128)(2,1)} %bitcast.11), custom_call_target="tpu_custom_call" | custom-call | tf_op jit(solution)/shard_map/pick_columns/pallas_call | solution.py:52
  4.4 2.2 %collective-permute-start.1 = (bf16[2,120,640]{2,1,0:T(8,128)(2,1)S(1)}, bf16[2,120,640]{2,1,0:T(8,128)(2,1)S(1)}, u32[]{:S(2)}, u32[]{:S(2)}) collective-permute-start(bf16[2,120,640]{2,1,0:T(8,128)(2,1)S(1)} %get-tuple-element.49), channel_id=1, source_target_pairs={{0,3},{1,2},{2,1},{3,0},{4,7},{5,6},{6,5},{7,4},{8,11},{9,10},{10,... | collective-permute-start | bytes 921608 | tf_op jit(solution)/shard_map/first0_b/ppermute | solution.py:430
  6.5 2.1 %pick_columns.4 = (bf16[2,120,896]{2,1,0:T(8,128)(2,1)S(1)}, bf16[2,120,896]{2,1,0:T(8,128)(2,1)S(1)}, bf16[4,120,896]{2,1,0:T(8,128)(2,1)S(1)}) custom-call(s32[4]{0:T(128)S(1)} %pad_add_fusion.refs_0_, bf16[120,16384]{1,0:T(8,128)(2,1)} %bitcast.12, bf16[4,120,640]{2,1,0:T(8,128)(2,1)S(1)} %get-tuple-element.47.refs_2_.refs_1_), custom_call_target="tpu_custom_call" | custom-call | tf_op jit(solution)/shard_map/pick_columns/pallas_call | solution.py:52
  10.1 2.9 %collective-permute-done.refs_2_ = bf16[2,120,640]{2,1,0:T(8,128)(2,1)S(1)} collective-permute-done((bf16[2,120,640]{2,1,0:T(8,128)(2,1)S(1)}, bf16[2,120,640]{2,1,0:T(8,128)(2,1)S(1)}, u32[]{:S(2)}, u32[]{:S(2)}) %collective-permute-start) | collective-permute-done | bytes 307232 | tf_op jit(solution)/shard_map/first0_a/ppermute | solution.py:430
  12.9 2.8 %collective-permute-done.1.refs_3_ = bf16[2,120,640]{2,1,0:T(8,128)(2,1)S(1)} collective-permute-done((bf16[2,120,640]{2,1,0:T(8,128)(2,1)S(1)}, bf16[2,120,640]{2,1,0:T(8,128)(2,1)S(1)}, u32[]{:S(2)}, u32[]{:S(2)}) %collective-permute-start.1) | collective-permute-done | bytes 307232 | tf_op jit(solution)/shard_map/first0_b/ppermute | solution.py:430
  16.6 2.3 %collective-permute-start.3 = (bf16[120,640]{1,0:T(8,128)(2,1)S(1)}, bf16[120,640]{1,0:T(8,128)(2,1)S(1)}, u32[]{:S(2)}, u32[]{:S(2)}) collective-permute-start(bf16[120,640]{1,0:T(8,128)(2,1)S(1)} %get-tuple-element.53), channel_id=1, source_target_pairs={{0,3},{1,2},{2,1},{3,0},{4,7},{5,6},{6,5},{7,4},{8,11},{9,10},{10,... | collective-permute-start | bytes 460808 | tf_op jit(solution)/shard_map/second0_b/ppermute | solution.py:430
  18.8 5.5 %collective-permute-done.2.refs_2_ = bf16[120,640]{1,0:T(8,128)(2,1)S(1)} collective-permute-done((bf16[120,640]{1,0:T(8,128)(2,1)S(1)}, bf16[120,640]{1,0:T(8,128)(2,1)S(1)}, u32[]{:S(2)}, u32[]{:S(2)}) %collective-permute-start.2) | collective-permute-done | bytes 153632 | tf_op jit(solution)/shard_map/second0_a/ppermute | solution.py:430
  24.3 2.5 %collective-permute-done.3.refs_3_ = bf16[120,640]{1,0:T(8,128)(2,1)S(1)} collective-permute-done((bf16[120,640]{1,0:T(8,128)(2,1)S(1)}, bf16[120,640]{1,0:T(8,128)(2,1)S(1)}, u32[]{:S(2)}, u32[]{:S(2)}) %collective-permute-start.3) | collective-permute-done | bytes 153632 | tf_op jit(solution)/shard_map/second0_b/ppermute | solution.py:430
  27.5 6.4 %collective-permute-start.4 = (bf16[2,120,640]{2,1,0:T(8,128)(2,1)S(1)}, bf16[2,120,640]{2,1,0:T(8,128)(2,1)S(1)}, u32[]{:S(2)}, u32[]{:S(2)}) collective-permute-start(bf16[2,120,640]{2,1,0:T(8,128)(2,1)S(1)} %get-tuple-element.55), channel_id=1, source_target_pairs={{0,4},{4,0},{1,5},{5,1},{2,6},{6,2},{3,7},{7,3},{8,12},{12,8},{9,1... | collective-permute-start | bytes 921608 | tf_op jit(solution)/shard_map/inner0/ppermute | solution.py:430
  34.7 2.3 %collective-permute-start.8 = (bf16[120,896]{1,0:T(8,128)(2,1)S(1)}, bf16[120,896]{1,0:T(8,128)(2,1)S(1)}, u32[]{:S(2)}, u32[]{:S(2)}) collective-permute-start(bf16[120,896]{1,0:T(8,128)(2,1)S(1)} %get-tuple-element.60), channel_id=1, source_target_pairs={{0,3},{1,2},{2,1},{3,0},{4,7},{5,6},{6,5},{7,4},{8,11},{9,10},{10,... | collective-permute-start | bytes 645128 | tf_op jit(solution)/shard_map/second1_b/ppermute | solution.py:430
  37.0 1.8 %pick_weights.1 = (bf16[2,256,256]{2,1,0:T(8,128)(2,1)S(1)}, bf16[2,256,256]{2,1,0:T(8,128)(2,1)S(1)}, bf16[2,256,256]{2,1,0:T(8,128)(2,1)S(1)}) custom-call(s32[4]{0:T(128)S(1)} %pad_add_fusion.refs_0_, bf16[16384,256]{1,0:T(8,128)(2,1)} %bitcast.14, f32[2,120,896]{2,1,0:T(8,128)S(1)} %get-tuple-element.58.refs_2_.refs_1_), custom_call_target="tpu_custom_call" | custom-call | tf_op jit(solution)/shard_map/pick_weights/pallas_call | solution.py:52
  41.4 3.5 %collective-permute-start.14 = (bf16[2,256,256]{2,1,0:T(8,128)(2,1)S(1)}, bf16[2,256,256]{2,1,0:T(8,128)(2,1)S(1)}, u32[]{:S(2)}, u32[]{:S(2)}) collective-permute-start(bf16[2,256,256]{2,1,0:T(8,128)(2,1)S(1)} %get-tuple-element.69), channel_id=1, source_target_pairs={{0,3},{1,0},{2,1},{3,2},{4,7},{5,4},{6,5},{7,6},{8,11},{9,8},{10,9... | collective-permute-start | bytes 786440 | tf_op jit(solution)/shard_map/weights3/ppermute | solution.py:430
  45.7 1.9 %pick_columns.5 = (bf16[2,120,512]{2,1,0:T(8,128)(2,1)S(1)}, bf16[2,120,512]{2,1,0:T(8,128)(2,1)S(1)}, bf16[4,120,512]{2,1,0:T(8,128)(2,1)S(1)}) custom-call(s32[4]{0:T(128)S(1)} %pad_add_fusion.refs_0_, bf16[120,16384]{1,0:T(8,128)(2,1)} %bitcast.13, f32[2,120,896]{2,1,0:T(8,128)S(1)} %get-tuple-element.62.refs_2_.refs_1_), custom_call_target="tpu_custom_call" | custom-call | tf_op jit(solution)/shard_map/pick_columns/pallas_call | solution.py:52
  48.5 3.2 %collective-permute-start.11 = (bf16[2,120,512]{2,1,0:T(8,128)(2,1)S(1)}, bf16[2,120,512]{2,1,0:T(8,128)(2,1)S(1)}, u32[]{:S(2)}, u32[]{:S(2)}) collective-permute-start(bf16[2,120,512]{2,1,0:T(8,128)(2,1)S(1)} %get-tuple-element.67), channel_id=1, source_target_pairs={{0,3},{1,2},{2,1},{3,0},{4,7},{5,6},{6,5},{7,4},{8,11},{9,10},{10,... | collective-permute-start | bytes 737288 | tf_op jit(solution)/shard_map/first2_b/ppermute | solution.py:430
  52.5 2.7 %collective-permute-start.9 = (bf16[2,120,896]{2,1,0:T(8,128)(2,1)S(1)}, bf16[2,120,896]{2,1,0:T(8,128)(2,1)S(1)}, u32[]{:S(2)}, u32[]{:S(2)}) collective-permute-start(bf16[2,120,896]{2,1,0:T(8,128)(2,1)S(1)} %get-tuple-element.65), channel_id=1, source_target_pairs={{0,4},{4,0},{1,5},{5,1},{2,6},{6,2},{3,7},{7,3},{8,12},{12,8},{9,1... | collective-permute-start | bytes 1290248 | tf_op jit(solution)/shard_map/inner1/ppermute | solution.py:430
  60.3 2.5 %collective-permute-start.16 = (bf16[120,512]{1,0:T(8,128)(2,1)S(1)}, bf16[120,512]{1,0:T(8,128)(2,1)S(1)}, u32[]{:S(2)}, u32[]{:S(2)}) collective-permute-start(bf16[120,512]{1,0:T(8,128)(2,1)S(1)} %get-tuple-element.72), channel_id=1, source_target_pairs={{0,3},{1,2},{2,1},{3,0},{4,7},{5,6},{6,5},{7,4},{8,11},{9,10},{10,... | collective-permute-start | bytes 368648 | tf_op jit(solution)/shard_map/second2_b/ppermute | solution.py:430
  62.8 2.4 %collective-permute-done.15.refs_2_ = bf16[120,512]{1,0:T(8,128)(2,1)S(1)} collective-permute-done((bf16[120,512]{1,0:T(8,128)(2,1)S(1)}, bf16[120,512]{1,0:T(8,128)(2,1)S(1)}, u32[]{:S(2)}, u32[]{:S(2)}) %collective-permute-start.15) | collective-permute-done | bytes 122912 | tf_op jit(solution)/shard_map/second2_a/ppermute | solution.py:430
  67.3 5.1 %collective-permute-start.17 = (bf16[2,120,512]{2,1,0:T(8,128)(2,1)S(1)}, bf16[2,120,512]{2,1,0:T(8,128)(2,1)S(1)}, u32[]{:S(2)}, u32[]{:S(2)}) collective-permute-start(bf16[2,120,512]{2,1,0:T(8,128)(2,1)S(1)} %get-tuple-element.75), channel_id=1, source_target_pairs={{0,4},{4,0},{1,5},{5,1},{2,6},{6,2},{3,7},{7,3},{8,12},{12,8},{9,1... | collective-permute-start | bytes 737288 | tf_op jit(solution)/shard_map/inner2/ppermute | solution.py:430
  77.7 5.6 %collective-permute-done.17.refs_2_ = bf16[2,120,512]{2,1,0:T(8,128)(2,1)S(1)} collective-permute-done((bf16[2,120,512]{2,1,0:T(8,128)(2,1)S(1)}, bf16[2,120,512]{2,1,0:T(8,128)(2,1)S(1)}, u32[]{:S(2)}, u32[]{:S(2)}) %collective-permute-start.17) | collective-permute-done | bytes 245792 | tf_op jit(solution)/shard_map/inner2/ppermute | solution.py:430
  84.1 1.8 %collective-permute-done.20.refs_13_ = bf16[3,256,256]{2,1,0:T(8,128)(2,1)S(1)} collective-permute-done((bf16[3,256,256]{2,1,0:T(8,128)(2,1)S(1)}, bf16[3,256,256]{2,1,0:T(8,128)(2,1)S(1)}, u32[]{:S(2)}, u32[]{:S(2)}) %collective-permute-start.20) | collective-permute-done | bytes 393248 | tf_op jit(solution)/shard_map/along_x2a/ppermute | solution.py:430
  87.1 3.2 %project.1 = (f32[3,120,256]{2,1,0:T(8,128)S(1)}, f32[120,256]{1,0:T(8,128)S(1)}, f32[120,128]{1,0:T(8,128)S(1)}, bf16[120,2048]{1,0:T(8,128)(2,1)}) custom-call(s32[4]{0:T(128)S(1)} %pad_add_fusion.refs_0_, bf16[120,640]{1,0:T(8,128)(2,1)S(1)} %get-tuple-element.64.refs_4_.refs_1_, bf16[120,896]{1,0:T(8,128)(2,1)S(1)} %get-tuple-element.74.refs_4_.refs_2_, ...), custom_call_target="tpu_custom_call" | custom-call | tf_op jit(solution)/shard_map/project/pallas_call | solution.py:52
  91.2 3.1 %collective-permute-start.27 = (bf16[120,384]{1,0:T(8,128)(2,1)S(1)}, bf16[120,384]{1,0:T(8,128)(2,1)S(1)}, u32[]{:S(2)}, u32[]{:S(2)}) collective-permute-start(bf16[120,384]{1,0:T(8,128)(2,1)S(1)} %get-tuple-element.89), channel_id=1, source_target_pairs={{0,3},{1,0},{2,1},{3,2},{4,7},{5,4},{6,5},{7,6},{8,11},{9,8},{10,9... | collective-permute-start | bytes 276488 | tf_op jit(solution)/shard_map/products1/ppermute | solution.py:430
  95.3 3.1 %collective-permute-done.27.refs_3_ = bf16[120,384]{1,0:T(8,128)(2,1)S(1)} collective-permute-done((bf16[120,384]{1,0:T(8,128)(2,1)S(1)}, bf16[120,384]{1,0:T(8,128)(2,1)S(1)}, u32[]{:S(2)}, u32[]{:S(2)}) %collective-permute-start.27) | collective-permute-done | bytes 92192 | tf_op jit(solution)/shard_map/products1/ppermute | solution.py:430
  98.4 2.8 %collective-permute-done.28.refs_4_ = bf16[120,384]{1,0:T(8,128)(2,1)S(1)} collective-permute-done((bf16[120,384]{1,0:T(8,128)(2,1)S(1)}, bf16[120,384]{1,0:T(8,128)(2,1)S(1)}, u32[]{:S(2)}, u32[]{:S(2)}) %collective-permute-start.28) | collective-permute-done | bytes 92192 | tf_op jit(solution)/shard_map/products2/ppermute | solution.py:430
  (59 shorter events, 28.6 us)
Async XLA Ops:
  2.7 10.2 %collective-permute-start = (bf16[2,120,640]{2,1,0:T(8,128)(2,1)S(1)}, bf16[2,120,640]{2,1,0:T(8,128)(2,1)S(1)}, u32[]{:S(2)}, u32[]{:S(2)}) collective-permute-start(bf16[2,120,640]{2,1,0:T(8,128)(2,1)S(1)} %get-tuple-element.48), channel_id=1, source_target_pairs={{0,1},{1,0},{2,3},{3,2},{4,5},{5,4},{6,7},{7,6},{8,9},{9,8},{10,11... | collective-permute-start | bytes 921608 | tf_op jit(solution)/shard_map/first0_a/ppermute | solution.py:430
  4.4 11.4 %collective-permute-start.1 = (bf16[2,120,640]{2,1,0:T(8,128)(2,1)S(1)}, bf16[2,120,640]{2,1,0:T(8,128)(2,1)S(1)}, u32[]{:S(2)}, u32[]{:S(2)}) collective-permute-start(bf16[2,120,640]{2,1,0:T(8,128)(2,1)S(1)} %get-tuple-element.49), channel_id=1, source_target_pairs={{0,3},{1,2},{2,1},{3,0},{4,7},{5,6},{6,5},{7,4},{8,11},{9,10},{10,... | collective-permute-start | bytes 921608 | tf_op jit(solution)/shard_map/first0_b/ppermute | solution.py:430
  8.7 25.2 %collective-permute-start.5 = (bf16[2,120,896]{2,1,0:T(8,128)(2,1)S(1)}, bf16[2,120,896]{2,1,0:T(8,128)(2,1)S(1)}, u32[]{:S(2)}, u32[]{:S(2)}) collective-permute-start(bf16[2,120,896]{2,1,0:T(8,128)(2,1)S(1)} %get-tuple-element.56), channel_id=1, source_target_pairs={{0,1},{1,0},{2,3},{3,2},{4,5},{5,4},{6,7},{7,6},{8,9},{9,8},{10,11... | collective-permute-start | bytes 1290248 | tf_op jit(solution)/shard_map/first1_a/ppermute | solution.py:430
  9.4 24.4 %collective-permute-start.6 = (bf16[2,120,896]{2,1,0:T(8,128)(2,1)S(1)}, bf16[2,120,896]{2,1,0:T(8,128)(2,1)S(1)}, u32[]{:S(2)}, u32[]{:S(2)}) collective-permute-start(bf16[2,120,896]{2,1,0:T(8,128)(2,1)S(1)} %get-tuple-element.57), channel_id=1, source_target_pairs={{0,3},{1,2},{2,1},{3,0},{4,7},{5,6},{6,5},{7,4},{8,11},{9,10},{10,... | collective-permute-start | bytes 1290248 | tf_op jit(solution)/shard_map/first1_b/ppermute | solution.py:430
  16.5 7.8 %collective-permute-start.2 = (bf16[120,640]{1,0:T(8,128)(2,1)S(1)}, bf16[120,640]{1,0:T(8,128)(2,1)S(1)}, u32[]{:S(2)}, u32[]{:S(2)}) collective-permute-start(bf16[120,640]{1,0:T(8,128)(2,1)S(1)} %get-tuple-element.52), channel_id=1, source_target_pairs={{0,1},{1,0},{2,3},{3,2},{4,5},{5,4},{6,7},{7,6},{8,9},{9,8},{10,11... | collective-permute-start | bytes 460808 | tf_op jit(solution)/shard_map/second0_a/ppermute | solution.py:430
  16.6 10.3 %collective-permute-start.3 = (bf16[120,640]{1,0:T(8,128)(2,1)S(1)}, bf16[120,640]{1,0:T(8,128)(2,1)S(1)}, u32[]{:S(2)}, u32[]{:S(2)}) collective-permute-start(bf16[120,640]{1,0:T(8,128)(2,1)S(1)} %get-tuple-element.53), channel_id=1, source_target_pairs={{0,3},{1,2},{2,1},{3,0},{4,7},{5,6},{6,5},{7,4},{8,11},{9,10},{10,... | collective-permute-start | bytes 460808 | tf_op jit(solution)/shard_map/second0_b/ppermute | solution.py:430
  27.5 21.0 %collective-permute-start.4 = (bf16[2,120,640]{2,1,0:T(8,128)(2,1)S(1)}, bf16[2,120,640]{2,1,0:T(8,128)(2,1)S(1)}, u32[]{:S(2)}, u32[]{:S(2)}) collective-permute-start(bf16[2,120,640]{2,1,0:T(8,128)(2,1)S(1)} %get-tuple-element.55), channel_id=1, source_target_pairs={{0,4},{4,0},{1,5},{5,1},{2,6},{6,2},{3,7},{7,3},{8,12},{12,8},{9,1... | collective-permute-start | bytes 921608 | tf_op jit(solution)/shard_map/inner0/ppermute | solution.py:430
  34.7 10.2 %collective-permute-start.8 = (bf16[120,896]{1,0:T(8,128)(2,1)S(1)}, bf16[120,896]{1,0:T(8,128)(2,1)S(1)}, u32[]{:S(2)}, u32[]{:S(2)}) collective-permute-start(bf16[120,896]{1,0:T(8,128)(2,1)S(1)} %get-tuple-element.60), channel_id=1, source_target_pairs={{0,3},{1,2},{2,1},{3,0},{4,7},{5,6},{6,5},{7,4},{8,11},{9,10},{10,... | collective-permute-start | bytes 645128 | tf_op jit(solution)/shard_map/second1_b/ppermute | solution.py:430
  38.8 13.6 %collective-permute-start.12 = (bf16[2,256,256]{2,1,0:T(8,128)(2,1)S(1)}, bf16[2,256,256]{2,1,0:T(8,128)(2,1)S(1)}, u32[]{:S(2)}, u32[]{:S(2)}) collective-permute-start(bf16[2,256,256]{2,1,0:T(8,128)(2,1)S(1)} %get-tuple-element.61.refs_5_), channel_id=1, source_target_pairs={{0,1},{1,2},{2,3},{3,0},{4,5},{5,6},{6,7},{7,4},{8,9},{9,10},{10,1... | collective-permute-start | bytes 786440 | tf_op jit(solution)/shard_map/weights1/ppermute | solution.py:430
  40.2 15.4 %collective-permute-start.13 = (bf16[2,256,256]{2,1,0:T(8,128)(2,1)S(1)}, bf16[2,256,256]{2,1,0:T(8,128)(2,1)S(1)}, u32[]{:S(2)}, u32[]{:S(2)}) collective-permute-start(bf16[2,256,256]{2,1,0:T(8,128)(2,1)S(1)} %get-tuple-element.68), channel_id=1, source_target_pairs={{0,2},{1,3},{2,0},{3,1},{4,6},{5,7},{6,4},{7,5},{8,10},{9,11},{10,... | collective-permute-start | bytes 786440 | tf_op jit(solution)/shard_map/weights2/ppermute | solution.py:430
  41.4 14.2 %collective-permute-start.14 = (bf16[2,256,256]{2,1,0:T(8,128)(2,1)S(1)}, bf16[2,256,256]{2,1,0:T(8,128)(2,1)S(1)}, u32[]{:S(2)}, u32[]{:S(2)}) collective-permute-start(bf16[2,256,256]{2,1,0:T(8,128)(2,1)S(1)} %get-tuple-element.69), channel_id=1, source_target_pairs={{0,3},{1,0},{2,1},{3,2},{4,7},{5,4},{6,5},{7,6},{8,11},{9,8},{10,9... | collective-permute-start | bytes 786440 | tf_op jit(solution)/shard_map/weights3/ppermute | solution.py:430
  47.6 12.0 %collective-permute-start.10 = (bf16[2,120,512]{2,1,0:T(8,128)(2,1)S(1)}, bf16[2,120,512]{2,1,0:T(8,128)(2,1)S(1)}, u32[]{:S(2)}, u32[]{:S(2)}) collective-permute-start(bf16[2,120,512]{2,1,0:T(8,128)(2,1)S(1)} %get-tuple-element.66), channel_id=1, source_target_pairs={{0,1},{1,0},{2,3},{3,2},{4,5},{5,4},{6,7},{7,6},{8,9},{9,8},{10,11... | collective-permute-start | bytes 737288 | tf_op jit(solution)/shard_map/first2_a/ppermute | solution.py:430
  48.5 11.1 %collective-permute-start.11 = (bf16[2,120,512]{2,1,0:T(8,128)(2,1)S(1)}, bf16[2,120,512]{2,1,0:T(8,128)(2,1)S(1)}, u32[]{:S(2)}, u32[]{:S(2)}) collective-permute-start(bf16[2,120,512]{2,1,0:T(8,128)(2,1)S(1)} %get-tuple-element.67), channel_id=1, source_target_pairs={{0,3},{1,2},{2,1},{3,0},{4,7},{5,6},{6,5},{7,4},{8,11},{9,10},{10,... | collective-permute-start | bytes 737288 | tf_op jit(solution)/shard_map/first2_b/ppermute | solution.py:430
  52.5 25.2 %collective-permute-start.9 = (bf16[2,120,896]{2,1,0:T(8,128)(2,1)S(1)}, bf16[2,120,896]{2,1,0:T(8,128)(2,1)S(1)}, u32[]{:S(2)}, u32[]{:S(2)}) collective-permute-start(bf16[2,120,896]{2,1,0:T(8,128)(2,1)S(1)} %get-tuple-element.65), channel_id=1, source_target_pairs={{0,4},{4,0},{1,5},{5,1},{2,6},{6,2},{3,7},{7,3},{8,12},{12,8},{9,1... | collective-permute-start | bytes 1290248 | tf_op jit(solution)/shard_map/inner1/ppermute | solution.py:430
  56.2 17.5 %collective-permute-start.18 = (bf16[2,3,256,256]{3,2,1,0:T(8,128)(2,1)S(1)}, bf16[2,3,256,256]{3,2,1,0:T(8,128)(2,1)S(1)}, u32[]{:S(2)}, u32[]{:S(2)}) collective-permute-start(bf16[2,3,256,256]{3,2,1,0:T(8,128)(2,1)S(1)} %stack.21.refs_4_.refs_10_), channel_id=1, source_target_pairs={{0,64},{64,128},{128,192},{192,0},{1,65},{65,129},{129,193},{193,1... | collective-permute-start | bytes 2359304 | tf_op jit(solution)/shard_map/along_x1/ppermute | solution.py:430
  57.8 16.0 %collective-permute-start.19 = (bf16[2,3,256,256]{3,2,1,0:T(8,128)(2,1)S(1)}, bf16[2,3,256,256]{3,2,1,0:T(8,128)(2,1)S(1)}, u32[]{:S(2)}, u32[]{:S(2)}) collective-permute-start(bf16[2,3,256,256]{3,2,1,0:T(8,128)(2,1)S(1)} %stack.21.refs_4_.refs_10_), channel_id=1, source_target_pairs={{0,192},{64,0},{128,64},{192,128},{1,193},{65,1},{129,65},{193,129... | collective-permute-start | bytes 2359304 | tf_op jit(solution)/shard_map/along_x3/ppermute | solution.py:430
  67.3 16.0 %collective-permute-start.17 = (bf16[2,120,512]{2,1,0:T(8,128)(2,1)S(1)}, bf16[2,120,512]{2,1,0:T(8,128)(2,1)S(1)}, u32[]{:S(2)}, u32[]{:S(2)}) collective-permute-start(bf16[2,120,512]{2,1,0:T(8,128)(2,1)S(1)} %get-tuple-element.75), channel_id=1, source_target_pairs={{0,4},{4,0},{1,5},{5,1},{2,6},{6,2},{3,7},{7,3},{8,12},{12,8},{9,1... | collective-permute-start | bytes 737288 | tf_op jit(solution)/shard_map/inner2/ppermute | solution.py:430
  72.5 14.6 %collective-permute-start.22 = (bf16[2,3,256,256]{3,2,1,0:T(8,128)(2,1)S(1)}, bf16[2,3,256,256]{3,2,1,0:T(8,128)(2,1)S(1)}, u32[]{:S(2)}, u32[]{:S(2)}) collective-permute-start(bf16[2,3,256,256]{3,2,1,0:T(8,128)(2,1)S(1)} %stack.21.refs_4_.refs_10_), channel_id=1, source_target_pairs={{0,8},{8,0},{1,9},{9,1},{2,10},{10,2},{3,11},{11,3},{4,12},{12,4},... | collective-permute-start | bytes 2359304 | tf_op jit(solution)/shard_map/core0/ppermute | solution.py:430
  74.4 11.5 %collective-permute-start.20 = (bf16[3,256,256]{2,1,0:T(8,128)(2,1)S(1)}, bf16[3,256,256]{2,1,0:T(8,128)(2,1)S(1)}, u32[]{:S(2)}, u32[]{:S(2)}) collective-permute-start(bf16[3,256,256]{2,1,0:T(8,128)(2,1)S(1)} %get-tuple-element.83), channel_id=1, source_target_pairs={{0,64},{64,128},{128,192},{192,0},{1,65},{65,129},{129,193},{193,1... | collective-permute-start | bytes 1179656 | tf_op jit(solution)/shard_map/along_x2a/ppermute | solution.py:430
  75.9 10.0 %collective-permute-start.21 = (bf16[3,256,256]{2,1,0:T(8,128)(2,1)S(1)}, bf16[3,256,256]{2,1,0:T(8,128)(2,1)S(1)}, u32[]{:S(2)}, u32[]{:S(2)}) collective-permute-start(bf16[3,256,256]{2,1,0:T(8,128)(2,1)S(1)} %get-tuple-element.84), channel_id=1, source_target_pairs={{0,192},{64,0},{128,64},{192,128},{1,193},{65,1},{129,65},{193,129... | collective-permute-start | bytes 1179656 | tf_op jit(solution)/shard_map/along_x2b/ppermute | solution.py:430
  77.7 9.4 %collective-permute-start.23 = (bf16[2,3,256,256]{3,2,1,0:T(8,128)(2,1)S(1)}, bf16[2,3,256,256]{3,2,1,0:T(8,128)(2,1)S(1)}, u32[]{:S(2)}, u32[]{:S(2)}) collective-permute-start(bf16[2,3,256,256]{3,2,1,0:T(8,128)(2,1)S(1)} %collective-permute-done.18.refs_1_.refs_11_), channel_id=1, source_target_pairs={{0,8},{8,0},{1,9},{9,1},{2,10},{10,2},{3,11},{11,3},{4,12},{12,4},... | collective-permute-start | bytes 2359304 | tf_op jit(solution)/shard_map/core1/ppermute | solution.py:430
  91.2 7.2 %collective-permute-start.27 = (bf16[120,384]{1,0:T(8,128)(2,1)S(1)}, bf16[120,384]{1,0:T(8,128)(2,1)S(1)}, u32[]{:S(2)}, u32[]{:S(2)}) collective-permute-start(bf16[120,384]{1,0:T(8,128)(2,1)S(1)} %get-tuple-element.89), channel_id=1, source_target_pairs={{0,3},{1,0},{2,1},{3,2},{4,7},{5,4},{6,5},{7,6},{8,11},{9,8},{10,9... | collective-permute-start | bytes 276488 | tf_op jit(solution)/shard_map/products1/ppermute | solution.py:430
  94.3 6.9 %collective-permute-start.28 = (bf16[120,384]{1,0:T(8,128)(2,1)S(1)}, bf16[120,384]{1,0:T(8,128)(2,1)S(1)}, u32[]{:S(2)}, u32[]{:S(2)}) collective-permute-start(bf16[120,384]{1,0:T(8,128)(2,1)S(1)} %get-tuple-element.90), channel_id=1, source_target_pairs={{0,2},{1,3},{2,0},{3,1},{4,6},{5,7},{6,4},{7,5},{8,10},{9,11},{10,... | collective-permute-start | bytes 276488 | tf_op jit(solution)/shard_map/products2/ppermute | solution.py:430
  94.3 7.5 %collective-permute-start.29 = (bf16[120,384]{1,0:T(8,128)(2,1)S(1)}, bf16[120,384]{1,0:T(8,128)(2,1)S(1)}, u32[]{:S(2)}, u32[]{:S(2)}) collective-permute-start(bf16[120,384]{1,0:T(8,128)(2,1)S(1)} %get-tuple-element.91), channel_id=1, source_target_pairs={{0,1},{1,2},{2,3},{3,0},{4,5},{5,6},{6,7},{7,4},{8,9},{9,10},{10,1... | collective-permute-start | bytes 276488 | tf_op jit(solution)/shard_map/products3/ppermute | solution.py:430
  (8 other events, 58.9 us)

commit v4 on v3

--- a/solution.py
+++ b/solution.py
@@ -10,7 +10,7 @@
 F32 = jnp.float32
 OUTER = 4
 UNIT = 256
-CHUNKS = ((0, 640), (640, 896), (1536, 512))
+CHUNKS = ((0, 1152), (1152, 896))
 ANY = pl.BlockSpec(memory_space=pl.ANY)
 HBM = pl.BlockSpec(memory_space=pltpu.HBM)
 VMEM = pl.BlockSpec(memory_space=pltpu.VMEM)
@@ -19,7 +19,7 @@
 PAIR_B = [(o, o ^ 3) for o in range(4)]
 SWAP = [(0, 1), (1, 0)]
 MB = 1024 * 1024
-COSTS = (0.0, 8.0, 0.0, 0.0, 0.0, 0.0, 0.0, 10.0, 0.0, 5.0, 5.0)
+COSTS = (0.0, 2.0, 0.0, 12.0, 0.0, 0.0, 0.0, 4.0, 10.0)
 COPY = pltpu.SemaphoreType.DMA
 
 
@@ -240,20 +240,21 @@
     )[0]
 
 
-def halves(ids, from_left, from_right, after=()):
+def halves(ids, own, from_left, from_right, after=()):
     shape = from_left.shape[1:]
 
-    def kernel(ids, a, b, left, right):
+    def kernel(ids, own, a, b, left, right, across):
         left[...] = a[0]
         right[...] = b[1]
+        across[...] = own[...]
 
     return call(
         "halves",
         kernel,
         ids,
-        (from_left, from_right),
-        [VMEM] * 2,
-        [sds(*shape), sds(*shape)],
+        (own, from_left, from_right),
+        [VMEM] * 3,
+        [sds(*shape), sds(*shape), sds(*own.shape)],
         after=after,
     )
 
@@ -435,45 +436,38 @@
             send(label + "_b", pair[1], "outer", PAIR_B),
         )
 
-    c0, c1, c2 = CHUNKS
+    c0, c1 = CHUNKS
     *p0, own0 = pick_columns(ids, partial, c0)
     r0 = cross("first0", p0)
-    *p1, own1 = pick_columns(ids, partial, c1, [own0, COSTS[0]])
+    *f0, keep0 = first_add(ids, own0, *r0, [COSTS[0]])
+    r0 = cross("second0", f0)
+    sent = pick_weights(ids, weight, [keep0])
+    got = [send(f"weights{k}", s, "outer", shift(k)) for k, s in zip((1, 2, 3), sent)]
+    *p1, own1 = pick_columns(ids, partial, c1, [sent[0], COSTS[2]])
     r1 = cross("first1", p1)
-    *f0, keep0 = first_add(ids, own0, *r0, [own1, COSTS[1]])
-    r0 = cross("second0", f0)
-    local0, z0 = second_add(ids, keep0, *r0, residual, c0, [keep0, COSTS[2]])
+    local0, z0 = second_add(ids, keep0, *r0, residual, c0, [own1, COSTS[1]])
     z0 = send("inner0", z0, "inner", SWAP)
-    *f1, keep1 = first_add(ids, own1, *r1, [local0, COSTS[3]])
-    r1 = cross("second1", f1)
-    sent = pick_weights(ids, weight, [keep1])
-    got = [send(f"weights{k}", s, "outer", shift(k)) for k, s in zip((1, 2, 3), sent)]
-    local1, z1 = second_add(ids, keep1, *r1, residual, c1, [sent[0], COSTS[4]])
-    z1 = send("inner1", z1, "inner", SWAP)
-    *p2, own2 = pick_columns(ids, partial, c2, [local1])
-    r2 = cross("first2", p2)
-    stream0, scaled0, squares0 = update(ids, local0, z0, gain, c0, [own2, COSTS[5]])
-    near0 = stack(ids, got, [stream0, COSTS[6]])
+    near0 = stack(ids, got, [local0, COSTS[3]])
     near1 = send("along_x1", near0, "x", shift(1))
     near3 = send("along_x3", near0, "x", shift(3))
-    *f2, keep2 = first_add(ids, own2, *r2, [near0, COSTS[7]])
-    r2 = cross("second2", f2)
-    local2, z2 = second_add(ids, keep2, *r2, residual, c2, [keep2, COSTS[8]])
-    z2 = send("inner2", z2, "inner", SWAP)
-    left, right = halves(ids, near1, near3)
+    *f1, keep1 = first_add(ids, own1, *r1, [near0, COSTS[4]])
+    r1 = cross("second1", f1)
+    local1, z1 = second_add(ids, keep1, *r1, residual, c1, [keep1, COSTS[5]])
+    z1 = send("inner1", z1, "inner", SWAP)
+    stream0, scaled0, squares0 = update(ids, local0, z0, gain, c0, [local1, COSTS[7]])
+    left, right, across = halves(ids, near0, near1, near3, [stream0, COSTS[6]])
     near2a = send("along_x2a", left, "x", shift(1))
     near2b = send("along_x2b", right, "x", shift(3))
-    stream1, scaled1, squares1 = update(ids, local1, z1, gain, c1, [local2, COSTS[9]])
-    stream2, scaled2, squares2 = update(ids, local2, z2, gain, c2, [stream1, COSTS[10]])
+    stream1, scaled1, squares1 = update(ids, local1, z1, gain, c1, [left, COSTS[8]])
     far0, far1, far2a, far2b, far3 = [
         send(f"core{k}", w, "core", SWAP)
-        for k, w in (("0", near0), ("1", near1), ("2a", near2a), ("2b", near2b), ("3", near3))
+        for k, w in (("0", across), ("1", near1), ("2a", near2a), ("2b", near2b), ("3", near3))
     ]
     some, own, total, stream = project(
         ids,
-        [stream0, stream1, stream2],
-        [scaled0, scaled1, scaled2],
-        [squares0, squares1, squares2],
+        [stream0, stream1],
+        [scaled0, scaled1],
+        [squares0, squares1],
         [
             (near0, 0, 2, 0, False),
             (near1, 0, 2, 1, False),
@@ -486,7 +480,7 @@
         ],
         weight,
     )
-    messages = complete(ids, some, total, [scaled0, scaled1, scaled2], [far2a, far2b])
+    messages = complete(ids, some, total, [scaled0, scaled1], [far2a, far2b])
     arrived = [
         send(f"products{k}", m, "outer", shift(-k)) for k, m in zip((1, 2, 3), messages)
     ]

time: 105 us -> 101 us (0.962)
  Pallas kernels: 20.7 us -> 17.3 us
    pallas_call x18 -> x14, Pallas kernels: 20.7 us -> 17.3 us  [call(): pl.pallas_call(kernel, in_specs=in_specs, out_specs=out_specs or [VMEM] *...]
    ppermute x30 -> x25, waiting for transfers between devices: 33.3 us -> 33.7 us  [send(): return lax.ppermute(value, axis, pairs)]
    ppermute x30 -> x25, starting transfers between devices: 48.2 us -> 48.2 us  [send(): return lax.ppermute(value, axis, pairs)]
  transfers between devices with their start and end apart: 30 -> 25, of which waited for: 13 -> 11; matrix products, arithmetic and copies ran while one was open for 0% -> 0% of each run, Pallas kernels for 16% -> 12%
where the time goes in v4:
time: 101 us; the launch traced here: 100 us
  starting transfers between devices  48.2 us (48%)
  waiting for transfers between devices  33.7 us (33%)
  Pallas kernels  17.3 us (17%)
    ppermute x25, starting transfers between devices, send(): return lax.ppermute(value, axis, pairs)  48.2 us
    ppermute x25, waiting for transfers between devices, send(): return lax.ppermute(value, axis, pairs)  33.7 us
    pallas_call x14, Pallas kernels, call(): pl.pallas_call(kernel, in_specs=in_specs, out_specs=out_specs or [VMEM] *...  17.3 us
  transfers between devices with their start and end apart: 25, of which 11 were waited for; matrix products, arithmetic and copies ran while one was open for 0% of the time, Pallas kernels for 12%

profile of v4, /device:TPU:32, one launch (start us, length us, event | category | flops | bytes accessed | tf_op | source)
XLA Modules:
  0.0 100.1 jit_solution(13580094010705747230)
XLA Ops:
  0.7 2.2 %pick_columns.2 = (bf16[2,120,1152]{2,1,0:T(8,128)(2,1)S(1)}, bf16[2,120,1152]{2,1,0:T(8,128)(2,1)S(1)}, bf16[4,120,1152]{2,1,0:T(8,128)(2,1)S(1)}) custom-call(s32[4]{0:T(128)S(1)} %pad_add_fusion.refs_0_, bf16[120,16384]{1,0:T(8,128)(2,1)} %bitcast.12), custom_call_target="tpu_custom_call" | custom-call | tf_op jit(solution)/shard_map/pick_columns/pallas_call | solution.py:52
  2.9 1.7 %collective-permute-start = (bf16[2,120,1152]{2,1,0:T(8,128)(2,1)S(1)}, bf16[2,120,1152]{2,1,0:T(8,128)(2,1)S(1)}, u32[]{:S(2)}, u32[]{:S(2)}) collective-permute-start(bf16[2,120,1152]{2,1,0:T(8,128)(2,1)S(1)} %get-tuple-element.38), channel_id=1, source_target_pairs={{0,1},{1,0},{2,3},{3,2},{4,5},{5,4},{6,7},{7,6},{8,9},{9,8},{10,11... | collective-permute-start | bytes 1658888 | tf_op jit(solution)/shard_map/first0_a/ppermute | solution.py:431
  4.5 2.2 %collective-permute-start.1 = (bf16[2,120,1152]{2,1,0:T(8,128)(2,1)S(1)}, bf16[2,120,1152]{2,1,0:T(8,128)(2,1)S(1)}, u32[]{:S(2)}, u32[]{:S(2)}) collective-permute-start(bf16[2,120,1152]{2,1,0:T(8,128)(2,1)S(1)} %get-tuple-element.39), channel_id=1, source_target_pairs={{0,3},{1,2},{2,1},{3,0},{4,7},{5,6},{6,5},{7,4},{8,11},{9,10},{10,... | collective-permute-start | bytes 1658888 | tf_op jit(solution)/shard_map/first0_b/ppermute | solution.py:431
  6.7 10.5 %collective-permute-done.refs_2_ = bf16[2,120,1152]{2,1,0:T(8,128)(2,1)S(1)} collective-permute-done((bf16[2,120,1152]{2,1,0:T(8,128)(2,1)S(1)}, bf16[2,120,1152]{2,1,0:T(8,128)(2,1)S(1)}, u32[]{:S(2)}, u32[]{:S(2)}) %collective-permute-start) | collective-permute-done | bytes 552992 | tf_op jit(solution)/shard_map/first0_a/ppermute | solution.py:431
  17.2 2.5 %collective-permute-done.1.refs_3_ = bf16[2,120,1152]{2,1,0:T(8,128)(2,1)S(1)} collective-permute-done((bf16[2,120,1152]{2,1,0:T(8,128)(2,1)S(1)}, bf16[2,120,1152]{2,1,0:T(8,128)(2,1)S(1)}, u32[]{:S(2)}, u32[]{:S(2)}) %collective-permute-start.1) | collective-permute-done | bytes 552992 | tf_op jit(solution)/shard_map/first0_b/ppermute | solution.py:431
  20.6 2.3 %collective-permute-start.3 = (bf16[120,1152]{1,0:T(8,128)(2,1)S(1)}, bf16[120,1152]{1,0:T(8,128)(2,1)S(1)}, u32[]{:S(2)}, u32[]{:S(2)}) collective-permute-start(bf16[120,1152]{1,0:T(8,128)(2,1)S(1)} %get-tuple-element.42), channel_id=1, source_target_pairs={{0,3},{1,2},{2,1},{3,0},{4,7},{5,6},{6,5},{7,4},{8,11},{9,10},{10,... | collective-permute-start | bytes 829448 | tf_op jit(solution)/shard_map/second0_b/ppermute | solution.py:431
  22.9 1.8 %pick_weights.1 = (bf16[2,256,256]{2,1,0:T(8,128)(2,1)S(1)}, bf16[2,256,256]{2,1,0:T(8,128)(2,1)S(1)}, bf16[2,256,256]{2,1,0:T(8,128)(2,1)S(1)}) custom-call(s32[4]{0:T(128)S(1)} %pad_add_fusion.refs_0_, bf16[16384,256]{1,0:T(8,128)(2,1)} %bitcast.10, f32[2,120,1152]{2,1,0:T(8,128)S(1)} %get-tuple-element.40.refs_2_.refs_1_), custom_call_target="tpu_custom_call" | custom-call | tf_op jit(solution)/shard_map/pick_weights/pallas_call | solution.py:52
  27.3 1.9 %collective-permute-start.9 = (bf16[2,256,256]{2,1,0:T(8,128)(2,1)S(1)}, bf16[2,256,256]{2,1,0:T(8,128)(2,1)S(1)}, u32[]{:S(2)}, u32[]{:S(2)}) collective-permute-start(bf16[2,256,256]{2,1,0:T(8,128)(2,1)S(1)} %get-tuple-element.50), channel_id=1, source_target_pairs={{0,3},{1,0},{2,1},{3,2},{4,7},{5,4},{6,5},{7,6},{8,11},{9,8},{10,9... | collective-permute-start | bytes 786440 | tf_op jit(solution)/shard_map/weights3/ppermute | solution.py:431
  29.2 2.1 %pick_columns.3 = (bf16[2,120,896]{2,1,0:T(8,128)(2,1)S(1)}, bf16[2,120,896]{2,1,0:T(8,128)(2,1)S(1)}, bf16[4,120,896]{2,1,0:T(8,128)(2,1)S(1)}) custom-call(s32[4]{0:T(128)S(1)} %pad_add_fusion.refs_0_, bf16[120,16384]{1,0:T(8,128)(2,1)} %bitcast.13, bf16[2,256,256]{2,1,0:T(8,128)(2,1)S(1)} %get-tuple-element.43.refs_2_), custom_call_target="tpu_custom_call" | custom-call | tf_op jit(solution)/shard_map/pick_columns/pallas_call | solution.py:52
  32.4 4.2 %collective-permute-start.6 = (bf16[2,120,896]{2,1,0:T(8,128)(2,1)S(1)}, bf16[2,120,896]{2,1,0:T(8,128)(2,1)S(1)}, u32[]{:S(2)}, u32[]{:S(2)}) collective-permute-start(bf16[2,120,896]{2,1,0:T(8,128)(2,1)S(1)} %get-tuple-element.48), channel_id=1, source_target_pairs={{0,3},{1,2},{2,1},{3,0},{4,7},{5,6},{6,5},{7,4},{8,11},{9,10},{10,... | collective-permute-start | bytes 1290248 | tf_op jit(solution)/shard_map/first1_b/ppermute | solution.py:431
  37.4 4.3 %collective-permute-done.7.refs_1_ = bf16[2,256,256]{2,1,0:T(8,128)(2,1)S(1)} collective-permute-done((bf16[2,256,256]{2,1,0:T(8,128)(2,1)S(1)}, bf16[2,256,256]{2,1,0:T(8,128)(2,1)S(1)}, u32[]{:S(2)}, u32[]{:S(2)}) %collective-permute-start.7) | collective-permute-done | bytes 262176 | tf_op jit(solution)/shard_map/weights1/ppermute | solution.py:431
  41.6 6.3 %collective-permute-start.4 = (bf16[2,120,1152]{2,1,0:T(8,128)(2,1)S(1)}, bf16[2,120,1152]{2,1,0:T(8,128)(2,1)S(1)}, u32[]{:S(2)}, u32[]{:S(2)}) collective-permute-start(bf16[2,120,1152]{2,1,0:T(8,128)(2,1)S(1)} %get-tuple-element.46), channel_id=1, source_target_pairs={{0,4},{4,0},{1,5},{5,1},{2,6},{6,2},{3,7},{7,3},{8,12},{12,8},{9,1... | collective-permute-start | bytes 1658888 | tf_op jit(solution)/shard_map/inner0/ppermute | solution.py:431
  50.1 1.7 %collective-permute-start.14 = (bf16[2,3,256,256]{3,2,1,0:T(8,128)(2,1)S(1)}, bf16[2,3,256,256]{3,2,1,0:T(8,128)(2,1)S(1)}, u32[]{:S(2)}, u32[]{:S(2)}) collective-permute-start(bf16[2,3,256,256]{3,2,1,0:T(8,128)(2,1)S(1)} %stack.21.refs_4_.refs_1_.refs_7_), channel_id=1, source_target_pairs={{0,192},{64,0},{128,64},{192,128},{1,193},{65,1},{129,65},{193,129... | collective-permute-start | bytes 2359304 | tf_op jit(solution)/shard_map/along_x3/ppermute | solution.py:431
  53.6 3.1 %collective-permute-start.11 = (bf16[120,896]{1,0:T(8,128)(2,1)S(1)}, bf16[120,896]{1,0:T(8,128)(2,1)S(1)}, u32[]{:S(2)}, u32[]{:S(2)}) collective-permute-start(bf16[120,896]{1,0:T(8,128)(2,1)S(1)} %get-tuple-element.53), channel_id=1, source_target_pairs={{0,3},{1,2},{2,1},{3,0},{4,7},{5,6},{6,5},{7,4},{8,11},{9,10},{10,... | collective-permute-start | bytes 645128 | tf_op jit(solution)/shard_map/second1_b/ppermute | solution.py:431
  56.7 1.9 %collective-permute-done.10.refs_2_ = bf16[120,896]{1,0:T(8,128)(2,1)S(1)} collective-permute-done((bf16[120,896]{1,0:T(8,128)(2,1)S(1)}, bf16[120,896]{1,0:T(8,128)(2,1)S(1)}, u32[]{:S(2)}, u32[]{:S(2)}) %collective-permute-start.10) | collective-permute-done | bytes 215072 | tf_op jit(solution)/shard_map/second1_a/ppermute | solution.py:431
  58.6 2.1 %collective-permute-done.11.refs_3_ = bf16[120,896]{1,0:T(8,128)(2,1)S(1)} collective-permute-done((bf16[120,896]{1,0:T(8,128)(2,1)S(1)}, bf16[120,896]{1,0:T(8,128)(2,1)S(1)}, u32[]{:S(2)}, u32[]{:S(2)}) %collective-permute-start.11) | collective-permute-done | bytes 215072 | tf_op jit(solution)/shard_map/second1_b/ppermute | solution.py:431
  61.4 4.2 %collective-permute-start.12 = (bf16[2,120,896]{2,1,0:T(8,128)(2,1)S(1)}, bf16[2,120,896]{2,1,0:T(8,128)(2,1)S(1)}, u32[]{:S(2)}, u32[]{:S(2)}) collective-permute-start(bf16[2,120,896]{2,1,0:T(8,128)(2,1)S(1)} %get-tuple-element.56), channel_id=1, source_target_pairs={{0,4},{4,0},{1,5},{5,1},{2,6},{6,2},{3,7},{7,3},{8,12},{12,8},{9,1... | collective-permute-start | bytes 1290248 | tf_op jit(solution)/shard_map/inner1/ppermute | solution.py:431
  68.7 1.7 %collective-permute-start.16 = (bf16[3,256,256]{2,1,0:T(8,128)(2,1)S(1)}, bf16[3,256,256]{2,1,0:T(8,128)(2,1)S(1)}, u32[]{:S(2)}, u32[]{:S(2)}) collective-permute-start(bf16[3,256,256]{2,1,0:T(8,128)(2,1)S(1)} %get-tuple-element.63), channel_id=1, source_target_pairs={{0,192},{64,0},{128,64},{192,128},{1,193},{65,1},{129,65},{193,129... | collective-permute-start | bytes 1179656 | tf_op jit(solution)/shard_map/along_x2b/ppermute | solution.py:431
  71.0 6.2 %collective-permute-done.12.refs_2_ = bf16[2,120,896]{2,1,0:T(8,128)(2,1)S(1)} collective-permute-done((bf16[2,120,896]{2,1,0:T(8,128)(2,1)S(1)}, bf16[2,120,896]{2,1,0:T(8,128)(2,1)S(1)}, u32[]{:S(2)}, u32[]{:S(2)}) %collective-permute-start.12) | collective-permute-done | bytes 430112 | tf_op jit(solution)/shard_map/inner1/ppermute | solution.py:431
  79.4 3.1 %project.1 = (f32[3,120,256]{2,1,0:T(8,128)S(1)}, f32[120,256]{1,0:T(8,128)S(1)}, f32[120,128]{1,0:T(8,128)S(1)}, bf16[120,2048]{1,0:T(8,128)(2,1)}) custom-call(s32[4]{0:T(128)S(1)} %pad_add_fusion.refs_0_, bf16[120,1152]{1,0:T(8,128)(2,1)S(1)} %get-tuple-element.55.refs_4_.refs_1_, bf16[120,896]{1,0:T(8,128)(2,1)S(1)} %get-tuple-element.58.refs_2_, ...), custom_call_target="tpu_custom_call" | custom-call | tf_op jit(solution)/shard_map/project/pallas_call | solution.py:52
  83.5 6.3 %collective-permute-start.22 = (bf16[120,384]{1,0:T(8,128)(2,1)S(1)}, bf16[120,384]{1,0:T(8,128)(2,1)S(1)}, u32[]{:S(2)}, u32[]{:S(2)}) collective-permute-start(bf16[120,384]{1,0:T(8,128)(2,1)S(1)} %get-tuple-element.69), channel_id=1, source_target_pairs={{0,3},{1,0},{2,1},{3,2},{4,7},{5,4},{6,5},{7,6},{8,11},{9,8},{10,9... | collective-permute-start | bytes 276488 | tf_op jit(solution)/shard_map/products1/ppermute | solution.py:431
  89.7 3.2 %collective-permute-start.23 = (bf16[120,384]{1,0:T(8,128)(2,1)S(1)}, bf16[120,384]{1,0:T(8,128)(2,1)S(1)}, u32[]{:S(2)}, u32[]{:S(2)}) collective-permute-start(bf16[120,384]{1,0:T(8,128)(2,1)S(1)} %get-tuple-element.70), channel_id=1, source_target_pairs={{0,2},{1,3},{2,0},{3,1},{4,6},{5,7},{6,4},{7,5},{8,10},{9,11},{10,... | collective-permute-start | bytes 276488 | tf_op jit(solution)/shard_map/products2/ppermute | solution.py:431
  94.3 2.3 %collective-permute-done.23.refs_4_ = bf16[120,384]{1,0:T(8,128)(2,1)S(1)} collective-permute-done((bf16[120,384]{1,0:T(8,128)(2,1)S(1)}, bf16[120,384]{1,0:T(8,128)(2,1)S(1)}, u32[]{:S(2)}, u32[]{:S(2)}) %collective-permute-start.23) | collective-permute-done | bytes 92192 | tf_op jit(solution)/shard_map/products2/ppermute | solution.py:431
  96.6 2.1 %collective-permute-done.24.refs_5_ = bf16[120,384]{1,0:T(8,128)(2,1)S(1)} collective-permute-done((bf16[120,384]{1,0:T(8,128)(2,1)S(1)}, bf16[120,384]{1,0:T(8,128)(2,1)S(1)}, u32[]{:S(2)}, u32[]{:S(2)}) %collective-permute-start.24) | collective-permute-done | bytes 92192 | tf_op jit(solution)/shard_map/products3/ppermute | solution.py:431
  (45 shorter events, 19.4 us)
Async XLA Ops:
  2.9 14.4 %collective-permute-start = (bf16[2,120,1152]{2,1,0:T(8,128)(2,1)S(1)}, bf16[2,120,1152]{2,1,0:T(8,128)(2,1)S(1)}, u32[]{:S(2)}, u32[]{:S(2)}) collective-permute-start(bf16[2,120,1152]{2,1,0:T(8,128)(2,1)S(1)} %get-tuple-element.38), channel_id=1, source_target_pairs={{0,1},{1,0},{2,3},{3,2},{4,5},{5,4},{6,7},{7,6},{8,9},{9,8},{10,11... | collective-permute-start | bytes 1658888 | tf_op jit(solution)/shard_map/first0_a/ppermute | solution.py:431
  4.5 15.2 %collective-permute-start.1 = (bf16[2,120,1152]{2,1,0:T(8,128)(2,1)S(1)}, bf16[2,120,1152]{2,1,0:T(8,128)(2,1)S(1)}, u32[]{:S(2)}, u32[]{:S(2)}) collective-permute-start(bf16[2,120,1152]{2,1,0:T(8,128)(2,1)S(1)} %get-tuple-element.39), channel_id=1, source_target_pairs={{0,3},{1,2},{2,1},{3,0},{4,7},{5,6},{6,5},{7,4},{8,11},{9,10},{10,... | collective-permute-start | bytes 1658888 | tf_op jit(solution)/shard_map/first0_b/ppermute | solution.py:431
  20.5 10.8 %collective-permute-start.2 = (bf16[120,1152]{1,0:T(8,128)(2,1)S(1)}, bf16[120,1152]{1,0:T(8,128)(2,1)S(1)}, u32[]{:S(2)}, u32[]{:S(2)}) collective-permute-start(bf16[120,1152]{1,0:T(8,128)(2,1)S(1)} %get-tuple-element.41), channel_id=1, source_target_pairs={{0,1},{1,0},{2,3},{3,2},{4,5},{5,4},{6,7},{7,6},{8,9},{9,8},{10,11... | collective-permute-start | bytes 829448 | tf_op jit(solution)/shard_map/second0_a/ppermute | solution.py:431
  20.6 11.7 %collective-permute-start.3 = (bf16[120,1152]{1,0:T(8,128)(2,1)S(1)}, bf16[120,1152]{1,0:T(8,128)(2,1)S(1)}, u32[]{:S(2)}, u32[]{:S(2)}) collective-permute-start(bf16[120,1152]{1,0:T(8,128)(2,1)S(1)} %get-tuple-element.42), channel_id=1, source_target_pairs={{0,3},{1,2},{2,1},{3,0},{4,7},{5,6},{6,5},{7,4},{8,11},{9,10},{10,... | collective-permute-start | bytes 829448 | tf_op jit(solution)/shard_map/second0_b/ppermute | solution.py:431
  24.7 16.9 %collective-permute-start.7 = (bf16[2,256,256]{2,1,0:T(8,128)(2,1)S(1)}, bf16[2,256,256]{2,1,0:T(8,128)(2,1)S(1)}, u32[]{:S(2)}, u32[]{:S(2)}) collective-permute-start(bf16[2,256,256]{2,1,0:T(8,128)(2,1)S(1)} %get-tuple-element.43.refs_2_), channel_id=1, source_target_pairs={{0,1},{1,2},{2,3},{3,0},{4,5},{5,6},{6,7},{7,4},{8,9},{9,10},{10,1... | collective-permute-start | bytes 786440 | tf_op jit(solution)/shard_map/weights1/ppermute | solution.py:431
  26.1 21.8 %collective-permute-start.8 = (bf16[2,256,256]{2,1,0:T(8,128)(2,1)S(1)}, bf16[2,256,256]{2,1,0:T(8,128)(2,1)S(1)}, u32[]{:S(2)}, u32[]{:S(2)}) collective-permute-start(bf16[2,256,256]{2,1,0:T(8,128)(2,1)S(1)} %get-tuple-element.49), channel_id=1, source_target_pairs={{0,2},{1,3},{2,0},{3,1},{4,6},{5,7},{6,4},{7,5},{8,10},{9,11},{10,... | collective-permute-start | bytes 786440 | tf_op jit(solution)/shard_map/weights2/ppermute | solution.py:431
  27.3 20.6 %collective-permute-start.9 = (bf16[2,256,256]{2,1,0:T(8,128)(2,1)S(1)}, bf16[2,256,256]{2,1,0:T(8,128)(2,1)S(1)}, u32[]{:S(2)}, u32[]{:S(2)}) collective-permute-start(bf16[2,256,256]{2,1,0:T(8,128)(2,1)S(1)} %get-tuple-element.50), channel_id=1, source_target_pairs={{0,3},{1,0},{2,1},{3,2},{4,7},{5,4},{6,5},{7,6},{8,11},{9,8},{10,9... | collective-permute-start | bytes 786440 | tf_op jit(solution)/shard_map/weights3/ppermute | solution.py:431
  31.4 20.5 %collective-permute-start.5 = (bf16[2,120,896]{2,1,0:T(8,128)(2,1)S(1)}, bf16[2,120,896]{2,1,0:T(8,128)(2,1)S(1)}, u32[]{:S(2)}, u32[]{:S(2)}) collective-permute-start(bf16[2,120,896]{2,1,0:T(8,128)(2,1)S(1)} %get-tuple-element.47), channel_id=1, source_target_pairs={{0,1},{1,0},{2,3},{3,2},{4,5},{5,4},{6,7},{7,6},{8,9},{9,8},{10,11... | collective-permute-start | bytes 1290248 | tf_op jit(solution)/shard_map/first1_a/ppermute | solution.py:431
  32.4 19.5 %collective-permute-start.6 = (bf16[2,120,896]{2,1,0:T(8,128)(2,1)S(1)}, bf16[2,120,896]{2,1,0:T(8,128)(2,1)S(1)}, u32[]{:S(2)}, u32[]{:S(2)}) collective-permute-start(bf16[2,120,896]{2,1,0:T(8,128)(2,1)S(1)} %get-tuple-element.48), channel_id=1, source_target_pairs={{0,3},{1,2},{2,1},{3,0},{4,7},{5,6},{6,5},{7,4},{8,11},{9,10},{10,... | collective-permute-start | bytes 1290248 | tf_op jit(solution)/shard_map/first1_b/ppermute | solution.py:431
  41.6 24.0 %collective-permute-start.4 = (bf16[2,120,1152]{2,1,0:T(8,128)(2,1)S(1)}, bf16[2,120,1152]{2,1,0:T(8,128)(2,1)S(1)}, u32[]{:S(2)}, u32[]{:S(2)}) collective-permute-start(bf16[2,120,1152]{2,1,0:T(8,128)(2,1)S(1)} %get-tuple-element.46), channel_id=1, source_target_pairs={{0,4},{4,0},{1,5},{5,1},{2,6},{6,2},{3,7},{7,3},{8,12},{12,8},{9,1... | collective-permute-start | bytes 1658888 | tf_op jit(solution)/shard_map/inner0/ppermute | solution.py:431
  48.5 17.9 %collective-permute-start.13 = (bf16[2,3,256,256]{3,2,1,0:T(8,128)(2,1)S(1)}, bf16[2,3,256,256]{3,2,1,0:T(8,128)(2,1)S(1)}, u32[]{:S(2)}, u32[]{:S(2)}) collective-permute-start(bf16[2,3,256,256]{3,2,1,0:T(8,128)(2,1)S(1)} %stack.21.refs_4_.refs_1_.refs_7_), channel_id=1, source_target_pairs={{0,64},{64,128},{128,192},{192,0},{1,65},{65,129},{129,193},{193,1... | collective-permute-start | bytes 2359304 | tf_op jit(solution)/shard_map/along_x1/ppermute | solution.py:431
  50.1 16.4 %collective-permute-start.14 = (bf16[2,3,256,256]{3,2,1,0:T(8,128)(2,1)S(1)}, bf16[2,3,256,256]{3,2,1,0:T(8,128)(2,1)S(1)}, u32[]{:S(2)}, u32[]{:S(2)}) collective-permute-start(bf16[2,3,256,256]{3,2,1,0:T(8,128)(2,1)S(1)} %stack.21.refs_4_.refs_1_.refs_7_), channel_id=1, source_target_pairs={{0,192},{64,0},{128,64},{192,128},{1,193},{65,1},{129,65},{193,129... | collective-permute-start | bytes 2359304 | tf_op jit(solution)/shard_map/along_x3/ppermute | solution.py:431
  52.6 6.0 %collective-permute-start.10 = (bf16[120,896]{1,0:T(8,128)(2,1)S(1)}, bf16[120,896]{1,0:T(8,128)(2,1)S(1)}, u32[]{:S(2)}, u32[]{:S(2)}) collective-permute-start(bf16[120,896]{1,0:T(8,128)(2,1)S(1)} %get-tuple-element.52), channel_id=1, source_target_pairs={{0,1},{1,0},{2,3},{3,2},{4,5},{5,4},{6,7},{7,6},{8,9},{9,8},{10,11... | collective-permute-start | bytes 645128 | tf_op jit(solution)/shard_map/second1_a/ppermute | solution.py:431
  53.6 7.1 %collective-permute-start.11 = (bf16[120,896]{1,0:T(8,128)(2,1)S(1)}, bf16[120,896]{1,0:T(8,128)(2,1)S(1)}, u32[]{:S(2)}, u32[]{:S(2)}) collective-permute-start(bf16[120,896]{1,0:T(8,128)(2,1)S(1)} %get-tuple-element.53), channel_id=1, source_target_pairs={{0,3},{1,2},{2,1},{3,0},{4,7},{5,6},{6,5},{7,4},{8,11},{9,10},{10,... | collective-permute-start | bytes 645128 | tf_op jit(solution)/shard_map/second1_b/ppermute | solution.py:431
  61.4 15.8 %collective-permute-start.12 = (bf16[2,120,896]{2,1,0:T(8,128)(2,1)S(1)}, bf16[2,120,896]{2,1,0:T(8,128)(2,1)S(1)}, u32[]{:S(2)}, u32[]{:S(2)}) collective-permute-start(bf16[2,120,896]{2,1,0:T(8,128)(2,1)S(1)} %get-tuple-element.56), channel_id=1, source_target_pairs={{0,4},{4,0},{1,5},{5,1},{2,6},{6,2},{3,7},{7,3},{8,12},{12,8},{9,1... | collective-permute-start | bytes 1290248 | tf_op jit(solution)/shard_map/inner1/ppermute | solution.py:431
  67.2 10.4 %collective-permute-start.15 = (bf16[3,256,256]{2,1,0:T(8,128)(2,1)S(1)}, bf16[3,256,256]{2,1,0:T(8,128)(2,1)S(1)}, u32[]{:S(2)}, u32[]{:S(2)}) collective-permute-start(bf16[3,256,256]{2,1,0:T(8,128)(2,1)S(1)} %get-tuple-element.57.refs_4_), channel_id=1, source_target_pairs={{0,64},{64,128},{128,192},{192,0},{1,65},{65,129},{129,193},{193,1... | collective-permute-start | bytes 1179656 | tf_op jit(solution)/shard_map/along_x2a/ppermute | solution.py:431
  68.7 8.9 %collective-permute-start.16 = (bf16[3,256,256]{2,1,0:T(8,128)(2,1)S(1)}, bf16[3,256,256]{2,1,0:T(8,128)(2,1)S(1)}, u32[]{:S(2)}, u32[]{:S(2)}) collective-permute-start(bf16[3,256,256]{2,1,0:T(8,128)(2,1)S(1)} %get-tuple-element.63), channel_id=1, source_target_pairs={{0,192},{64,0},{128,64},{192,128},{1,193},{65,1},{129,65},{193,129... | collective-permute-start | bytes 1179656 | tf_op jit(solution)/shard_map/along_x2b/ppermute | solution.py:431
  70.5 8.4 %collective-permute-start.17 = (bf16[2,3,256,256]{3,2,1,0:T(8,128)(2,1)S(1)}, bf16[2,3,256,256]{3,2,1,0:T(8,128)(2,1)S(1)}, u32[]{:S(2)}, u32[]{:S(2)}) collective-permute-start(bf16[2,3,256,256]{3,2,1,0:T(8,128)(2,1)S(1)} %get-tuple-element.64), channel_id=1, source_target_pairs={{0,8},{8,0},{1,9},{9,1},{2,10},{10,2},{3,11},{11,3},{4,12},{12,4},... | collective-permute-start | bytes 2359304 | tf_op jit(solution)/shard_map/core0/ppermute | solution.py:431
  70.5 8.4 %collective-permute-start.18 = (bf16[2,3,256,256]{3,2,1,0:T(8,128)(2,1)S(1)}, bf16[2,3,256,256]{3,2,1,0:T(8,128)(2,1)S(1)}, u32[]{:S(2)}, u32[]{:S(2)}) collective-permute-start(bf16[2,3,256,256]{3,2,1,0:T(8,128)(2,1)S(1)} %collective-permute-done.13.refs_2_.refs_8_), channel_id=1, source_target_pairs={{0,8},{8,0},{1,9},{9,1},{2,10},{10,2},{3,11},{11,3},{4,12},{12,4},... | collective-permute-start | bytes 2359304 | tf_op jit(solution)/shard_map/core1/ppermute | solution.py:431
  77.5 5.0 %collective-permute-start.20 = (bf16[3,256,256]{2,1,0:T(8,128)(2,1)S(1)}, bf16[3,256,256]{2,1,0:T(8,128)(2,1)S(1)}, u32[]{:S(2)}, u32[]{:S(2)}) collective-permute-start(bf16[3,256,256]{2,1,0:T(8,128)(2,1)S(1)} %collective-permute-done.15.refs_10_), channel_id=1, source_target_pairs={{0,8},{8,0},{1,9},{9,1},{2,10},{10,2},{3,11},{11,3},{4,12},{12,4},... | collective-permute-start | bytes 1179656 | tf_op jit(solution)/shard_map/core2a/ppermute | solution.py:431
  77.7 4.9 %collective-permute-start.21 = (bf16[3,256,256]{2,1,0:T(8,128)(2,1)S(1)}, bf16[3,256,256]{2,1,0:T(8,128)(2,1)S(1)}, u32[]{:S(2)}, u32[]{:S(2)}) collective-permute-start(bf16[3,256,256]{2,1,0:T(8,128)(2,1)S(1)} %collective-permute-done.16.refs_11_), channel_id=1, source_target_pairs={{0,8},{8,0},{1,9},{9,1},{2,10},{10,2},{3,11},{11,3},{4,12},{12,4},... | collective-permute-start | bytes 1179656 | tf_op jit(solution)/shard_map/core2b/ppermute | solution.py:431
  83.5 10.8 %collective-permute-start.22 = (bf16[120,384]{1,0:T(8,128)(2,1)S(1)}, bf16[120,384]{1,0:T(8,128)(2,1)S(1)}, u32[]{:S(2)}, u32[]{:S(2)}) collective-permute-start(bf16[120,384]{1,0:T(8,128)(2,1)S(1)} %get-tuple-element.69), channel_id=1, source_target_pairs={{0,3},{1,0},{2,1},{3,2},{4,7},{5,4},{6,5},{7,6},{8,11},{9,8},{10,9... | collective-permute-start | bytes 276488 | tf_op jit(solution)/shard_map/products1/ppermute | solution.py:431
  89.7 6.9 %collective-permute-start.23 = (bf16[120,384]{1,0:T(8,128)(2,1)S(1)}, bf16[120,384]{1,0:T(8,128)(2,1)S(1)}, u32[]{:S(2)}, u32[]{:S(2)}) collective-permute-start(bf16[120,384]{1,0:T(8,128)(2,1)S(1)} %get-tuple-element.70), channel_id=1, source_target_pairs={{0,2},{1,3},{2,0},{3,1},{4,6},{5,7},{6,4},{7,5},{8,10},{9,11},{10,... | collective-permute-start | bytes 276488 | tf_op jit(solution)/shard_map/products2/ppermute | solution.py:431
  93.0 5.8 %collective-permute-start.24 = (bf16[120,384]{1,0:T(8,128)(2,1)S(1)}, bf16[120,384]{1,0:T(8,128)(2,1)S(1)}, u32[]{:S(2)}, u32[]{:S(2)}) collective-permute-start(bf16[120,384]{1,0:T(8,128)(2,1)S(1)} %get-tuple-element.71), channel_id=1, source_target_pairs={{0,1},{1,2},{2,3},{3,0},{4,5},{5,6},{6,7},{7,4},{8,9},{9,10},{10,1... | collective-permute-start | bytes 276488 | tf_op jit(solution)/shard_map/products3/ppermute | solution.py:431
  (3 other events, 16.5 us)

commit v5 on v4

--- a/solution.py
+++ b/solution.py
@@ -10,7 +10,7 @@
 F32 = jnp.float32
 OUTER = 4
 UNIT = 256
-CHUNKS = ((0, 1152), (1152, 896))
+CHUNKS = ((0, 1280), (1280, 768))
 ANY = pl.BlockSpec(memory_space=pl.ANY)
 HBM = pl.BlockSpec(memory_space=pltpu.HBM)
 VMEM = pl.BlockSpec(memory_space=pltpu.VMEM)
@@ -19,7 +19,7 @@
 PAIR_B = [(o, o ^ 3) for o in range(4)]
 SWAP = [(0, 1), (1, 0)]
 MB = 1024 * 1024
-COSTS = (0.0, 2.0, 0.0, 12.0, 0.0, 0.0, 0.0, 4.0, 10.0)
+COSTS = (0.0, 2.0, 0.0, 2.0, 0.0, 0.0, 0.0, 4.0, 7.0)
 COPY = pltpu.SemaphoreType.DMA
 
 

time: 101 us -> 102 us (level)
  waiting for transfers between devices: 33.7 us -> 42.4 us
  starting transfers between devices: 48.2 us -> 39.7 us
    ppermute x25, waiting for transfers between devices: 33.7 us -> 42.4 us  [send(): return lax.ppermute(value, axis, pairs)]
    ppermute x25, starting transfers between devices: 48.2 us -> 39.7 us  [send(): return lax.ppermute(value, axis, pairs)]
  transfers between devices with their start and end apart: 25 -> 25, of which waited for: 11 -> 12; matrix products, arithmetic and copies ran while one was open for 0% -> 0% of each run, Pallas kernels for 12% -> 12%
where the time goes in v5:
time: 102 us; the launch traced here: 100 us
  waiting for transfers between devices  42.4 us (42%)
  starting transfers between devices  39.7 us (39%)
  Pallas kernels  17.3 us (17%)
    ppermute x25, waiting for transfers between devices, send(): return lax.ppermute(value, axis, pairs)  42.4 us
    ppermute x25, starting transfers between devices, send(): return lax.ppermute(value, axis, pairs)  39.7 us
    pallas_call x14, Pallas kernels, call(): pl.pallas_call(kernel, in_specs=in_specs, out_specs=out_specs or [VMEM] *...  17.3 us
  transfers between devices with their start and end apart: 25, of which 12 were waited for; matrix products, arithmetic and copies ran while one was open for 0% of the time, Pallas kernels for 12%

profile of v5, /device:TPU:32, one launch (start us, length us, event | category | flops | bytes accessed | tf_op | source)
XLA Modules:
  0.0 100.4 jit_solution(9573199022707507069)
XLA Ops:
  0.7 2.2 %pick_columns.2 = (bf16[2,120,1280]{2,1,0:T(8,128)(2,1)S(1)}, bf16[2,120,1280]{2,1,0:T(8,128)(2,1)S(1)}, bf16[4,120,1280]{2,1,0:T(8,128)(2,1)S(1)}) custom-call(s32[4]{0:T(128)S(1)} %pad_add_fusion.refs_0_, bf16[120,16384]{1,0:T(8,128)(2,1)} %bitcast.12), custom_call_target="tpu_custom_call" | custom-call | tf_op jit(solution)/shard_map/pick_columns/pallas_call | solution.py:52
  3.0 1.7 %collective-permute-start = (bf16[2,120,1280]{2,1,0:T(8,128)(2,1)S(1)}, bf16[2,120,1280]{2,1,0:T(8,128)(2,1)S(1)}, u32[]{:S(2)}, u32[]{:S(2)}) collective-permute-start(bf16[2,120,1280]{2,1,0:T(8,128)(2,1)S(1)} %get-tuple-element.38), channel_id=1, source_target_pairs={{0,1},{1,0},{2,3},{3,2},{4,5},{5,4},{6,7},{7,6},{8,9},{9,8},{10,11... | collective-permute-start | bytes 1843208 | tf_op jit(solution)/shard_map/first0_a/ppermute | solution.py:431
  4.6 2.2 %collective-permute-start.1 = (bf16[2,120,1280]{2,1,0:T(8,128)(2,1)S(1)}, bf16[2,120,1280]{2,1,0:T(8,128)(2,1)S(1)}, u32[]{:S(2)}, u32[]{:S(2)}) collective-permute-start(bf16[2,120,1280]{2,1,0:T(8,128)(2,1)S(1)} %get-tuple-element.39), channel_id=1, source_target_pairs={{0,3},{1,2},{2,1},{3,0},{4,7},{5,6},{6,5},{7,4},{8,11},{9,10},{10,... | collective-permute-start | bytes 1843208 | tf_op jit(solution)/shard_map/first0_b/ppermute | solution.py:431
  6.8 11.8 %collective-permute-done.refs_2_ = bf16[2,120,1280]{2,1,0:T(8,128)(2,1)S(1)} collective-permute-done((bf16[2,120,1280]{2,1,0:T(8,128)(2,1)S(1)}, bf16[2,120,1280]{2,1,0:T(8,128)(2,1)S(1)}, u32[]{:S(2)}, u32[]{:S(2)}) %collective-permute-start) | collective-permute-done | bytes 614432 | tf_op jit(solution)/shard_map/first0_a/ppermute | solution.py:431
  18.6 2.5 %collective-permute-done.1.refs_3_ = bf16[2,120,1280]{2,1,0:T(8,128)(2,1)S(1)} collective-permute-done((bf16[2,120,1280]{2,1,0:T(8,128)(2,1)S(1)}, bf16[2,120,1280]{2,1,0:T(8,128)(2,1)S(1)}, u32[]{:S(2)}, u32[]{:S(2)}) %collective-permute-start.1) | collective-permute-done | bytes 614432 | tf_op jit(solution)/shard_map/first0_b/ppermute | solution.py:431
  22.1 2.3 %collective-permute-start.3 = (bf16[120,1280]{1,0:T(8,128)(2,1)S(1)}, bf16[120,1280]{1,0:T(8,128)(2,1)S(1)}, u32[]{:S(2)}, u32[]{:S(2)}) collective-permute-start(bf16[120,1280]{1,0:T(8,128)(2,1)S(1)} %get-tuple-element.42), channel_id=1, source_target_pairs={{0,3},{1,2},{2,1},{3,0},{4,7},{5,6},{6,5},{7,4},{8,11},{9,10},{10,... | collective-permute-start | bytes 921608 | tf_op jit(solution)/shard_map/second0_b/ppermute | solution.py:431
  24.4 1.8 %pick_weights.1 = (bf16[2,256,256]{2,1,0:T(8,128)(2,1)S(1)}, bf16[2,256,256]{2,1,0:T(8,128)(2,1)S(1)}, bf16[2,256,256]{2,1,0:T(8,128)(2,1)S(1)}) custom-call(s32[4]{0:T(128)S(1)} %pad_add_fusion.refs_0_, bf16[16384,256]{1,0:T(8,128)(2,1)} %bitcast.10, f32[2,120,1280]{2,1,0:T(8,128)S(1)} %get-tuple-element.40.refs_2_.refs_1_), custom_call_target="tpu_custom_call" | custom-call | tf_op jit(solution)/shard_map/pick_weights/pallas_call | solution.py:52
  28.8 1.9 %collective-permute-start.9 = (bf16[2,256,256]{2,1,0:T(8,128)(2,1)S(1)}, bf16[2,256,256]{2,1,0:T(8,128)(2,1)S(1)}, u32[]{:S(2)}, u32[]{:S(2)}) collective-permute-start(bf16[2,256,256]{2,1,0:T(8,128)(2,1)S(1)} %get-tuple-element.50), channel_id=1, source_target_pairs={{0,3},{1,0},{2,1},{3,2},{4,7},{5,4},{6,5},{7,6},{8,11},{9,8},{10,9... | collective-permute-start | bytes 786440 | tf_op jit(solution)/shard_map/weights3/ppermute | solution.py:431
  30.7 2.0 %pick_columns.3 = (bf16[2,120,768]{2,1,0:T(8,128)(2,1)S(1)}, bf16[2,120,768]{2,1,0:T(8,128)(2,1)S(1)}, bf16[4,120,768]{2,1,0:T(8,128)(2,1)S(1)}) custom-call(s32[4]{0:T(128)S(1)} %pad_add_fusion.refs_0_, bf16[120,16384]{1,0:T(8,128)(2,1)} %bitcast.13, bf16[2,256,256]{2,1,0:T(8,128)(2,1)S(1)} %get-tuple-element.43.refs_2_), custom_call_target="tpu_custom_call" | custom-call | tf_op jit(solution)/shard_map/pick_columns/pallas_call | solution.py:52
  32.8 3.7 %collective-permute-done.3.refs_3_ = bf16[120,1280]{1,0:T(8,128)(2,1)S(1)} collective-permute-done((bf16[120,1280]{1,0:T(8,128)(2,1)S(1)}, bf16[120,1280]{1,0:T(8,128)(2,1)S(1)}, u32[]{:S(2)}, u32[]{:S(2)}) %collective-permute-start.3) | collective-permute-done | bytes 307232 | tf_op jit(solution)/shard_map/second0_b/ppermute | solution.py:431
  37.3 6.4 %collective-permute-start.4 = (bf16[2,120,1280]{2,1,0:T(8,128)(2,1)S(1)}, bf16[2,120,1280]{2,1,0:T(8,128)(2,1)S(1)}, u32[]{:S(2)}, u32[]{:S(2)}) collective-permute-start(bf16[2,120,1280]{2,1,0:T(8,128)(2,1)S(1)} %get-tuple-element.46), channel_id=1, source_target_pairs={{0,4},{4,0},{1,5},{5,1},{2,6},{6,2},{3,7},{7,3},{8,12},{12,8},{9,1... | collective-permute-start | bytes 1843208 | tf_op jit(solution)/shard_map/inner0/ppermute | solution.py:431
  43.7 1.6 %collective-permute-start.5 = (bf16[2,120,768]{2,1,0:T(8,128)(2,1)S(1)}, bf16[2,120,768]{2,1,0:T(8,128)(2,1)S(1)}, u32[]{:S(2)}, u32[]{:S(2)}) collective-permute-start(bf16[2,120,768]{2,1,0:T(8,128)(2,1)S(1)} %get-tuple-element.47), channel_id=1, source_target_pairs={{0,1},{1,0},{2,3},{3,2},{4,5},{5,4},{6,7},{7,6},{8,9},{9,8},{10,11... | collective-permute-start | bytes 1105928 | tf_op jit(solution)/shard_map/first1_a/ppermute | solution.py:431
  45.3 2.3 %collective-permute-start.6 = (bf16[2,120,768]{2,1,0:T(8,128)(2,1)S(1)}, bf16[2,120,768]{2,1,0:T(8,128)(2,1)S(1)}, u32[]{:S(2)}, u32[]{:S(2)}) collective-permute-start(bf16[2,120,768]{2,1,0:T(8,128)(2,1)S(1)} %get-tuple-element.48), channel_id=1, source_target_pairs={{0,3},{1,2},{2,1},{3,0},{4,7},{5,6},{6,5},{7,4},{8,11},{9,10},{10,... | collective-permute-start | bytes 1105928 | tf_op jit(solution)/shard_map/first1_b/ppermute | solution.py:431
  49.8 1.7 %collective-permute-start.14 = (bf16[2,3,256,256]{3,2,1,0:T(8,128)(2,1)S(1)}, bf16[2,3,256,256]{3,2,1,0:T(8,128)(2,1)S(1)}, u32[]{:S(2)}, u32[]{:S(2)}) collective-permute-start(bf16[2,3,256,256]{3,2,1,0:T(8,128)(2,1)S(1)} %stack.21.refs_4_.refs_1_.refs_7_), channel_id=1, source_target_pairs={{0,192},{64,0},{128,64},{192,128},{1,193},{65,1},{129,65},{193,129... | collective-permute-start | bytes 2359304 | tf_op jit(solution)/shard_map/along_x3/ppermute | solution.py:431
  52.3 3.7 %collective-permute-done.6.refs_3_ = bf16[2,120,768]{2,1,0:T(8,128)(2,1)S(1)} collective-permute-done((bf16[2,120,768]{2,1,0:T(8,128)(2,1)S(1)}, bf16[2,120,768]{2,1,0:T(8,128)(2,1)S(1)}, u32[]{:S(2)}, u32[]{:S(2)}) %collective-permute-start.6) | collective-permute-done | bytes 368672 | tf_op jit(solution)/shard_map/first1_b/ppermute | solution.py:431
  57.4 2.6 %collective-permute-start.11 = (bf16[120,768]{1,0:T(8,128)(2,1)S(1)}, bf16[120,768]{1,0:T(8,128)(2,1)S(1)}, u32[]{:S(2)}, u32[]{:S(2)}) collective-permute-start(bf16[120,768]{1,0:T(8,128)(2,1)S(1)} %get-tuple-element.53), channel_id=1, source_target_pairs={{0,3},{1,2},{2,1},{3,0},{4,7},{5,6},{6,5},{7,4},{8,11},{9,10},{10,... | collective-permute-start | bytes 552968 | tf_op jit(solution)/shard_map/second1_b/ppermute | solution.py:431
  60.0 2.4 %collective-permute-done.10.refs_2_ = bf16[120,768]{1,0:T(8,128)(2,1)S(1)} collective-permute-done((bf16[120,768]{1,0:T(8,128)(2,1)S(1)}, bf16[120,768]{1,0:T(8,128)(2,1)S(1)}, u32[]{:S(2)}, u32[]{:S(2)}) %collective-permute-start.10) | collective-permute-done | bytes 184352 | tf_op jit(solution)/shard_map/second1_a/ppermute | solution.py:431
  62.4 1.7 %collective-permute-done.11.refs_3_ = bf16[120,768]{1,0:T(8,128)(2,1)S(1)} collective-permute-done((bf16[120,768]{1,0:T(8,128)(2,1)S(1)}, bf16[120,768]{1,0:T(8,128)(2,1)S(1)}, u32[]{:S(2)}, u32[]{:S(2)}) %collective-permute-start.11) | collective-permute-done | bytes 184352 | tf_op jit(solution)/shard_map/second1_b/ppermute | solution.py:431
  69.2 1.7 %collective-permute-start.16 = (bf16[3,256,256]{2,1,0:T(8,128)(2,1)S(1)}, bf16[3,256,256]{2,1,0:T(8,128)(2,1)S(1)}, u32[]{:S(2)}, u32[]{:S(2)}) collective-permute-start(bf16[3,256,256]{2,1,0:T(8,128)(2,1)S(1)} %get-tuple-element.63), channel_id=1, source_target_pairs={{0,192},{64,0},{128,64},{192,128},{1,193},{65,1},{129,65},{193,129... | collective-permute-start | bytes 1179656 | tf_op jit(solution)/shard_map/along_x2b/ppermute | solution.py:431
  71.4 8.2 %collective-permute-done.12.refs_2_ = bf16[2,120,768]{2,1,0:T(8,128)(2,1)S(1)} collective-permute-done((bf16[2,120,768]{2,1,0:T(8,128)(2,1)S(1)}, bf16[2,120,768]{2,1,0:T(8,128)(2,1)S(1)}, u32[]{:S(2)}, u32[]{:S(2)}) %collective-permute-start.12) | collective-permute-done | bytes 368672 | tf_op jit(solution)/shard_map/inner1/ppermute | solution.py:431
  81.9 3.1 %project.1 = (f32[3,120,256]{2,1,0:T(8,128)S(1)}, f32[120,256]{1,0:T(8,128)S(1)}, f32[120,128]{1,0:T(8,128)S(1)}, bf16[120,2048]{1,0:T(8,128)(2,1)}) custom-call(s32[4]{0:T(128)S(1)} %pad_add_fusion.refs_0_, bf16[120,1280]{1,0:T(8,128)(2,1)S(1)} %get-tuple-element.55.refs_4_.refs_1_, bf16[120,768]{1,0:T(8,128)(2,1)S(1)} %get-tuple-element.58.refs_2_, ...), custom_call_target="tpu_custom_call" | custom-call | tf_op jit(solution)/shard_map/project/pallas_call | solution.py:52
  85.9 5.5 %collective-permute-start.22 = (bf16[120,384]{1,0:T(8,128)(2,1)S(1)}, bf16[120,384]{1,0:T(8,128)(2,1)S(1)}, u32[]{:S(2)}, u32[]{:S(2)}) collective-permute-start(bf16[120,384]{1,0:T(8,128)(2,1)S(1)} %get-tuple-element.69), channel_id=1, source_target_pairs={{0,3},{1,0},{2,1},{3,2},{4,7},{5,4},{6,5},{7,6},{8,11},{9,8},{10,9... | collective-permute-start | bytes 276488 | tf_op jit(solution)/shard_map/products1/ppermute | solution.py:431
  92.4 3.2 %collective-permute-done.22.refs_3_ = bf16[120,384]{1,0:T(8,128)(2,1)S(1)} collective-permute-done((bf16[120,384]{1,0:T(8,128)(2,1)S(1)}, bf16[120,384]{1,0:T(8,128)(2,1)S(1)}, u32[]{:S(2)}, u32[]{:S(2)}) %collective-permute-start.22) | collective-permute-done | bytes 92192 | tf_op jit(solution)/shard_map/products1/ppermute | solution.py:431
  95.6 2.8 %collective-permute-done.23.refs_4_ = bf16[120,384]{1,0:T(8,128)(2,1)S(1)} collective-permute-done((bf16[120,384]{1,0:T(8,128)(2,1)S(1)}, bf16[120,384]{1,0:T(8,128)(2,1)S(1)}, u32[]{:S(2)}, u32[]{:S(2)}) %collective-permute-start.23) | collective-permute-done | bytes 92192 | tf_op jit(solution)/shard_map/products2/ppermute | solution.py:431
  (45 shorter events, 20.3 us)
Async XLA Ops:
  3.0 15.7 %collective-permute-start = (bf16[2,120,1280]{2,1,0:T(8,128)(2,1)S(1)}, bf16[2,120,1280]{2,1,0:T(8,128)(2,1)S(1)}, u32[]{:S(2)}, u32[]{:S(2)}) collective-permute-start(bf16[2,120,1280]{2,1,0:T(8,128)(2,1)S(1)} %get-tuple-element.38), channel_id=1, source_target_pairs={{0,1},{1,0},{2,3},{3,2},{4,5},{5,4},{6,7},{7,6},{8,9},{9,8},{10,11... | collective-permute-start | bytes 1843208 | tf_op jit(solution)/shard_map/first0_a/ppermute | solution.py:431
  4.6 16.5 %collective-permute-start.1 = (bf16[2,120,1280]{2,1,0:T(8,128)(2,1)S(1)}, bf16[2,120,1280]{2,1,0:T(8,128)(2,1)S(1)}, u32[]{:S(2)}, u32[]{:S(2)}) collective-permute-start(bf16[2,120,1280]{2,1,0:T(8,128)(2,1)S(1)} %get-tuple-element.39), channel_id=1, source_target_pairs={{0,3},{1,2},{2,1},{3,0},{4,7},{5,6},{6,5},{7,4},{8,11},{9,10},{10,... | collective-permute-start | bytes 1843208 | tf_op jit(solution)/shard_map/first0_b/ppermute | solution.py:431
  22.0 10.8 %collective-permute-start.2 = (bf16[120,1280]{1,0:T(8,128)(2,1)S(1)}, bf16[120,1280]{1,0:T(8,128)(2,1)S(1)}, u32[]{:S(2)}, u32[]{:S(2)}) collective-permute-start(bf16[120,1280]{1,0:T(8,128)(2,1)S(1)} %get-tuple-element.41), channel_id=1, source_target_pairs={{0,1},{1,0},{2,3},{3,2},{4,5},{5,4},{6,7},{7,6},{8,9},{9,8},{10,11... | collective-permute-start | bytes 921608 | tf_op jit(solution)/shard_map/second0_a/ppermute | solution.py:431
  22.1 14.4 %collective-permute-start.3 = (bf16[120,1280]{1,0:T(8,128)(2,1)S(1)}, bf16[120,1280]{1,0:T(8,128)(2,1)S(1)}, u32[]{:S(2)}, u32[]{:S(2)}) collective-permute-start(bf16[120,1280]{1,0:T(8,128)(2,1)S(1)} %get-tuple-element.42), channel_id=1, source_target_pairs={{0,3},{1,2},{2,1},{3,0},{4,7},{5,6},{6,5},{7,4},{8,11},{9,10},{10,... | collective-permute-start | bytes 921608 | tf_op jit(solution)/shard_map/second0_b/ppermute | solution.py:431
  26.2 19.1 %collective-permute-start.7 = (bf16[2,256,256]{2,1,0:T(8,128)(2,1)S(1)}, bf16[2,256,256]{2,1,0:T(8,128)(2,1)S(1)}, u32[]{:S(2)}, u32[]{:S(2)}) collective-permute-start(bf16[2,256,256]{2,1,0:T(8,128)(2,1)S(1)} %get-tuple-element.43.refs_2_), channel_id=1, source_target_pairs={{0,1},{1,2},{2,3},{3,0},{4,5},{5,6},{6,7},{7,4},{8,9},{9,10},{10,1... | collective-permute-start | bytes 786440 | tf_op jit(solution)/shard_map/weights1/ppermute | solution.py:431
  27.6 20.1 %collective-permute-start.8 = (bf16[2,256,256]{2,1,0:T(8,128)(2,1)S(1)}, bf16[2,256,256]{2,1,0:T(8,128)(2,1)S(1)}, u32[]{:S(2)}, u32[]{:S(2)}) collective-permute-start(bf16[2,256,256]{2,1,0:T(8,128)(2,1)S(1)} %get-tuple-element.49), channel_id=1, source_target_pairs={{0,2},{1,3},{2,0},{3,1},{4,6},{5,7},{6,4},{7,5},{8,10},{9,11},{10,... | collective-permute-start | bytes 786440 | tf_op jit(solution)/shard_map/weights2/ppermute | solution.py:431
  28.8 18.9 %collective-permute-start.9 = (bf16[2,256,256]{2,1,0:T(8,128)(2,1)S(1)}, bf16[2,256,256]{2,1,0:T(8,128)(2,1)S(1)}, u32[]{:S(2)}, u32[]{:S(2)}) collective-permute-start(bf16[2,256,256]{2,1,0:T(8,128)(2,1)S(1)} %get-tuple-element.50), channel_id=1, source_target_pairs={{0,3},{1,0},{2,1},{3,2},{4,7},{5,4},{6,5},{7,6},{8,11},{9,8},{10,9... | collective-permute-start | bytes 786440 | tf_op jit(solution)/shard_map/weights3/ppermute | solution.py:431
  37.3 28.7 %collective-permute-start.4 = (bf16[2,120,1280]{2,1,0:T(8,128)(2,1)S(1)}, bf16[2,120,1280]{2,1,0:T(8,128)(2,1)S(1)}, u32[]{:S(2)}, u32[]{:S(2)}) collective-permute-start(bf16[2,120,1280]{2,1,0:T(8,128)(2,1)S(1)} %get-tuple-element.46), channel_id=1, source_target_pairs={{0,4},{4,0},{1,5},{5,1},{2,6},{6,2},{3,7},{7,3},{8,12},{12,8},{9,1... | collective-permute-start | bytes 1843208 | tf_op jit(solution)/shard_map/inner0/ppermute | solution.py:431
  43.7 8.7 %collective-permute-start.5 = (bf16[2,120,768]{2,1,0:T(8,128)(2,1)S(1)}, bf16[2,120,768]{2,1,0:T(8,128)(2,1)S(1)}, u32[]{:S(2)}, u32[]{:S(2)}) collective-permute-start(bf16[2,120,768]{2,1,0:T(8,128)(2,1)S(1)} %get-tuple-element.47), channel_id=1, source_target_pairs={{0,1},{1,0},{2,3},{3,2},{4,5},{5,4},{6,7},{7,6},{8,9},{9,8},{10,11... | collective-permute-start | bytes 1105928 | tf_op jit(solution)/shard_map/first1_a/ppermute | solution.py:431
  45.3 10.7 %collective-permute-start.6 = (bf16[2,120,768]{2,1,0:T(8,128)(2,1)S(1)}, bf16[2,120,768]{2,1,0:T(8,128)(2,1)S(1)}, u32[]{:S(2)}, u32[]{:S(2)}) collective-permute-start(bf16[2,120,768]{2,1,0:T(8,128)(2,1)S(1)} %get-tuple-element.48), channel_id=1, source_target_pairs={{0,3},{1,2},{2,1},{3,0},{4,7},{5,6},{6,5},{7,4},{8,11},{9,10},{10,... | collective-permute-start | bytes 1105928 | tf_op jit(solution)/shard_map/first1_b/ppermute | solution.py:431
  48.3 18.6 %collective-permute-start.13 = (bf16[2,3,256,256]{3,2,1,0:T(8,128)(2,1)S(1)}, bf16[2,3,256,256]{3,2,1,0:T(8,128)(2,1)S(1)}, u32[]{:S(2)}, u32[]{:S(2)}) collective-permute-start(bf16[2,3,256,256]{3,2,1,0:T(8,128)(2,1)S(1)} %stack.21.refs_4_.refs_1_.refs_7_), channel_id=1, source_target_pairs={{0,64},{64,128},{128,192},{192,0},{1,65},{65,129},{129,193},{193,1... | collective-permute-start | bytes 2359304 | tf_op jit(solution)/shard_map/along_x1/ppermute | solution.py:431
  49.8 17.1 %collective-permute-start.14 = (bf16[2,3,256,256]{3,2,1,0:T(8,128)(2,1)S(1)}, bf16[2,3,256,256]{3,2,1,0:T(8,128)(2,1)S(1)}, u32[]{:S(2)}, u32[]{:S(2)}) collective-permute-start(bf16[2,3,256,256]{3,2,1,0:T(8,128)(2,1)S(1)} %stack.21.refs_4_.refs_1_.refs_7_), channel_id=1, source_target_pairs={{0,192},{64,0},{128,64},{192,128},{1,193},{65,1},{129,65},{193,129... | collective-permute-start | bytes 2359304 | tf_op jit(solution)/shard_map/along_x3/ppermute | solution.py:431
  56.8 5.6 %collective-permute-start.10 = (bf16[120,768]{1,0:T(8,128)(2,1)S(1)}, bf16[120,768]{1,0:T(8,128)(2,1)S(1)}, u32[]{:S(2)}, u32[]{:S(2)}) collective-permute-start(bf16[120,768]{1,0:T(8,128)(2,1)S(1)} %get-tuple-element.52), channel_id=1, source_target_pairs={{0,1},{1,0},{2,3},{3,2},{4,5},{5,4},{6,7},{7,6},{8,9},{9,8},{10,11... | collective-permute-start | bytes 552968 | tf_op jit(solution)/shard_map/second1_a/ppermute | solution.py:431
  57.4 6.7 %collective-permute-start.11 = (bf16[120,768]{1,0:T(8,128)(2,1)S(1)}, bf16[120,768]{1,0:T(8,128)(2,1)S(1)}, u32[]{:S(2)}, u32[]{:S(2)}) collective-permute-start(bf16[120,768]{1,0:T(8,128)(2,1)S(1)} %get-tuple-element.53), channel_id=1, source_target_pairs={{0,3},{1,2},{2,1},{3,0},{4,7},{5,6},{6,5},{7,4},{8,11},{9,10},{10,... | collective-permute-start | bytes 552968 | tf_op jit(solution)/shard_map/second1_b/ppermute | solution.py:431
  64.8 14.8 %collective-permute-start.12 = (bf16[2,120,768]{2,1,0:T(8,128)(2,1)S(1)}, bf16[2,120,768]{2,1,0:T(8,128)(2,1)S(1)}, u32[]{:S(2)}, u32[]{:S(2)}) collective-permute-start(bf16[2,120,768]{2,1,0:T(8,128)(2,1)S(1)} %get-tuple-element.56), channel_id=1, source_target_pairs={{0,4},{4,0},{1,5},{5,1},{2,6},{6,2},{3,7},{7,3},{8,12},{12,8},{9,1... | collective-permute-start | bytes 1105928 | tf_op jit(solution)/shard_map/inner1/ppermute | solution.py:431
  67.6 12.1 %collective-permute-start.15 = (bf16[3,256,256]{2,1,0:T(8,128)(2,1)S(1)}, bf16[3,256,256]{2,1,0:T(8,128)(2,1)S(1)}, u32[]{:S(2)}, u32[]{:S(2)}) collective-permute-start(bf16[3,256,256]{2,1,0:T(8,128)(2,1)S(1)} %get-tuple-element.57.refs_4_), channel_id=1, source_target_pairs={{0,64},{64,128},{128,192},{192,0},{1,65},{65,129},{129,193},{193,1... | collective-permute-start | bytes 1179656 | tf_op jit(solution)/shard_map/along_x2a/ppermute | solution.py:431
  69.2 11.0 %collective-permute-start.16 = (bf16[3,256,256]{2,1,0:T(8,128)(2,1)S(1)}, bf16[3,256,256]{2,1,0:T(8,128)(2,1)S(1)}, u32[]{:S(2)}, u32[]{:S(2)}) collective-permute-start(bf16[3,256,256]{2,1,0:T(8,128)(2,1)S(1)} %get-tuple-element.63), channel_id=1, source_target_pairs={{0,192},{64,0},{128,64},{192,128},{1,193},{65,1},{129,65},{193,129... | collective-permute-start | bytes 1179656 | tf_op jit(solution)/shard_map/along_x2b/ppermute | solution.py:431
  70.9 10.1 %collective-permute-start.17 = (bf16[2,3,256,256]{3,2,1,0:T(8,128)(2,1)S(1)}, bf16[2,3,256,256]{3,2,1,0:T(8,128)(2,1)S(1)}, u32[]{:S(2)}, u32[]{:S(2)}) collective-permute-start(bf16[2,3,256,256]{3,2,1,0:T(8,128)(2,1)S(1)} %get-tuple-element.64), channel_id=1, source_target_pairs={{0,8},{8,0},{1,9},{9,1},{2,10},{10,2},{3,11},{11,3},{4,12},{12,4},... | collective-permute-start | bytes 2359304 | tf_op jit(solution)/shard_map/core0/ppermute | solution.py:431
  70.9 10.1 %collective-permute-start.18 = (bf16[2,3,256,256]{3,2,1,0:T(8,128)(2,1)S(1)}, bf16[2,3,256,256]{3,2,1,0:T(8,128)(2,1)S(1)}, u32[]{:S(2)}, u32[]{:S(2)}) collective-permute-start(bf16[2,3,256,256]{3,2,1,0:T(8,128)(2,1)S(1)} %collective-permute-done.13.refs_2_.refs_8_), channel_id=1, source_target_pairs={{0,8},{8,0},{1,9},{9,1},{2,10},{10,2},{3,11},{11,3},{4,12},{12,4},... | collective-permute-start | bytes 2359304 | tf_op jit(solution)/shard_map/core1/ppermute | solution.py:431
  79.6 5.4 %collective-permute-start.20 = (bf16[3,256,256]{2,1,0:T(8,128)(2,1)S(1)}, bf16[3,256,256]{2,1,0:T(8,128)(2,1)S(1)}, u32[]{:S(2)}, u32[]{:S(2)}) collective-permute-start(bf16[3,256,256]{2,1,0:T(8,128)(2,1)S(1)} %collective-permute-done.15.refs_10_), channel_id=1, source_target_pairs={{0,8},{8,0},{1,9},{9,1},{2,10},{10,2},{3,11},{11,3},{4,12},{12,4},... | collective-permute-start | bytes 1179656 | tf_op jit(solution)/shard_map/core2a/ppermute | solution.py:431
  80.2 4.9 %collective-permute-start.21 = (bf16[3,256,256]{2,1,0:T(8,128)(2,1)S(1)}, bf16[3,256,256]{2,1,0:T(8,128)(2,1)S(1)}, u32[]{:S(2)}, u32[]{:S(2)}) collective-permute-start(bf16[3,256,256]{2,1,0:T(8,128)(2,1)S(1)} %collective-permute-done.16.refs_11_), channel_id=1, source_target_pairs={{0,8},{8,0},{1,9},{9,1},{2,10},{10,2},{3,11},{11,3},{4,12},{12,4},... | collective-permute-start | bytes 1179656 | tf_op jit(solution)/shard_map/core2b/ppermute | solution.py:431
  85.9 9.7 %collective-permute-start.22 = (bf16[120,384]{1,0:T(8,128)(2,1)S(1)}, bf16[120,384]{1,0:T(8,128)(2,1)S(1)}, u32[]{:S(2)}, u32[]{:S(2)}) collective-permute-start(bf16[120,384]{1,0:T(8,128)(2,1)S(1)} %get-tuple-element.69), channel_id=1, source_target_pairs={{0,3},{1,0},{2,1},{3,2},{4,7},{5,4},{6,5},{7,6},{8,11},{9,8},{10,9... | collective-permute-start | bytes 276488 | tf_op jit(solution)/shard_map/products1/ppermute | solution.py:431
  91.5 7.0 %collective-permute-start.23 = (bf16[120,384]{1,0:T(8,128)(2,1)S(1)}, bf16[120,384]{1,0:T(8,128)(2,1)S(1)}, u32[]{:S(2)}, u32[]{:S(2)}) collective-permute-start(bf16[120,384]{1,0:T(8,128)(2,1)S(1)} %get-tuple-element.70), channel_id=1, source_target_pairs={{0,2},{1,3},{2,0},{3,1},{4,6},{5,7},{6,4},{7,5},{8,10},{9,11},{10,... | collective-permute-start | bytes 276488 | tf_op jit(solution)/shard_map/products2/ppermute | solution.py:431
  91.5 7.6 %collective-permute-start.24 = (bf16[120,384]{1,0:T(8,128)(2,1)S(1)}, bf16[120,384]{1,0:T(8,128)(2,1)S(1)}, u32[]{:S(2)}, u32[]{:S(2)}) collective-permute-start(bf16[120,384]{1,0:T(8,128)(2,1)S(1)} %get-tuple-element.71), channel_id=1, source_target_pairs={{0,1},{1,2},{2,3},{3,0},{4,5},{5,6},{6,7},{7,4},{8,9},{9,10},{10,1... | collective-permute-start | bytes 276488 | tf_op jit(solution)/shard_map/products3/ppermute | solution.py:431
  (3 other events, 19.3 us)

commit v6 on v4

--- a/solution.py
+++ b/solution.py
@@ -19,7 +19,7 @@
 PAIR_B = [(o, o ^ 3) for o in range(4)]
 SWAP = [(0, 1), (1, 0)]
 MB = 1024 * 1024
-COSTS = (0.0, 2.0, 0.0, 12.0, 0.0, 0.0, 0.0, 4.0, 10.0)
+COSTS = (0.0, 4.0, 0.0, 12.0, 0.0, 0.0, 0.0, 4.0, 10.0)
 COPY = pltpu.SemaphoreType.DMA
 
 

time: 101 us -> 105 us (1.040)
  the two profiles are of different devices: /device:TPU:32 before, /device:TPU:2 now
where the time goes in v6:
time: 105 us
  starting transfers between devices  47.4 us (45%)
  waiting for transfers between devices  39.3 us (37%)
  Pallas kernels  17.3 us (16%)
    ppermute x25, starting transfers between devices, send(): return lax.ppermute(value, axis, pairs)  47.4 us
    ppermute x25, waiting for transfers between devices, send(): return lax.ppermute(value, axis, pairs)  39.3 us
    pallas_call x14, Pallas kernels, call(): pl.pallas_call(kernel, in_specs=in_specs, out_specs=out_specs or [VMEM] *...  17.3 us
  transfers between devices with their start and end apart: 25, of which 10 were waited for; matrix products, arithmetic and copies ran while one was open for 0% of the time, Pallas kernels for 12%

profile of v6, /device:TPU:2, one launch (start us, length us, event | category | flops | bytes accessed | tf_op | source)
XLA Modules:
  0.0 104.9 jit_solution(8534305203755733894)
XLA Ops:
  0.7 2.2 %pick_columns.2 = (bf16[2,120,1152]{2,1,0:T(8,128)(2,1)S(1)}, bf16[2,120,1152]{2,1,0:T(8,128)(2,1)S(1)}, bf16[4,120,1152]{2,1,0:T(8,128)(2,1)S(1)}) custom-call(s32[4]{0:T(128)S(1)} %pad_add_fusion.refs_0_, bf16[120,16384]{1,0:T(8,128)(2,1)} %bitcast.12), custom_call_target="tpu_custom_call" | custom-call | tf_op jit(solution)/shard_map/pick_columns/pallas_call | solution.py:52
  2.9 1.7 %collective-permute-start = (bf16[2,120,1152]{2,1,0:T(8,128)(2,1)S(1)}, bf16[2,120,1152]{2,1,0:T(8,128)(2,1)S(1)}, u32[]{:S(2)}, u32[]{:S(2)}) collective-permute-start(bf16[2,120,1152]{2,1,0:T(8,128)(2,1)S(1)} %get-tuple-element.38), channel_id=1, source_target_pairs={{0,1},{1,0},{2,3},{3,2},{4,5},{5,4},{6,7},{7,6},{8,9},{9,8},{10,11... | collective-permute-start | bytes 1658888 | tf_op jit(solution)/shard_map/first0_a/ppermute | solution.py:431
  4.5 2.2 %collective-permute-start.1 = (bf16[2,120,1152]{2,1,0:T(8,128)(2,1)S(1)}, bf16[2,120,1152]{2,1,0:T(8,128)(2,1)S(1)}, u32[]{:S(2)}, u32[]{:S(2)}) collective-permute-start(bf16[2,120,1152]{2,1,0:T(8,128)(2,1)S(1)} %get-tuple-element.39), channel_id=1, source_target_pairs={{0,3},{1,2},{2,1},{3,0},{4,7},{5,6},{6,5},{7,4},{8,11},{9,10},{10,... | collective-permute-start | bytes 1658888 | tf_op jit(solution)/shard_map/first0_b/ppermute | solution.py:431
  6.7 10.5 %collective-permute-done.refs_2_ = bf16[2,120,1152]{2,1,0:T(8,128)(2,1)S(1)} collective-permute-done((bf16[2,120,1152]{2,1,0:T(8,128)(2,1)S(1)}, bf16[2,120,1152]{2,1,0:T(8,128)(2,1)S(1)}, u32[]{:S(2)}, u32[]{:S(2)}) %collective-permute-start) | collective-permute-done | bytes 552992 | tf_op jit(solution)/shard_map/first0_a/ppermute | solution.py:431
  17.2 2.5 %collective-permute-done.1.refs_3_ = bf16[2,120,1152]{2,1,0:T(8,128)(2,1)S(1)} collective-permute-done((bf16[2,120,1152]{2,1,0:T(8,128)(2,1)S(1)}, bf16[2,120,1152]{2,1,0:T(8,128)(2,1)S(1)}, u32[]{:S(2)}, u32[]{:S(2)}) %collective-permute-start.1) | collective-permute-done | bytes 552992 | tf_op jit(solution)/shard_map/first0_b/ppermute | solution.py:431
  20.6 2.3 %collective-permute-start.3 = (bf16[120,1152]{1,0:T(8,128)(2,1)S(1)}, bf16[120,1152]{1,0:T(8,128)(2,1)S(1)}, u32[]{:S(2)}, u32[]{:S(2)}) collective-permute-start(bf16[120,1152]{1,0:T(8,128)(2,1)S(1)} %get-tuple-element.42), channel_id=1, source_target_pairs={{0,3},{1,2},{2,1},{3,0},{4,7},{5,6},{6,5},{7,4},{8,11},{9,10},{10,... | collective-permute-start | bytes 829448 | tf_op jit(solution)/shard_map/second0_b/ppermute | solution.py:431
  22.9 1.8 %pick_weights.1 = (bf16[2,256,256]{2,1,0:T(8,128)(2,1)S(1)}, bf16[2,256,256]{2,1,0:T(8,128)(2,1)S(1)}, bf16[2,256,256]{2,1,0:T(8,128)(2,1)S(1)}) custom-call(s32[4]{0:T(128)S(1)} %pad_add_fusion.refs_0_, bf16[16384,256]{1,0:T(8,128)(2,1)} %bitcast.10, f32[2,120,1152]{2,1,0:T(8,128)S(1)} %get-tuple-element.40.refs_2_.refs_1_), custom_call_target="tpu_custom_call" | custom-call | tf_op jit(solution)/shard_map/pick_weights/pallas_call | solution.py:52
  24.7 2.1 %pick_columns.3 = (bf16[2,120,896]{2,1,0:T(8,128)(2,1)S(1)}, bf16[2,120,896]{2,1,0:T(8,128)(2,1)S(1)}, bf16[4,120,896]{2,1,0:T(8,128)(2,1)S(1)}) custom-call(s32[4]{0:T(128)S(1)} %pad_add_fusion.refs_0_, bf16[120,16384]{1,0:T(8,128)(2,1)} %bitcast.13, bf16[2,256,256]{2,1,0:T(8,128)(2,1)S(1)} %get-tuple-element.43.refs_2_), custom_call_target="tpu_custom_call" | custom-call | tf_op jit(solution)/shard_map/pick_columns/pallas_call | solution.py:52
  26.9 1.4 %collective-permute-start.7 = (bf16[2,256,256]{2,1,0:T(8,128)(2,1)S(1)}, bf16[2,256,256]{2,1,0:T(8,128)(2,1)S(1)}, u32[]{:S(2)}, u32[]{:S(2)}) collective-permute-start(bf16[2,256,256]{2,1,0:T(8,128)(2,1)S(1)} %get-tuple-element.43.refs_2_), channel_id=1, source_target_pairs={{0,1},{1,2},{2,3},{3,0},{4,5},{5,6},{6,7},{7,4},{8,9},{9,10},{10,1... | collective-permute-start | bytes 786440 | tf_op jit(solution)/shard_map/weights1/ppermute | solution.py:431
  29.5 1.9 %collective-permute-start.9 = (bf16[2,256,256]{2,1,0:T(8,128)(2,1)S(1)}, bf16[2,256,256]{2,1,0:T(8,128)(2,1)S(1)}, u32[]{:S(2)}, u32[]{:S(2)}) collective-permute-start(bf16[2,256,256]{2,1,0:T(8,128)(2,1)S(1)} %get-tuple-element.50), channel_id=1, source_target_pairs={{0,3},{1,0},{2,1},{3,2},{4,7},{5,4},{6,5},{7,6},{8,11},{9,8},{10,9... | collective-permute-start | bytes 786440 | tf_op jit(solution)/shard_map/weights3/ppermute | solution.py:431
  31.5 2.2 %collective-permute-start.6 = (bf16[2,120,896]{2,1,0:T(8,128)(2,1)S(1)}, bf16[2,120,896]{2,1,0:T(8,128)(2,1)S(1)}, u32[]{:S(2)}, u32[]{:S(2)}) collective-permute-start(bf16[2,120,896]{2,1,0:T(8,128)(2,1)S(1)} %get-tuple-element.48), channel_id=1, source_target_pairs={{0,3},{1,2},{2,1},{3,0},{4,7},{5,6},{6,5},{7,4},{8,11},{9,10},{10,... | collective-permute-start | bytes 1290248 | tf_op jit(solution)/shard_map/first1_b/ppermute | solution.py:431
  34.5 8.1 %collective-permute-done.7.refs_1_ = bf16[2,256,256]{2,1,0:T(8,128)(2,1)S(1)} collective-permute-done((bf16[2,256,256]{2,1,0:T(8,128)(2,1)S(1)}, bf16[2,256,256]{2,1,0:T(8,128)(2,1)S(1)}, u32[]{:S(2)}, u32[]{:S(2)}) %collective-permute-start.7) | collective-permute-done | bytes 262176 | tf_op jit(solution)/shard_map/weights1/ppermute | solution.py:431
  42.6 7.2 %collective-permute-start.4 = (bf16[2,120,1152]{2,1,0:T(8,128)(2,1)S(1)}, bf16[2,120,1152]{2,1,0:T(8,128)(2,1)S(1)}, u32[]{:S(2)}, u32[]{:S(2)}) collective-permute-start(bf16[2,120,1152]{2,1,0:T(8,128)(2,1)S(1)} %get-tuple-element.46), channel_id=1, source_target_pairs={{0,4},{4,0},{1,5},{5,1},{2,6},{6,2},{3,7},{7,3},{8,12},{12,8},{9,1... | collective-permute-start | bytes 1658888 | tf_op jit(solution)/shard_map/inner0/ppermute | solution.py:431
  50.4 1.6 %collective-permute-start.13 = (bf16[2,3,256,256]{3,2,1,0:T(8,128)(2,1)S(1)}, bf16[2,3,256,256]{3,2,1,0:T(8,128)(2,1)S(1)}, u32[]{:S(2)}, u32[]{:S(2)}) collective-permute-start(bf16[2,3,256,256]{3,2,1,0:T(8,128)(2,1)S(1)} %stack.21.refs_4_.refs_1_.refs_7_), channel_id=1, source_target_pairs={{0,64},{64,128},{128,192},{192,0},{1,65},{65,129},{129,193},{193,1... | collective-permute-start | bytes 2359304 | tf_op jit(solution)/shard_map/along_x1/ppermute | solution.py:431
  53.3 1.4 %collective-permute-start.11 = (bf16[120,896]{1,0:T(8,128)(2,1)S(1)}, bf16[120,896]{1,0:T(8,128)(2,1)S(1)}, u32[]{:S(2)}, u32[]{:S(2)}) collective-permute-start(bf16[120,896]{1,0:T(8,128)(2,1)S(1)} %get-tuple-element.53), channel_id=1, source_target_pairs={{0,3},{1,2},{2,1},{3,0},{4,7},{5,6},{6,5},{7,4},{8,11},{9,10},{10,... | collective-permute-start | bytes 645128 | tf_op jit(solution)/shard_map/second1_b/ppermute | solution.py:431
  54.7 4.5 %collective-permute-done.10.refs_2_ = bf16[120,896]{1,0:T(8,128)(2,1)S(1)} collective-permute-done((bf16[120,896]{1,0:T(8,128)(2,1)S(1)}, bf16[120,896]{1,0:T(8,128)(2,1)S(1)}, u32[]{:S(2)}, u32[]{:S(2)}) %collective-permute-start.10) | collective-permute-done | bytes 215072 | tf_op jit(solution)/shard_map/second1_a/ppermute | solution.py:431
  61.2 6.1 %collective-permute-start.12 = (bf16[2,120,896]{2,1,0:T(8,128)(2,1)S(1)}, bf16[2,120,896]{2,1,0:T(8,128)(2,1)S(1)}, u32[]{:S(2)}, u32[]{:S(2)}) collective-permute-start(bf16[2,120,896]{2,1,0:T(8,128)(2,1)S(1)} %get-tuple-element.56), channel_id=1, source_target_pairs={{0,4},{4,0},{1,5},{5,1},{2,6},{6,2},{3,7},{7,3},{8,12},{12,8},{9,1... | collective-permute-start | bytes 1290248 | tf_op jit(solution)/shard_map/inner1/ppermute | solution.py:431
  69.4 1.6 %collective-permute-start.15 = (bf16[3,256,256]{2,1,0:T(8,128)(2,1)S(1)}, bf16[3,256,256]{2,1,0:T(8,128)(2,1)S(1)}, u32[]{:S(2)}, u32[]{:S(2)}) collective-permute-start(bf16[3,256,256]{2,1,0:T(8,128)(2,1)S(1)} %get-tuple-element.57.refs_4_), channel_id=1, source_target_pairs={{0,64},{64,128},{128,192},{192,0},{1,65},{65,129},{129,193},{193,1... | collective-permute-start | bytes 1179656 | tf_op jit(solution)/shard_map/along_x2a/ppermute | solution.py:431
  72.0 6.5 %collective-permute-done.12.refs_2_ = bf16[2,120,896]{2,1,0:T(8,128)(2,1)S(1)} collective-permute-done((bf16[2,120,896]{2,1,0:T(8,128)(2,1)S(1)}, bf16[2,120,896]{2,1,0:T(8,128)(2,1)S(1)}, u32[]{:S(2)}, u32[]{:S(2)}) %collective-permute-start.12) | collective-permute-done | bytes 430112 | tf_op jit(solution)/shard_map/inner1/ppermute | solution.py:431
  80.8 3.1 %project.1 = (f32[3,120,256]{2,1,0:T(8,128)S(1)}, f32[120,256]{1,0:T(8,128)S(1)}, f32[120,128]{1,0:T(8,128)S(1)}, bf16[120,2048]{1,0:T(8,128)(2,1)}) custom-call(s32[4]{0:T(128)S(1)} %pad_add_fusion.refs_0_, bf16[120,1152]{1,0:T(8,128)(2,1)S(1)} %get-tuple-element.55.refs_4_.refs_1_, bf16[120,896]{1,0:T(8,128)(2,1)S(1)} %get-tuple-element.58.refs_2_, ...), custom_call_target="tpu_custom_call" | custom-call | tf_op jit(solution)/shard_map/project/pallas_call | solution.py:52
  84.8 2.8 %collective-permute-start.22 = (bf16[120,384]{1,0:T(8,128)(2,1)S(1)}, bf16[120,384]{1,0:T(8,128)(2,1)S(1)}, u32[]{:S(2)}, u32[]{:S(2)}) collective-permute-start(bf16[120,384]{1,0:T(8,128)(2,1)S(1)} %get-tuple-element.69), channel_id=1, source_target_pairs={{0,3},{1,0},{2,1},{3,2},{4,7},{5,4},{6,5},{7,6},{8,11},{9,8},{10,9... | collective-permute-start | bytes 276488 | tf_op jit(solution)/shard_map/products1/ppermute | solution.py:431
  87.6 10.2 %collective-permute-start.23 = (bf16[120,384]{1,0:T(8,128)(2,1)S(1)}, bf16[120,384]{1,0:T(8,128)(2,1)S(1)}, u32[]{:S(2)}, u32[]{:S(2)}) collective-permute-start(bf16[120,384]{1,0:T(8,128)(2,1)S(1)} %get-tuple-element.70), channel_id=1, source_target_pairs={{0,2},{1,3},{2,0},{3,1},{4,6},{5,7},{6,4},{7,5},{8,10},{9,11},{10,... | collective-permute-start | bytes 276488 | tf_op jit(solution)/shard_map/products2/ppermute | solution.py:431
  99.1 2.1 %collective-permute-done.23.refs_4_ = bf16[120,384]{1,0:T(8,128)(2,1)S(1)} collective-permute-done((bf16[120,384]{1,0:T(8,128)(2,1)S(1)}, bf16[120,384]{1,0:T(8,128)(2,1)S(1)}, u32[]{:S(2)}, u32[]{:S(2)}) %collective-permute-start.23) | collective-permute-done | bytes 92192 | tf_op jit(solution)/shard_map/products2/ppermute | solution.py:431
  101.3 2.3 %collective-permute-done.24.refs_5_ = bf16[120,384]{1,0:T(8,128)(2,1)S(1)} collective-permute-done((bf16[120,384]{1,0:T(8,128)(2,1)S(1)}, bf16[120,384]{1,0:T(8,128)(2,1)S(1)}, u32[]{:S(2)}, u32[]{:S(2)}) %collective-permute-start.24) | collective-permute-done | bytes 92192 | tf_op jit(solution)/shard_map/products3/ppermute | solution.py:431
  (45 shorter events, 16.0 us)
Async XLA Ops:
  2.9 14.4 %collective-permute-start = (bf16[2,120,1152]{2,1,0:T(8,128)(2,1)S(1)}, bf16[2,120,1152]{2,1,0:T(8,128)(2,1)S(1)}, u32[]{:S(2)}, u32[]{:S(2)}) collective-permute-start(bf16[2,120,1152]{2,1,0:T(8,128)(2,1)S(1)} %get-tuple-element.38), channel_id=1, source_target_pairs={{0,1},{1,0},{2,3},{3,2},{4,5},{5,4},{6,7},{7,6},{8,9},{9,8},{10,11... | collective-permute-start | bytes 1658888 | tf_op jit(solution)/shard_map/first0_a/ppermute | solution.py:431
  4.5 15.2 %collective-permute-start.1 = (bf16[2,120,1152]{2,1,0:T(8,128)(2,1)S(1)}, bf16[2,120,1152]{2,1,0:T(8,128)(2,1)S(1)}, u32[]{:S(2)}, u32[]{:S(2)}) collective-permute-start(bf16[2,120,1152]{2,1,0:T(8,128)(2,1)S(1)} %get-tuple-element.39), channel_id=1, source_target_pairs={{0,3},{1,2},{2,1},{3,0},{4,7},{5,6},{6,5},{7,4},{8,11},{9,10},{10,... | collective-permute-start | bytes 1658888 | tf_op jit(solution)/shard_map/first0_b/ppermute | solution.py:431
  20.5 10.9 %collective-permute-start.2 = (bf16[120,1152]{1,0:T(8,128)(2,1)S(1)}, bf16[120,1152]{1,0:T(8,128)(2,1)S(1)}, u32[]{:S(2)}, u32[]{:S(2)}) collective-permute-start(bf16[120,1152]{1,0:T(8,128)(2,1)S(1)} %get-tuple-element.41), channel_id=1, source_target_pairs={{0,1},{1,0},{2,3},{3,2},{4,5},{5,4},{6,7},{7,6},{8,9},{9,8},{10,11... | collective-permute-start | bytes 829448 | tf_op jit(solution)/shard_map/second0_a/ppermute | solution.py:431
  20.6 10.9 %collective-permute-start.3 = (bf16[120,1152]{1,0:T(8,128)(2,1)S(1)}, bf16[120,1152]{1,0:T(8,128)(2,1)S(1)}, u32[]{:S(2)}, u32[]{:S(2)}) collective-permute-start(bf16[120,1152]{1,0:T(8,128)(2,1)S(1)} %get-tuple-element.42), channel_id=1, source_target_pairs={{0,3},{1,2},{2,1},{3,0},{4,7},{5,6},{6,5},{7,4},{8,11},{9,10},{10,... | collective-permute-start | bytes 829448 | tf_op jit(solution)/shard_map/second0_b/ppermute | solution.py:431
  26.9 15.7 %collective-permute-start.7 = (bf16[2,256,256]{2,1,0:T(8,128)(2,1)S(1)}, bf16[2,256,256]{2,1,0:T(8,128)(2,1)S(1)}, u32[]{:S(2)}, u32[]{:S(2)}) collective-permute-start(bf16[2,256,256]{2,1,0:T(8,128)(2,1)S(1)} %get-tuple-element.43.refs_2_), channel_id=1, source_target_pairs={{0,1},{1,2},{2,3},{3,0},{4,5},{5,6},{6,7},{7,4},{8,9},{9,10},{10,1... | collective-permute-start | bytes 786440 | tf_op jit(solution)/shard_map/weights1/ppermute | solution.py:431
  28.3 21.5 %collective-permute-start.8 = (bf16[2,256,256]{2,1,0:T(8,128)(2,1)S(1)}, bf16[2,256,256]{2,1,0:T(8,128)(2,1)S(1)}, u32[]{:S(2)}, u32[]{:S(2)}) collective-permute-start(bf16[2,256,256]{2,1,0:T(8,128)(2,1)S(1)} %get-tuple-element.49), channel_id=1, source_target_pairs={{0,2},{1,3},{2,0},{3,1},{4,6},{5,7},{6,4},{7,5},{8,10},{9,11},{10,... | collective-permute-start | bytes 786440 | tf_op jit(solution)/shard_map/weights2/ppermute | solution.py:431
  29.5 20.3 %collective-permute-start.9 = (bf16[2,256,256]{2,1,0:T(8,128)(2,1)S(1)}, bf16[2,256,256]{2,1,0:T(8,128)(2,1)S(1)}, u32[]{:S(2)}, u32[]{:S(2)}) collective-permute-start(bf16[2,256,256]{2,1,0:T(8,128)(2,1)S(1)} %get-tuple-element.50), channel_id=1, source_target_pairs={{0,3},{1,0},{2,1},{3,2},{4,7},{5,4},{6,5},{7,6},{8,11},{9,8},{10,9... | collective-permute-start | bytes 786440 | tf_op jit(solution)/shard_map/weights3/ppermute | solution.py:431
  31.4 21.1 %collective-permute-start.5 = (bf16[2,120,896]{2,1,0:T(8,128)(2,1)S(1)}, bf16[2,120,896]{2,1,0:T(8,128)(2,1)S(1)}, u32[]{:S(2)}, u32[]{:S(2)}) collective-permute-start(bf16[2,120,896]{2,1,0:T(8,128)(2,1)S(1)} %get-tuple-element.47), channel_id=1, source_target_pairs={{0,1},{1,0},{2,3},{3,2},{4,5},{5,4},{6,7},{7,6},{8,9},{9,8},{10,11... | collective-permute-start | bytes 1290248 | tf_op jit(solution)/shard_map/first1_a/ppermute | solution.py:431
  31.5 21.0 %collective-permute-start.6 = (bf16[2,120,896]{2,1,0:T(8,128)(2,1)S(1)}, bf16[2,120,896]{2,1,0:T(8,128)(2,1)S(1)}, u32[]{:S(2)}, u32[]{:S(2)}) collective-permute-start(bf16[2,120,896]{2,1,0:T(8,128)(2,1)S(1)} %get-tuple-element.48), channel_id=1, source_target_pairs={{0,3},{1,2},{2,1},{3,0},{4,7},{5,6},{6,5},{7,4},{8,11},{9,10},{10,... | collective-permute-start | bytes 1290248 | tf_op jit(solution)/shard_map/first1_b/ppermute | solution.py:431
  42.6 25.3 %collective-permute-start.4 = (bf16[2,120,1152]{2,1,0:T(8,128)(2,1)S(1)}, bf16[2,120,1152]{2,1,0:T(8,128)(2,1)S(1)}, u32[]{:S(2)}, u32[]{:S(2)}) collective-permute-start(bf16[2,120,1152]{2,1,0:T(8,128)(2,1)S(1)} %get-tuple-element.46), channel_id=1, source_target_pairs={{0,4},{4,0},{1,5},{5,1},{2,6},{6,2},{3,7},{7,3},{8,12},{12,8},{9,1... | collective-permute-start | bytes 1658888 | tf_op jit(solution)/shard_map/inner0/ppermute | solution.py:431
  50.4 18.4 %collective-permute-start.13 = (bf16[2,3,256,256]{3,2,1,0:T(8,128)(2,1)S(1)}, bf16[2,3,256,256]{3,2,1,0:T(8,128)(2,1)S(1)}, u32[]{:S(2)}, u32[]{:S(2)}) collective-permute-start(bf16[2,3,256,256]{3,2,1,0:T(8,128)(2,1)S(1)} %stack.21.refs_4_.refs_1_.refs_7_), channel_id=1, source_target_pairs={{0,64},{64,128},{128,192},{192,0},{1,65},{65,129},{129,193},{193,1... | collective-permute-start | bytes 2359304 | tf_op jit(solution)/shard_map/along_x1/ppermute | solution.py:431
  51.9 16.8 %collective-permute-start.14 = (bf16[2,3,256,256]{3,2,1,0:T(8,128)(2,1)S(1)}, bf16[2,3,256,256]{3,2,1,0:T(8,128)(2,1)S(1)}, u32[]{:S(2)}, u32[]{:S(2)}) collective-permute-start(bf16[2,3,256,256]{3,2,1,0:T(8,128)(2,1)S(1)} %stack.21.refs_4_.refs_1_.refs_7_), channel_id=1, source_target_pairs={{0,192},{64,0},{128,64},{192,128},{1,193},{65,1},{129,65},{193,129... | collective-permute-start | bytes 2359304 | tf_op jit(solution)/shard_map/along_x3/ppermute | solution.py:431
  53.2 6.0 %collective-permute-start.10 = (bf16[120,896]{1,0:T(8,128)(2,1)S(1)}, bf16[120,896]{1,0:T(8,128)(2,1)S(1)}, u32[]{:S(2)}, u32[]{:S(2)}) collective-permute-start(bf16[120,896]{1,0:T(8,128)(2,1)S(1)} %get-tuple-element.52), channel_id=1, source_target_pairs={{0,1},{1,0},{2,3},{3,2},{4,5},{5,4},{6,7},{7,6},{8,9},{9,8},{10,11... | collective-permute-start | bytes 645128 | tf_op jit(solution)/shard_map/second1_a/ppermute | solution.py:431
  53.3 7.2 %collective-permute-start.11 = (bf16[120,896]{1,0:T(8,128)(2,1)S(1)}, bf16[120,896]{1,0:T(8,128)(2,1)S(1)}, u32[]{:S(2)}, u32[]{:S(2)}) collective-permute-start(bf16[120,896]{1,0:T(8,128)(2,1)S(1)} %get-tuple-element.53), channel_id=1, source_target_pairs={{0,3},{1,2},{2,1},{3,0},{4,7},{5,6},{6,5},{7,4},{8,11},{9,10},{10,... | collective-permute-start | bytes 645128 | tf_op jit(solution)/shard_map/second1_b/ppermute | solution.py:431
  61.2 17.3 %collective-permute-start.12 = (bf16[2,120,896]{2,1,0:T(8,128)(2,1)S(1)}, bf16[2,120,896]{2,1,0:T(8,128)(2,1)S(1)}, u32[]{:S(2)}, u32[]{:S(2)}) collective-permute-start(bf16[2,120,896]{2,1,0:T(8,128)(2,1)S(1)} %get-tuple-element.56), channel_id=1, source_target_pairs={{0,4},{4,0},{1,5},{5,1},{2,6},{6,2},{3,7},{7,3},{8,12},{12,8},{9,1... | collective-permute-start | bytes 1290248 | tf_op jit(solution)/shard_map/inner1/ppermute | solution.py:431
  69.4 9.1 %collective-permute-start.15 = (bf16[3,256,256]{2,1,0:T(8,128)(2,1)S(1)}, bf16[3,256,256]{2,1,0:T(8,128)(2,1)S(1)}, u32[]{:S(2)}, u32[]{:S(2)}) collective-permute-start(bf16[3,256,256]{2,1,0:T(8,128)(2,1)S(1)} %get-tuple-element.57.refs_4_), channel_id=1, source_target_pairs={{0,64},{64,128},{128,192},{192,0},{1,65},{65,129},{129,193},{193,1... | collective-permute-start | bytes 1179656 | tf_op jit(solution)/shard_map/along_x2a/ppermute | solution.py:431
  71.0 8.1 %collective-permute-start.16 = (bf16[3,256,256]{2,1,0:T(8,128)(2,1)S(1)}, bf16[3,256,256]{2,1,0:T(8,128)(2,1)S(1)}, u32[]{:S(2)}, u32[]{:S(2)}) collective-permute-start(bf16[3,256,256]{2,1,0:T(8,128)(2,1)S(1)} %get-tuple-element.63), channel_id=1, source_target_pairs={{0,192},{64,0},{128,64},{192,128},{1,193},{65,1},{129,65},{193,129... | collective-permute-start | bytes 1179656 | tf_op jit(solution)/shard_map/along_x2b/ppermute | solution.py:431
  71.5 8.4 %collective-permute-start.17 = (bf16[2,3,256,256]{3,2,1,0:T(8,128)(2,1)S(1)}, bf16[2,3,256,256]{3,2,1,0:T(8,128)(2,1)S(1)}, u32[]{:S(2)}, u32[]{:S(2)}) collective-permute-start(bf16[2,3,256,256]{3,2,1,0:T(8,128)(2,1)S(1)} %get-tuple-element.64), channel_id=1, source_target_pairs={{0,8},{8,0},{1,9},{9,1},{2,10},{10,2},{3,11},{11,3},{4,12},{12,4},... | collective-permute-start | bytes 2359304 | tf_op jit(solution)/shard_map/core0/ppermute | solution.py:431
  71.5 8.4 %collective-permute-start.18 = (bf16[2,3,256,256]{3,2,1,0:T(8,128)(2,1)S(1)}, bf16[2,3,256,256]{3,2,1,0:T(8,128)(2,1)S(1)}, u32[]{:S(2)}, u32[]{:S(2)}) collective-permute-start(bf16[2,3,256,256]{3,2,1,0:T(8,128)(2,1)S(1)} %collective-permute-done.13.refs_2_.refs_8_), channel_id=1, source_target_pairs={{0,8},{8,0},{1,9},{9,1},{2,10},{10,2},{3,11},{11,3},{4,12},{12,4},... | collective-permute-start | bytes 2359304 | tf_op jit(solution)/shard_map/core1/ppermute | solution.py:431
  78.5 5.4 %collective-permute-start.20 = (bf16[3,256,256]{2,1,0:T(8,128)(2,1)S(1)}, bf16[3,256,256]{2,1,0:T(8,128)(2,1)S(1)}, u32[]{:S(2)}, u32[]{:S(2)}) collective-permute-start(bf16[3,256,256]{2,1,0:T(8,128)(2,1)S(1)} %collective-permute-done.15.refs_10_), channel_id=1, source_target_pairs={{0,8},{8,0},{1,9},{9,1},{2,10},{10,2},{3,11},{11,3},{4,12},{12,4},... | collective-permute-start | bytes 1179656 | tf_op jit(solution)/shard_map/core2a/ppermute | solution.py:431
  79.0 4.9 %collective-permute-start.21 = (bf16[3,256,256]{2,1,0:T(8,128)(2,1)S(1)}, bf16[3,256,256]{2,1,0:T(8,128)(2,1)S(1)}, u32[]{:S(2)}, u32[]{:S(2)}) collective-permute-start(bf16[3,256,256]{2,1,0:T(8,128)(2,1)S(1)} %collective-permute-done.16.refs_11_), channel_id=1, source_target_pairs={{0,8},{8,0},{1,9},{9,1},{2,10},{10,2},{3,11},{11,3},{4,12},{12,4},... | collective-permute-start | bytes 1179656 | tf_op jit(solution)/shard_map/core2b/ppermute | solution.py:431
  84.8 14.3 %collective-permute-start.22 = (bf16[120,384]{1,0:T(8,128)(2,1)S(1)}, bf16[120,384]{1,0:T(8,128)(2,1)S(1)}, u32[]{:S(2)}, u32[]{:S(2)}) collective-permute-start(bf16[120,384]{1,0:T(8,128)(2,1)S(1)} %get-tuple-element.69), channel_id=1, source_target_pairs={{0,3},{1,0},{2,1},{3,2},{4,7},{5,4},{6,5},{7,6},{8,11},{9,8},{10,9... | collective-permute-start | bytes 276488 | tf_op jit(solution)/shard_map/products1/ppermute | solution.py:431
  87.6 13.7 %collective-permute-start.23 = (bf16[120,384]{1,0:T(8,128)(2,1)S(1)}, bf16[120,384]{1,0:T(8,128)(2,1)S(1)}, u32[]{:S(2)}, u32[]{:S(2)}) collective-permute-start(bf16[120,384]{1,0:T(8,128)(2,1)S(1)} %get-tuple-element.70), channel_id=1, source_target_pairs={{0,2},{1,3},{2,0},{3,1},{4,6},{5,7},{6,4},{7,5},{8,10},{9,11},{10,... | collective-permute-start | bytes 276488 | tf_op jit(solution)/shard_map/products2/ppermute | solution.py:431
  97.8 5.8 %collective-permute-start.24 = (bf16[120,384]{1,0:T(8,128)(2,1)S(1)}, bf16[120,384]{1,0:T(8,128)(2,1)S(1)}, u32[]{:S(2)}, u32[]{:S(2)}) collective-permute-start(bf16[120,384]{1,0:T(8,128)(2,1)S(1)} %get-tuple-element.71), channel_id=1, source_target_pairs={{0,1},{1,2},{2,3},{3,0},{4,5},{5,6},{6,7},{7,4},{8,9},{9,10},{10,1... | collective-permute-start | bytes 276488 | tf_op jit(solution)/shard_map/products3/ppermute | solution.py:431
  (3 other events, 18.6 us)
